TPU v7x, 32 devices: a whole 2x2x4 slice. The times are simulated.
32 devices in a mesh: dp: 8 (over z, y), zero: 4 (over x, core).
Axes of the slice: x: 2, y: 2, z: 4, core: 2. Of those that a mesh axis runs over, the one named last changes fastest.
Arguments:
- tokens: bfloat16 [64, 1024, 576], P(('dp', 'zero')), may hold values from -6 to 6
- cotangent: bfloat16 [64, 1024, 576], P(('dp', 'zero')), may hold values from -6 to 6
- lengths: int32 [64], replicated, may hold values from 128 to 1024, as said below
- balance: int32 [4, 16], replicated, may hold values from 0 to 15, as said below
- master: float32 [3545408], P('zero'), may hold values from -3 to 3, as said below
- moment_one: float32 [3545408], P('zero'), may hold values from -640 to 640
- moment_two: float32 [3545408], P('zero'), may hold values from 100 to 100000
Outputs:
- output: bfloat16 [64, 1024, 576], P(('dp', 'zero'))
- grad_tokens: bfloat16 [64, 1024, 576], P(('dp', 'zero'))
- grads: float32 [3545408], P('zero')
- update_dir: float32 [3545408], P('zero')
- new_moment_one: float32 [3545408], P('zero')
- new_moment_two: float32 [3545408], P('zero')
- grad_gains: float32 [2, 576], P(None, 'zero')
Inputs may be any that keep to these rules, and one draw needn't show every extreme that they name: `lengths`: in every draw one sequence has exactly 1024 tokens and one exactly 128. `balance`: each row is a permutation. The 2 sequences that one balanced device holds come from 2 different data indices, and the 2 sequences of one loader device go to 2 different data indices. `master`: the flat vector in the order of the steps.
All inputs are finite; a program needn't handle non-finite values.
Results may differ from a plain program's by a relative error of at most 0.014.
The roundings to bfloat16 on the way count: a program that leaves them out, or rounds other values in their place, can miss the bound.
Values may be sent and summed in bfloat16 or wider, within the bound.
A program may use at most 384 MiB of HBM per device.

v0:
```python
import jax
import jax.numpy as jnp
from jax import lax
from jax.sharding import PartitionSpec as P

D = 576
HEADS = 9
KV_HEADS = 3
HEAD_DIM = 64
FF = 1536
QKVG = 969
PARAMS = 3545408


EPSILON = 1e-05
ROPE_BASE = 100000.0
BETA_ONE = 0.9
BETA_TWO = 0.95
BIAS_ONE = 1.0 - BETA_ONE**10
BIAS_TWO = 1.0 - BETA_TWO**10
MASK_VALUE = -1e30


def split_flat(flat):
    sizes_list = [D * QKVG, HEADS * HEAD_DIM * D, 2 * D * FF, FF * D, 2 * D, 2 * HEAD_DIM]
    shapes_list = [(D, QKVG), (HEADS * HEAD_DIM, D), (D, 2 * FF), (FF, D), (2, D), (2, HEAD_DIM)]
    pieces = []
    offset = 0
    for entry_count, shape_pair in zip(sizes_list, shapes_list):
        pieces.append(flat[offset : offset + entry_count].reshape(shape_pair))
        offset = offset + entry_count
    return pieces


def rms_gain(values, gain_vec):
    return (
        values * lax.rsqrt(jnp.mean(values * values, axis=-1, keepdims=True) + EPSILON) * gain_vec
    )


def rotate(values, positions):
    half_width = values.shape[-1] // 2
    frequency = ROPE_BASE ** (-(jnp.arange(half_width, dtype=jnp.float32) * 2.0) / values.shape[-1])
    angles = positions[:, None] * frequency[None, :]
    cosine = jnp.cos(angles)[:, None, :]
    sine_part = jnp.sin(angles)[:, None, :]
    first_half = values[..., :half_width]
    second_half = values[..., half_width:]
    return jnp.concatenate(
        [
            first_half * cosine - second_half * sine_part,
            second_half * cosine + first_half * sine_part,
        ],
        axis=-1,
    )


def gate_heads(attended, gate_logit):
    return (attended * jax.nn.sigmoid(gate_logit)[..., None]).reshape(attended.shape[0], -1)


def swiglu(gate_up):
    hidden_width = gate_up.shape[-1] // 2
    return jax.nn.silu(gate_up[:, :hidden_width]) * gate_up[:, hidden_width:]


def lane_mask(lane_rows, start_row, block_rows, lane_length):
    positions = jnp.arange(lane_rows, dtype=jnp.int32)
    query_pos = positions[start_row : start_row + block_rows]
    return (positions[None, :] <= query_pos[:, None]) & (positions[None, :] < lane_length)


def attend_lane(query_low, key_low, value_low, lane_length):
    lane_rows = query_low.shape[0]
    block_rows = min(512, lane_rows)
    score_scale = query_low.shape[-1] ** (-0.5)
    block_outputs = []
    block_totals = []
    for start_row in range(0, lane_rows, block_rows):
        query_block = query_low[start_row : start_row + block_rows]
        scores = (
            jnp.einsum("qkrd,nkd->krqn", query_block, key_low, preferred_element_type=jnp.float32)
            * score_scale
        )
        scores = jnp.where(
            lane_mask(lane_rows, start_row, block_rows, lane_length), scores, MASK_VALUE
        )
        row_peak = jnp.max(scores, axis=-1, keepdims=True)
        exp_scores = jnp.exp(scores - row_peak)
        row_total = jnp.sum(exp_scores, axis=-1, keepdims=True)
        prob_low = (exp_scores / row_total).astype(jnp.bfloat16)
        block_outputs.append(
            jnp.einsum("krqn,nkd->qkrd", prob_low, value_low, preferred_element_type=jnp.float32)
        )
        block_totals.append(row_peak[..., 0] + jnp.log(row_total[..., 0]))
    return (jnp.concatenate(block_outputs, axis=0), jnp.concatenate(block_totals, axis=-1))


def attend_back(query_low, key_low, value_low, lane_length, log_totals, grad_att_low):
    lane_rows = query_low.shape[0]
    block_rows = min(512, lane_rows)
    score_scale = query_low.shape[-1] ** (-0.5)
    grad_blocks = []
    key_grads = jnp.zeros(key_low.shape, jnp.float32)
    value_grads = jnp.zeros(value_low.shape, jnp.float32)
    for start_row in range(0, lane_rows, block_rows):
        query_block = query_low[start_row : start_row + block_rows]
        grad_slice = grad_att_low[start_row : start_row + block_rows]
        scores = (
            jnp.einsum("qkrd,nkd->krqn", query_block, key_low, preferred_element_type=jnp.float32)
            * score_scale
        )
        scores = jnp.where(
            lane_mask(lane_rows, start_row, block_rows, lane_length), scores, MASK_VALUE
        )
        prob_full = jnp.exp(scores - log_totals[..., start_row : start_row + block_rows, None])
        prob_low = prob_full.astype(jnp.bfloat16)
        grad_prob = jnp.einsum(
            "qkrd,nkd->krqn", grad_slice, value_low, preferred_element_type=jnp.float32
        )
        grad_score = (
            prob_full * (grad_prob - jnp.sum(prob_full * grad_prob, axis=-1, keepdims=True))
        ).astype(jnp.bfloat16)
        grad_blocks.append(
            jnp.einsum("krqn,nkd->qkrd", grad_score, key_low, preferred_element_type=jnp.float32)
            * score_scale
        )
        key_grads = (
            key_grads
            + jnp.einsum(
                "krqn,qkrd->nkd", grad_score, query_block, preferred_element_type=jnp.float32
            )
            * score_scale
        )
        value_grads = value_grads + jnp.einsum(
            "krqn,qkrd->nkd", prob_low, grad_slice, preferred_element_type=jnp.float32
        )
    return (jnp.concatenate(grad_blocks, axis=0), key_grads, value_grads)


def layer_pass(tokens, cotangent, lane_length, weights):
    w_in, w_out, w_mlp, w_down, gains, head_gains = split_flat(weights)
    gains_full = gains.astype(jnp.float32)
    head_full = head_gains.astype(jnp.float32)
    seq_count, lane_rows, model_width = tokens.shape
    row_count = seq_count * lane_rows
    group_size = HEADS // KV_HEADS
    width_q = HEADS * HEAD_DIM
    width_k = KV_HEADS * HEAD_DIM
    positions = jnp.arange(lane_rows, dtype=jnp.float32)
    valid_rows = (jnp.arange(lane_rows, dtype=jnp.int32)[None, :] < lane_length[:, None]).reshape(
        row_count, 1
    )
    moved = tokens.astype(jnp.float32).reshape(row_count, model_width)
    normed, first_back = jax.vjp(rms_gain, moved, gains_full[0])
    normed_low = normed.astype(jnp.bfloat16)
    projected = jnp.dot(normed_low, w_in, preferred_element_type=jnp.float32)
    query_raw = projected[:, :width_q].reshape(seq_count, lane_rows, HEADS, HEAD_DIM)
    key_raw = projected[:, width_q : width_q + width_k].reshape(
        seq_count, lane_rows, KV_HEADS, HEAD_DIM
    )
    value_raw = projected[:, width_q + width_k : width_q + 2 * width_k]
    gate_logit = projected[:, width_q + 2 * width_k :]

    def head_prep(query_in, key_in, head_gain):
        return (
            rotate(rms_gain(query_in, head_gain[0]), positions),
            rotate(rms_gain(key_in, head_gain[1]), positions),
        )

    (queries, keys_rot), heads_back = jax.vjp(head_prep, query_raw, key_raw, head_full)
    query_low = queries.astype(jnp.bfloat16).reshape(
        seq_count, lane_rows, KV_HEADS, group_size, HEAD_DIM
    )
    key_low = keys_rot.astype(jnp.bfloat16)
    value_low = value_raw.astype(jnp.bfloat16).reshape(seq_count, lane_rows, KV_HEADS, HEAD_DIM)
    attended, log_totals = lax.map(
        lambda packed: attend_lane(*packed), (query_low, key_low, value_low, lane_length)
    )
    gated_out, gate_back = jax.vjp(
        gate_heads, attended.reshape(row_count, HEADS, HEAD_DIM), gate_logit
    )
    gated_low = gated_out.astype(jnp.bfloat16)
    hidden_in = moved + jnp.dot(gated_low, w_out, preferred_element_type=jnp.float32)
    mixed_in, second_back = jax.vjp(rms_gain, hidden_in, gains_full[1])
    mixed_low = mixed_in.astype(jnp.bfloat16)
    gate_up = jnp.dot(mixed_low, w_mlp, preferred_element_type=jnp.float32)
    activated, swiglu_back = jax.vjp(swiglu, gate_up)
    activated_low = activated.astype(jnp.bfloat16)
    result = hidden_in + jnp.dot(activated_low, w_down, preferred_element_type=jnp.float32)
    result = (
        jnp.where(valid_rows, result, 0.0)
        .astype(jnp.bfloat16)
        .reshape(seq_count, lane_rows, model_width)
    )
    grad_out_low = jnp.where(
        valid_rows, cotangent.reshape(row_count, model_width), jnp.zeros((), jnp.bfloat16)
    )
    grad_out = grad_out_low.astype(jnp.float32)
    grad_down = jnp.dot(activated_low.T, grad_out_low, preferred_element_type=jnp.float32)
    (grad_gate_up,) = swiglu_back(
        jnp.dot(grad_out_low, w_down.T, preferred_element_type=jnp.float32)
    )
    gate_up_low = grad_gate_up.astype(jnp.bfloat16)
    grad_mlp = jnp.dot(mixed_low.T, gate_up_low, preferred_element_type=jnp.float32)
    grad_mixed = jnp.dot(gate_up_low, w_mlp.T, preferred_element_type=jnp.float32)
    grad_hidden_norm, grad_gain_two = second_back(grad_mixed)
    grad_hidden = grad_out + grad_hidden_norm
    branch_low = grad_hidden.astype(jnp.bfloat16)
    grad_w_out = jnp.dot(gated_low.T, branch_low, preferred_element_type=jnp.float32)
    grad_gated = jnp.dot(branch_low, w_out.T, preferred_element_type=jnp.float32)
    grad_att, grad_logit = gate_back(grad_gated)
    grad_att_low = grad_att.astype(jnp.bfloat16).reshape(
        seq_count, lane_rows, KV_HEADS, group_size, HEAD_DIM
    )
    grad_query, grad_key, grad_value = lax.map(
        lambda packed: attend_back(*packed),
        (query_low, key_low, value_low, lane_length, log_totals, grad_att_low),
    )
    grad_query_raw, grad_key_raw, grad_head = heads_back(
        (grad_query.reshape(seq_count, lane_rows, HEADS, HEAD_DIM), grad_key)
    )
    grad_proj = jnp.concatenate(
        [
            grad_query_raw.reshape(row_count, width_q),
            grad_key_raw.reshape(row_count, width_k),
            grad_value.reshape(row_count, width_k),
            grad_logit,
        ],
        axis=1,
    ).astype(jnp.bfloat16)
    grad_w_in = jnp.dot(normed_low.T, grad_proj, preferred_element_type=jnp.float32)
    grad_normed = jnp.dot(grad_proj, w_in.T, preferred_element_type=jnp.float32)
    grad_moved, grad_gain_one = first_back(grad_normed)
    grad_tokens = (
        (grad_hidden + grad_moved).astype(jnp.bfloat16).reshape(seq_count, lane_rows, model_width)
    )
    flat_grads = jnp.concatenate(
        [
            grad_w_in.reshape(-1),
            grad_w_out.reshape(-1),
            grad_mlp.reshape(-1),
            grad_down.reshape(-1),
            jnp.stack([grad_gain_one, grad_gain_two]).reshape(-1),
            grad_head.reshape(-1),
        ]
    )
    return (result, grad_tokens, flat_grads)


def lane_routes(balance, lengths, data_rank, zero_rank, seq_count, data_size, zero_size):
    balance_row = lax.dynamic_index_in_dim(balance, zero_rank, 0, keepdims=False)
    source_dev = balance_row // seq_count
    source_pos = balance_row % seq_count
    owned = (source_dev == data_rank).reshape(data_size, seq_count)
    lane_for = jnp.sum(jnp.where(owned, source_pos.reshape(data_size, seq_count), 0), axis=1)
    has_lane = jnp.any(owned, axis=1)
    senders = lax.dynamic_slice_in_dim(source_dev, data_rank * seq_count, seq_count)
    sender_pos = lax.dynamic_slice_in_dim(source_pos, data_rank * seq_count, seq_count)
    slot_lengths = jnp.take(lengths, (senders * zero_size + zero_rank) * seq_count + sender_pos)
    lane_match = has_lane[:, None] & (
        lane_for[:, None] == jnp.arange(seq_count, dtype=jnp.int32)[None, :]
    )
    lane_target = jnp.sum(
        jnp.where(lane_match, jnp.arange(data_size, dtype=jnp.int32)[:, None], 0), axis=0
    )
    return (lane_for, has_lane, senders, lane_target, slot_lengths)


def send_lanes(lanes_data, lane_for, has_lane, senders):
    outgoing = jnp.where(
        has_lane[:, None, None],
        jnp.take(lanes_data, lane_for, axis=0),
        jnp.zeros((), lanes_data.dtype),
    )
    arrived = lax.all_to_all(outgoing, "dp", split_axis=0, concat_axis=0, tiled=True)
    return jnp.take(arrived, senders, axis=0)


def return_lanes(lanes_data, senders, lane_target, data_size):
    outgoing = (
        jnp.zeros((data_size,) + lanes_data.shape[1:], lanes_data.dtype).at[senders].set(lanes_data)
    )
    arrived = lax.all_to_all(outgoing, "dp", split_axis=0, concat_axis=0, tiled=True)
    return jnp.take(arrived, lane_target, axis=0)


def local(tokens, cotangent, lengths, balance, master, moment_one, moment_two):
    data_rank = lax.axis_index("dp")
    zero_rank = lax.axis_index("zero")
    data_size = lax.axis_size("dp")
    zero_size = lax.axis_size("zero")
    seq_count = tokens.shape[0]
    weights = lax.all_gather(master.astype(jnp.bfloat16), "zero", axis=0, tiled=True)
    lane_for, has_lane, senders, lane_target, slot_lengths = lane_routes(
        balance, lengths, data_rank, zero_rank, seq_count, data_size, zero_size
    )
    arrived = send_lanes(tokens, lane_for, has_lane, senders)
    output, grad_balanced, local_grads = layer_pass(arrived, cotangent, slot_lengths, weights)
    grad_tokens = return_lanes(grad_balanced, senders, lane_target, data_size)
    gain_start = PARAMS - 2 * D - 2 * HEAD_DIM
    gain_width = D // zero_size
    local_gain = (
        local_grads[gain_start : gain_start + 2 * D]
        .reshape(2, zero_size, gain_width)
        .transpose(1, 0, 2)
    )
    grad_part, gain_part = (
        lax.psum_scatter(local_grads, "zero", scatter_dimension=0, tiled=True),
        lax.psum_scatter(local_gain, "zero", scatter_dimension=0, tiled=True),
    )
    grad_shard, gain_shard = lax.psum((grad_part, gain_part), "dp")
    grad_gains = gain_shard.reshape(2, gain_width)
    next_one = BETA_ONE * moment_one + (1.0 - BETA_ONE) * grad_shard
    next_two = BETA_TWO * moment_two + (1.0 - BETA_TWO) * grad_shard * grad_shard
    update_dir = next_one / BIAS_ONE / jnp.sqrt(next_two / BIAS_TWO)
    return (output, grad_tokens, grad_shard, update_dir, next_one, next_two, grad_gains)


def solution(mesh):
    placed = (
        P(("dp", "zero"), None, None),
        P(("dp", "zero"), None, None),
        P(),
        P(),
        P("zero"),
        P("zero"),
        P("zero"),
    )
    return jax.shard_map(
        local,
        mesh=mesh,
        in_specs=placed,
        out_specs=(
            P(("dp", "zero"), None, None),
            P(("dp", "zero"), None, None),
            P("zero"),
            P("zero"),
            P("zero"),
            P("zero"),
            P(None, "zero"),
        ),
        check_vma=False,
    )
```

profile of v0, /device:TPU:0, one launch (start us, length us, event | category | flops | bytes accessed | tf_op | source)
XLA Modules:
  0.0 1502.9 jit_solution(16375228713987012431)
XLA Ops:
  36.6 27.6 %dynamic-update-slice = bf16[3545408]{0:T(1024)(128)(2,1)} dynamic-update-slice(bf16[3545408]{0:T(1024)(128)(2,1)} %broadcast.455, bf16[886352]{0:T(1024)(128)(2,1)S(1)} %convert_element_type.78, u32[]{:T(128)} %bitcast.53) | dynamic-update-slice | bytes 3545412
  71.8 126.9 %all-reduce.17.cloned.1.call-done = bf16[3545408]{0:T(1024)(128)(2,1)} async-done(((bf16[3545408]{0:T(1024)(128)(2,1)}), bf16[3545408]{0:T(1024)(128)(2,1)}) %all-reduce.17.cloned.1.call-update) | async-done | bytes 7090832
  225.4 9.9 all-to-all-done
  283.2 90.4 %while.26 = (s32[]{:T(128)}, f32[2,1024,3,3,64]{1,4,3,2,0:T(8,128)}, f32[2,3,3,1024]{3,2,1,0:T(4,128)S(1)}, bf16[2,1024,3,64]{1,3,2,0:T(8,128)(2,1)}, s32[2]{0:T...) while((s32[]{:T(128)}, ...), condition=%wide.region_10.12_spmd, body=%wide.region_5.11_spmd.sunk | while | flops 2531853312 | bytes 160719584 | solution.py:177
  298.6 11.3 fusion.224
  309.9 9.2 fusion.226
  343.7 11.3 fusion.224
  355.0 9.2 fusion.226
  388.3 14.3 fusion.158
  402.7 23.7 %fusion.123 = (f32[2048,1536]{1,0:T(8,128)}, f32[2048,1536]{1,0:T(8,128)}, bf16[2048,1536]{1,0:T(8,128)(2,1)}) fusion(f32[2048,3072]{1,0:T(8,128)} %fusion.158, bf16[2048,576]{0,1:T(8,128)(2,1)S(1)} %bitcast.479, bf16[1536,576]{1,0:T(8,128)(2,1)S(1)} %copy-done.28), kind=kOutput, calls=%fused_computation.202 | convolution fusion | flops 3667918848 | bytes 60751872 | tf_op jit(solution)/shard_map/dot_general | solution.py:202
  426.4 16.6 %multiply_reduce_fusion.1 = (f32[576]{0:T(1024)}, f32[2048]{0:T(1024)S(1)}, f32[2048,576]{0,1:T(8,128)}) fusion(f32[2048,576]{0,1:T(8,128)} %copy-done.10, f32[2048]{0:T(1024)S(1)} %fusion.142, f32[576]{0:T(1024)S(1)} %copy-done.48, bf16[576,3072]{1,0:T(8,128)(2,1)} %reshape.377, f32[2048,1536]{1,0:T(8,128)} %get-tuple-element.271, ...), kind=kOutput, calls=%fused_computation.154 | convolution fusion | flops 7267415552 | bytes 38162944 | tf_op jit(solution)/shard_map/dot_general | solution.py:206
  443.0 16.3 %convolution_bitcast_fusion.2 = f32[72,24,8,128]{3,2,1,0:T(8,128)} fusion(f32[2048,1536]{1,0:T(8,128)} %get-tuple-element.271, f32[2048,1536]{1,0:T(8,128)} %get-tuple-element.270, f32[2048,576]{0,1:T(8,128)} %copy-done.10, f32[576]{0:T(1024)S(1)} %copy-done.48, f32[2048]{0:T(1024)S(1)} %fusion.142), kind=kOutput, calls=%fused_computation.174 | convolution fusion | flops 7263879168 | bytes 36972800 | tf_op jit(solution)/shard_map/dot_general | solution.py:205
  492.4 220.5 %while.27 = (s32[]{:T(128)}, f32[2,1024,3,3,64]{1,4,3,2,0:T(8,128)}, f32[2,1024,3,64]{1,3,2,0:T(8,128)}, bf16[2,1024,3,64]{1,3,2,0:T(8,128)(2,1)S(1)}, bf16[2,10...) while((s32[]{:T(128)}, ...), condition=%wide.region_16.18_spmd, body=%wide.region_13.17_spmd.sunk | while | flops 6185213952 | bytes 353757376 | solution.py:216
  530.6 13.1 fusion.242
  543.7 13.1 fusion.244
  556.7 29.1 %fusion.245 = (bf16[3,3,512,1024]{2,3,1,0:T(8,128)(2,1)S(1)}, bf16[3,3,512,1024]{2,3,1,0:T(8,128)(2,1)}) fusion(f32[3,1024,512,3]{2,1,3,0:T(8,128)} %get-tuple-element.431, f32[3,1024,512,3]{2,1,3,0:T(8,128)} %fusion.239, f32[3,3,512]{2,1,0:T(4,128)S(1)} %get-tuple-element.432, f32[3,3,512]{2,1,0:T(4,128)S(1)} %get-tuple-element.429, ...), kind=kLoop, calls=%fused_computation.54.clone.1 | loop fusion | flops 56623104 | bytes 95494144 | tf_op jit(solution)/shard_map/while/body/eval_jaxpr/convert_element_type | solution.py:123
  640.6 13.1 fusion.242
  653.7 13.1 fusion.244
  666.7 29.1 %fusion.245 = (bf16[3,3,512,1024]{2,3,1,0:T(8,128)(2,1)S(1)}, bf16[3,3,512,1024]{2,3,1,0:T(8,128)(2,1)}) fusion(f32[3,1024,512,3]{2,1,3,0:T(8,128)} %get-tuple-element.431, f32[3,1024,512,3]{2,1,3,0:T(8,128)} %fusion.239, f32[3,3,512]{2,1,0:T(4,128)S(1)} %get-tuple-element.432, f32[3,3,512]{2,1,0:T(4,128)S(1)} %get-tuple-element.429, ...), kind=kLoop, calls=%fused_computation.54.clone.1 | loop fusion | flops 56623104 | bytes 95494144 | tf_op jit(solution)/shard_map/while/body/eval_jaxpr/convert_element_type | solution.py:123
  726.5 11.9 multiply_reduce_fusion
  790.6 114.9 %concatenate.35 = f32[3545408]{0:T(1024)} concatenate(f32[558144]{0:T(1024)S(1)} %reshape.388, f32[331776]{0:T(1024)} %reshape.390, f32[1769472]{0:T(1024)} %bitcast.464, f32[884736]{0:T(1024)} %reshape.392, f32[1152]{0:T(1024)S(1)} %reshape.395, f32[128]{0:T(128)S(1)} %reshape.396), dimensions={0} | concatenate | bytes 28363264 | tf_op jit(solution)/shard_map/concatenate | solution.py:238
  906.4 245.2 %all-reduce.19.cloned.1.call-done = f32[3545408]{0:T(1024)} async-done(((f32[3545408]{0:T(1024)}), f32[3545408]{0:T(1024)}) %all-reduce.19.cloned.1.call-update) | async-done | bytes 14181648
  1195.8 183.4 %psum.15 = f32[2,144]{1,0:T(2,128)} all-reduce(f32[2,144]{1,0:T(2,128)S(1)} %dynamic-slice_bitcast_fusion.17), channel_id=1, replica_groups=mesh['dp'=8,'zero'=4] {'dp'}, use_global_device_ids=true, to_apply=%region_30.32 | all-reduce | flops 288 | bytes 2304 | tf_op jit(solution)/shard_map/psum | solution.py:312
  1379.2 94.8 %all-reduce.15.cloned.1.call-done = f32[886352]{0:T(1024)} async-done(((f32[886352]{0:T(1024)}), f32[886352]{0:T(1024)}) %all-reduce.15.cloned.1.call-update) | async-done | bytes 3545424 | tf_op jit(solution)/shard_map/psum | solution.py:312
  (391 shorter events, 447.7 us)
Async XLA Ops:
  22.4 212.9 %all-to-all-start = ((bf16[8,1024,576]{1,2,0:T(8,128)(2,1)}), bf16[8,1024,576]{1,2,0:T(8,128)(2,1)}, u32[]{:S(2)}, u32[]{:S(2)}) async-start(bf16[8,1024,576]{1,2,0:T(8,128)(2,1)} %select_select_fusion), calls=%async_computation | async-start | bytes 18874368 | tf_op jit(solution)/shard_map/all_to_all | solution.py:276
  29.7 169.0 %all-reduce.17.cloned.1.call-start = ((), (), s32[]{:S(2)}) async-start(), calls=%async_computation.3 | async-start | bytes 14184448
  36.6 27.7 %copy-start.60 = (s32[4,16]{1,0:T(4,128)S(1)}, s32[4,16]{1,0:T(4,128)}, u32[]{:S(2)}) copy-start(s32[4,16]{1,0:T(4,128)} %param.16) | copy-start | bytes 772
  36.6 27.9 %copy-start.3 = (s32[64]{0:T(128)S(1)}, s32[64]{0:T(128)}, u32[]{:S(2)}) copy-start(s32[64]{0:T(128)} %param.15) | copy-start | bytes 772
  64.2 1087.4 %all-reduce.19.cloned.1.call-start = ((), (), s32[]{:S(2)}) async-start(), calls=%async_computation.4 | async-start | bytes 28368896
  71.2 140.4 %copy-start.55 = (s32[2]{0:T(128)}, s32[2]{0:T(128)S(1)}, u32[]{:S(2)}) copy-start(s32[2]{0:T(128)S(1)} %get-tuple-element.249) | copy-start | bytes 28
  71.8 203.7 %copy-start.20 = (f32[1024,32]{0,1:T(8,128)}, f32[1024,32]{0,1:T(8,128)S(1)}, u32[]{:S(2)}) copy-start(f32[1024,32]{0,1:T(8,128)S(1)} %get-tuple-element.293) | copy-start | bytes 393220
  71.8 203.7 %copy-start.22 = (f32[1024,32]{0,1:T(8,128)}, f32[1024,32]{0,1:T(8,128)S(1)}, u32[]{:S(2)}) copy-start(f32[1024,32]{0,1:T(8,128)S(1)} %get-tuple-element.294) | copy-start | bytes 393220
  224.0 48.6 %copy-start.53 = (f32[64]{0:T(128)}, f32[64]{0:T(128)S(1)}, u32[]{:S(2)}) copy-start(f32[64]{0:T(128)S(1)} %get-tuple-element.292) | copy-start | bytes 772
  224.0 49.1 %copy-start.49 = (f32[64]{0:T(128)}, f32[64]{0:T(128)S(1)}, u32[]{:S(2)}) copy-start(f32[64]{0:T(128)S(1)} %get-tuple-element.291) | copy-start | bytes 772
  225.4 16.1 %copy-start.44 = (f32[576]{0:T(1024)}, f32[576]{0:T(1024)S(1)}, u32[]{:S(2)}) copy-start(f32[576]{0:T(1024)S(1)} %get-tuple-element.288) | copy-start | bytes 6916
  309.9 16.0 %slice-start.10 = ((s8[4718592]{0:T(1024)(128)(4,1)}), s8[4194304]{0:T(1024)(128)(4,1)S(1)}, s32[]{:S(2)}) async-start(s8[4718592]{0:T(1024)(128)(4,1)} %bitcast.460), calls=%async_computation.15 | async-start | bytes 8388608 | tf_op jit(solution)/shard_map/while
  355.0 16.0 %slice-start.10 = ((s8[4718592]{0:T(1024)(128)(4,1)}), s8[4194304]{0:T(1024)(128)(4,1)S(1)}, s32[]{:S(2)}) async-start(s8[4718592]{0:T(1024)(128)(4,1)} %bitcast.460), calls=%async_computation.15 | async-start | bytes 8388608 | tf_op jit(solution)/shard_map/while
  388.3 14.4 copy-start.10
  388.3 14.4 copy-start.27
  388.3 14.4 copy-start.28
  443.0 16.3 %copy-start.41 = (f32[1,8,2,128]{3,2,1,0:T(2,128)S(1)}, f32[1,8,2,128]{3,2,1,0:T(2,128)}, u32[]{:S(2)}) copy-start(f32[1,8,2,128]{3,2,1,0:T(2,128)} %get-tuple-element.285) | copy-start | bytes 24580
  726.5 21.0 %slice-start.4 = ((s8[4718592]{0:T(1024)(128)(4,1)}), s8[4194304]{0:T(1024)(128)(4,1)S(1)}, s32[]{:S(2)}) async-start(s8[4718592]{0:T(1024)(128)(4,1)} %bitcast.450), calls=%async_computation.9 | async-start | bytes 8388608
  747.6 13.3 slice-start.14
  767.9 13.4 slice-start.12
  905.5 568.5 %all-reduce.15.cloned.1.call-start = ((), (), s32[]{:S(2)}) async-start(), calls=%async_computation.2 | async-start | bytes 7094272 | tf_op jit(solution)/shard_map/psum | solution.py:312
  906.4 250.1 %copy-start.58 = (pred[8]{0:T(512)(128)(4,1)S(1)}, pred[8]{0:T(512)(128)(4,1)}, u32[]{:S(2)}) copy-start(pred[8]{0:T(512)(128)(4,1)} %copy-done.57) | copy-start | bytes 28
  906.4 250.1 %copy-start.62 = (s32[8]{0:T(128)S(1)}, s32[8]{0:T(128)}, u32[]{:S(2)}) copy-start(s32[8]{0:T(128)} %copy-done.61) | copy-start | bytes 100
  1183.4 299.5 %all-to-all-start.1 = ((bf16[8,1024,576]{1,2,0:T(8,128)(2,1)}), bf16[8,1024,576]{1,2,0:T(8,128)(2,1)}, u32[]{:S(2)}, u32[]{:S(2)}) async-start(bf16[8,1024,576]{1,2,0:T(8,128)(2,1)} %scatter_fusion), calls=%async_computation.1 | async-start | bytes 18874368 | tf_op jit(solution)/shard_map/all_to_all | solution.py:284
  (65 other events, 338.9 us)
Sparse Core Ops, SparseCore 0:
  64.3 134.3 all-reduce.16
  905.6 245.9 all-reduce.18
  1156.6 317.4 all-reduce.14
where the time goes:
time: 1520 us; the launch traced here: 1500 us
  waiting for transfers between devices  477 us (31%)
  matrix products  321 us (21%)
  local copies, waits for them, and re-layouts  307 us (20%)
  blocking collectives  190 us (12%)
  other arithmetic  177 us (12%)
  between operations  16.6 us (1%)
    unnamed x5, waiting for transfers between devices  372 us
    psum x1, blocking collectives, local(): grad_shard, gain_shard = lax.psum((grad_part, gain_part), 'dp')  183 us
    concatenate x1, local copies, waits for them, and re-layouts, layer_pass(): jnp.concatenate([grad_w_in.reshape(-1), grad_w_out.reshape(-1), grad_mlp....  115 us
    psum x1, waiting for transfers between devices, local(): grad_shard, gain_shard = lax.psum((grad_part, gain_part), 'dp')  94.8 us
    convert_element_type x2, other arithmetic, attend_back(): grad_score = (prob_full * (grad_prob - jnp.sum(prob_full * grad_prob, axi...  58.3 us
    unnamed x159, local copies, waits for them, and re-layouts  53.9 us
    dot_general x4, matrix products, attend_back(): jnp.einsum('qkrd,nkd->krqn', grad_slice, value_low, preferred_element_typ...  52.3 us
    dot_general x4, matrix products, attend_back(): jnp.einsum('qkrd,nkd->krqn', query_block, key_low, preferred_element_type...  35.9 us
  transfers between devices with their start and end apart: 5, of which 4 were waited for; matrix products, arithmetic and copies ran while one was open for 7% of the time, Pallas kernels for 0%

commit v1 on v0

v1 whole, which is shorter than its diff:
```python
import functools
import math

import jax
import jax.numpy as jnp
import numpy as np
from jax import lax
from jax.experimental import pallas as pl
from jax.experimental.pallas import tpu as pltpu
from jax.sharding import PartitionSpec as P

D = 576
HEADS = 9
KV_HEADS = 3
GROUP = HEADS // KV_HEADS
HEAD_DIM = 64
HALF = HEAD_DIM // 2
FF = 1536
LANE = 1024
QKVG = 969
QKVG_PAD = 1024
WIDTH_Q = HEADS * HEAD_DIM
WIDTH_K = KV_HEADS * HEAD_DIM
PARAMS = 3545408
EPSILON = 1e-05
ROPE_BASE = 100000.0
BETA_ONE = 0.9
BETA_TWO = 0.95
BIAS_ONE = 1.0 - BETA_ONE**10
BIAS_TWO = 1.0 - BETA_TWO**10
SCALE = HEAD_DIM ** (-0.5)
EXP_SCALE = SCALE * math.log2(math.e)
F32 = jnp.float32
BF16 = jnp.bfloat16
BLOCK = 256
BLOCKS = LANE // BLOCK
FF_CHUNK = 768
MLP_BLOCK = 512
MLP_BLOCKS = LANE // MLP_BLOCK
PROJ_BLOCK = 512
PROJ_BLOCKS = LANE // PROJ_BLOCK
VMEM_LIMIT = 60 * 1024 * 1024


def dot(a, b, ca, cb):
    return lax.dot_general(a, b, (((ca,), (cb,)), ((), ())), preferred_element_type=F32)


def rope_tables():
    frequency = ROPE_BASE ** (-(np.arange(HALF, dtype=np.float32) * np.float32(2.0)) / np.float32(HEAD_DIM))
    angles = np.arange(LANE, dtype=np.float32)[None, :] * frequency.astype(np.float32)[:, None]
    return np.cos(angles).astype(np.float32), np.sin(angles).astype(np.float32)


def mean_square_scale(values, axis):
    return lax.rsqrt(jnp.mean(values * values, axis=axis, keepdims=True) + EPSILON)


def block_spec(shape, index):
    return pl.BlockSpec(shape, index)


def whole(shape):
    return pl.BlockSpec(shape, lambda *_: (0,) * len(shape), pipeline_mode=pl.Buffered(1))


def full_col_map(lane, block, lens):
    return (lane, 0, block)


def last_block(lens, lane, block):
    return jnp.minimum(block, (lens[lane] - 1) // BLOCK)


def project_kernel(lens, tok_t, w_in, gain_cols, head_gains, cosine, sine, q_t, k_n, k_t, v_n, v_t, raw, gate, w_in_t):
    lane, block = pl.program_id(0), pl.program_id(1)

    @pl.when((lane == 0) & (block == 0))
    def _():
        w_in_t[...] = w_in[...].T

    @pl.when(block * PROJ_BLOCK < lens[lane])
    def _():
        x = tok_t[0].astype(F32)
        normed = (x * mean_square_scale(x, 0) * gain_cols[0]).astype(BF16)
        projected = dot(w_in_t[...], normed, 1, 0)
        raw[0] = projected[: WIDTH_Q + WIDTH_K]
        cos, sin = cosine[...], sine[...]
        for head in range(HEADS + KV_HEADS):
            u = projected[head * HEAD_DIM : (head + 1) * HEAD_DIM]
            y = u * mean_square_scale(u, 0) * head_gains[0 if head < HEADS else 1]
            y1, y2 = y[:HALF], y[HALF:]
            turned = jnp.concatenate([y1 * cos - y2 * sin, y2 * cos + y1 * sin], axis=0)
            if head < HEADS:
                q_t[0, head * HEAD_DIM : (head + 1) * HEAD_DIM] = turned.astype(BF16)
            else:
                k = head - HEADS
                k_t[0, k * HEAD_DIM : (k + 1) * HEAD_DIM] = turned.astype(BF16)
                k_n[0, k] = turned.T.astype(BF16)
        values = projected[WIDTH_Q + WIDTH_K : WIDTH_Q + 2 * WIDTH_K]
        v_t[0] = values.astype(BF16)
        for k in range(KV_HEADS):
            v_n[0, k] = values[k * HEAD_DIM : (k + 1) * HEAD_DIM].T.astype(BF16)
        gate[0] = projected[WIDTH_Q + 2 * WIDTH_K : WIDTH_Q + 2 * WIDTH_K + 16]

    @pl.when(block * PROJ_BLOCK >= lens[lane])
    def _():
        for ref in (q_t, k_n, k_t, v_n, v_t):
            ref[...] = jnp.zeros_like(ref)


def col_map(lane, block, lens):
    return (lane, 0, last_block(lens, lane, block))


def mlp_row_map(lane, block, lens):
    return (lane, jnp.minimum(block, (lens[lane] - 1) // MLP_BLOCK), 0)


def mlp_col_map(lane, block, lens):
    return (lane, 0, jnp.minimum(block, (lens[lane] - 1) // MLP_BLOCK))


def proj_col_map(lane, block, lens):
    return (lane, 0, jnp.minimum(block, (lens[lane] - 1) // PROJ_BLOCK))


def proj_table_map(lane, block, lens):
    return (0, jnp.minimum(block, (lens[lane] - 1) // PROJ_BLOCK))


def full_head_map(lane, block, lens):
    return (lane, 0, block, 0)


def project(lens, tokens_t, w_in, gain_cols, head_gains, cosine, sine):
    lanes = tokens_t.shape[0]
    shape = jax.ShapeDtypeStruct
    return pl.pallas_call(
        project_kernel,
        name="project",
        grid_spec=pltpu.PrefetchScalarGridSpec(
            num_scalar_prefetch=1,
            grid=(lanes, PROJ_BLOCKS),
            in_specs=[
                pl.BlockSpec((1, D, PROJ_BLOCK), proj_col_map),
                whole((D, QKVG_PAD)),
                whole((2, D, 1)),
                whole((2, HEAD_DIM, 1)),
                pl.BlockSpec((HALF, PROJ_BLOCK), proj_table_map),
                pl.BlockSpec((HALF, PROJ_BLOCK), proj_table_map),
            ],
            out_specs=[
                pl.BlockSpec((1, WIDTH_Q, PROJ_BLOCK), full_col_map),
                pl.BlockSpec((1, KV_HEADS, PROJ_BLOCK, HEAD_DIM), full_head_map),
                pl.BlockSpec((1, WIDTH_K, PROJ_BLOCK), full_col_map),
                pl.BlockSpec((1, KV_HEADS, PROJ_BLOCK, HEAD_DIM), full_head_map),
                pl.BlockSpec((1, WIDTH_K, PROJ_BLOCK), full_col_map),
                pl.BlockSpec((1, WIDTH_Q + WIDTH_K, PROJ_BLOCK), proj_col_map),
                pl.BlockSpec((1, 16, PROJ_BLOCK), proj_col_map),
            ],
            scratch_shapes=[pltpu.VMEM((QKVG_PAD, D), BF16)],
        ),
        out_shape=[
            shape((lanes, WIDTH_Q, LANE), BF16),
            shape((lanes, KV_HEADS, LANE, HEAD_DIM), BF16),
            shape((lanes, WIDTH_K, LANE), BF16),
            shape((lanes, KV_HEADS, LANE, HEAD_DIM), BF16),
            shape((lanes, WIDTH_K, LANE), BF16),
            shape((lanes, WIDTH_Q + WIDTH_K, LANE), F32),
            shape((lanes, 16, LANE), F32),
        ],
        cost_estimate=pl.CostEstimate(flops=0, bytes_accessed=0, transcendentals=0),
        compiler_params=pltpu.CompilerParams(vmem_limit_bytes=VMEM_LIMIT),
    )(lens, tokens_t, w_in, gain_cols, head_gains, cosine, sine)


def causal_tile(values, fill):
    key_pos = lax.broadcasted_iota(jnp.int32, values.shape, 0)
    query_pos = lax.broadcasted_iota(jnp.int32, values.shape, 1)
    return jnp.where(key_pos <= query_pos, values, fill)


def attend_kernel(lens, q_t, k_n, v_t, out_t, log_total):
    lane, block = pl.program_id(0), pl.program_id(1)
    log_total[0] = jnp.zeros((16, BLOCK), F32)

    for level in range(BLOCKS):

        @pl.when((block == level) & (level * BLOCK < lens[lane]))
        def _():
            before = level * BLOCK
            for head in range(HEADS):
                g = head // GROUP
                query = q_t[0, head * HEAD_DIM : (head + 1) * HEAD_DIM]
                values = v_t.at[0, g * HEAD_DIM : (g + 1) * HEAD_DIM]
                weights = jnp.exp2(dot(k_n[0, g, before : before + BLOCK], query, 1, 0) * EXP_SCALE)
                weights = causal_tile(weights, 0.0)
                total = jnp.sum(weights, axis=0, keepdims=True)
                mixed = dot(values[:, before : before + BLOCK], weights.astype(BF16), 1, 0)
                if before:
                    weights = jnp.exp2(dot(k_n[0, g, :before], query, 1, 0) * EXP_SCALE)
                    total += jnp.sum(weights, axis=0, keepdims=True)
                    mixed += dot(values[:, :before], weights.astype(BF16), 1, 0)
                out_t[0, head * HEAD_DIM : (head + 1) * HEAD_DIM] = mixed * (1.0 / total)
                log_total[0, head : head + 1] = jnp.log2(total)


def attend(lens, q_t, k_n, v_t):
    lanes = q_t.shape[0]
    shape = jax.ShapeDtypeStruct
    return pl.pallas_call(
        attend_kernel,
        name="attend",
        grid_spec=pltpu.PrefetchScalarGridSpec(
            num_scalar_prefetch=1,
            grid=(lanes, BLOCKS),
            in_specs=[
                pl.BlockSpec((1, WIDTH_Q, BLOCK), col_map),
                pl.BlockSpec((1, KV_HEADS, LANE, HEAD_DIM), lambda lane, block, lens: (lane, 0, 0, 0)),
                pl.BlockSpec((1, WIDTH_K, LANE), lambda lane, block, lens: (lane, 0, 0)),
            ],
            out_specs=[
                pl.BlockSpec((1, WIDTH_Q, BLOCK), col_map),
                pl.BlockSpec((1, 16, BLOCK), full_col_map),
            ],
        ),
        out_shape=[
            shape((lanes, WIDTH_Q, LANE), F32),
            shape((lanes, 16, LANE), F32),
        ],
        cost_estimate=pl.CostEstimate(flops=0, bytes_accessed=0, transcendentals=0),
        compiler_params=pltpu.CompilerParams(vmem_limit_bytes=VMEM_LIMIT),
    )(lens, q_t, k_n, v_t)


OUT_ROWS = WIDTH_Q * D // 128
MLP_ROWS = D * 2 * FF // 128
DOWN_ROWS = FF * D // 128
LATE_ROWS = OUT_ROWS + MLP_ROWS + DOWN_ROWS
WIDE_TILES = 2 * FF // 128
WIDE_STEP = 48
PAIR_STEP = 32
PAIR_ROWS = PAIR_STEP * 9


def pack_wide(source, target, stage, first_row):
    @pl.loop(0, D // WIDE_STEP)
    def _(piece):
        rows = pl.ds(pl.multiple_of(piece * WIDE_STEP, WIDE_STEP), WIDE_STEP)
        for tile in range(WIDE_TILES):
            stage[pl.ds(tile, WIDE_STEP, stride=WIDE_TILES), :] = source[rows, tile * 128 : (tile + 1) * 128]
        size = WIDE_STEP * WIDE_TILES
        target[pl.ds(pl.multiple_of(first_row + piece * size, 16), size), :] = stage[:size].astype(BF16)


def set_tiles(target, value):
    for t in range(4):
        target[t] = value[:, t * 128 : (t + 1) * 128]
    target[4, :, :64] = value[:, 512:]


def pack_pairs(rows_ref, stage):
    tiles = [rows_ref[t, pl.ds(parity, PAIR_STEP, stride=2), :] for parity in range(2) for t in range(5)]
    even, odd = tiles[:5], tiles[5:]
    for t in range(4):
        stage[pl.ds(t, PAIR_STEP, stride=9), :] = even[t]
    stage[pl.ds(4, PAIR_STEP, stride=9), :] = jnp.concatenate([even[4][:, :64], odd[0][:, :64]], axis=1)
    for t in range(4):
        right = odd[t + 1][:, :64]
        stage[pl.ds(5 + t, PAIR_STEP, stride=9), :] = jnp.concatenate([odd[t][:, 64:], right], axis=1)


def mlp_kernel(lens, att_t, gate, tok_t, gains, w_out, w_mlp, w_down, out_parts, hidden_in, act_low, gate_slope, up_slope, total):
    lane, block = pl.program_id(0), pl.program_id(1)

    @pl.when(block * MLP_BLOCK >= lens[lane])
    def _():
        out_parts[...] = jnp.zeros_like(out_parts)

    @pl.when(block * MLP_BLOCK < lens[lane])
    def _():
        att = att_t[0].reshape(HEADS, HEAD_DIM, MLP_BLOCK)
        sig = jax.nn.sigmoid(gate[0, :HEADS])[:, None, :]
        gated_t = (att * sig).reshape(WIDTH_Q, MLP_BLOCK).astype(BF16)
        hidden = tok_t[0].T.astype(F32) + dot(gated_t, w_out[...], 0, 0)
        hidden_in[0] = hidden
        mixed = (hidden * mean_square_scale(hidden, 1) * gains[1:2]).astype(BF16)
        valid_t = lax.broadcasted_iota(jnp.int32, (1, MLP_BLOCK), 1) + block * MLP_BLOCK < lens[lane]
        total[...] = hidden

        @pl.loop(0, FF // FF_CHUNK, unroll=True)
        def _(chunk):
            low = pl.ds(pl.multiple_of(chunk * FF_CHUNK, FF_CHUNK), FF_CHUNK)
            high = pl.ds(pl.multiple_of(FF + chunk * FF_CHUNK, FF_CHUNK), FF_CHUNK)
            g = dot(mixed, w_mlp[:, low], 1, 0)
            u = dot(mixed, w_mlp[:, high], 1, 0)
            s = jax.nn.sigmoid(g)
            gs = g * s
            act = (gs * u).astype(BF16)
            total[...] += dot(act, w_down[low, :], 1, 0)
            act_low[0, :, low] = act
            gate_slope[0, :, low] = (u * (s * (1.0 + g * (1.0 - s)))).astype(BF16)
            up_slope[0, :, low] = gs.astype(BF16)

        out_t = jnp.where(valid_t, total[...].T, 0.0).astype(BF16)
        width = out_parts.shape[3]
        for part in range(out_parts.shape[0]):
            out_parts[part, 0] = out_t[:, part * width : (part + 1) * width]


def part_map(lane, block, lens):
    return (block, lane, 0, 0)


def kept_part_map(lane, block, lens):
    return (jnp.minimum(block, (lens[lane] - 1) // MLP_BLOCK), lane, 0, 0)


def mlp(lens, att_t, gate, tokens_t, gains, w_out, w_mlp, w_down, dp_size):
    lanes = tokens_t.shape[0]
    width = LANE // dp_size
    shape = jax.ShapeDtypeStruct
    return pl.pallas_call(
        mlp_kernel,
        name="mlp",
        grid_spec=pltpu.PrefetchScalarGridSpec(
            num_scalar_prefetch=1,
            grid=(lanes, MLP_BLOCKS),
            in_specs=[
                pl.BlockSpec((1, WIDTH_Q, MLP_BLOCK), mlp_col_map),
                pl.BlockSpec((1, 16, MLP_BLOCK), mlp_col_map),
                pl.BlockSpec((1, D, MLP_BLOCK), mlp_col_map),
                whole((2, D)),
                whole((WIDTH_Q, D)),
                whole((D, 2 * FF)),
                whole((FF, D)),
            ],
            out_specs=[
                pl.BlockSpec((dp_size // MLP_BLOCKS, 1, D, width), part_map),
                pl.BlockSpec((1, MLP_BLOCK, D), mlp_row_map),
                pl.BlockSpec((1, MLP_BLOCK, FF), mlp_row_map),
                pl.BlockSpec((1, MLP_BLOCK, FF), mlp_row_map),
                pl.BlockSpec((1, MLP_BLOCK, FF), mlp_row_map),
            ],
            scratch_shapes=[pltpu.VMEM((MLP_BLOCK, D), F32)],
        ),
        out_shape=[
            shape((dp_size, lanes, D, width), BF16),
            shape((lanes, LANE, D), F32),
            shape((lanes, LANE, FF), BF16),
            shape((lanes, LANE, FF), BF16),
            shape((lanes, LANE, FF), BF16),
        ],
        compiler_params=pltpu.CompilerParams(vmem_limit_bytes=VMEM_LIMIT),
    )(lens, att_t, gate, tokens_t, gains, w_out, w_mlp, w_down)


def mlp_back_kernel(lens, att_t, gate, cot_parts, hidden_in, act_low, gate_slope, up_slope, gains, w_out, w_mlp, w_down,
                    grad_hidden_t, grad_att_t, logit_delta, late, g_gain,
                    back, g_out, g_mlp, g_down_t, stage, pair_rows):
    lane, block = pl.program_id(0), pl.program_id(1)

    @pl.when((lane == 0) & (block == 0))
    def _():
        g_out[...] = jnp.zeros_like(g_out)
        g_mlp[...] = jnp.zeros_like(g_mlp)
        g_down_t[...] = jnp.zeros_like(g_down_t)
        g_gain[...] = jnp.zeros_like(g_gain)

    @pl.when(block * MLP_BLOCK >= lens[lane])
    def _():
        grad_att_t[...] = jnp.zeros_like(grad_att_t)
        logit_delta[...] = jnp.zeros_like(logit_delta)

    @pl.when(block * MLP_BLOCK < lens[lane])
    def _():
        att = att_t[0].reshape(HEADS, HEAD_DIM, MLP_BLOCK)
        sig = jax.nn.sigmoid(gate[0, :HEADS])[:, None, :]
        gated_t = (att * sig).reshape(WIDTH_Q, MLP_BLOCK).astype(BF16)
        hidden = hidden_in[0]
        scale = mean_square_scale(hidden, 1)
        gain = gains[1:2]
        mixed_t = (hidden * scale * gain).astype(BF16).T
        valid_t = lax.broadcasted_iota(jnp.int32, (1, MLP_BLOCK), 1) + block * MLP_BLOCK < lens[lane]
        cot_t = jnp.concatenate([cot_parts[part, 0] for part in range(cot_parts.shape[0])], axis=1)
        grad_low_t = jnp.where(valid_t, cot_t.astype(F32), 0.0).astype(BF16)
        grad_low = grad_low_t.T
        back[...] = jnp.zeros_like(back)

        @pl.loop(0, FF // FF_CHUNK, unroll=True)
        def _(chunk):
            low = pl.ds(pl.multiple_of(chunk * FF_CHUNK, FF_CHUNK), FF_CHUNK)
            high = pl.ds(pl.multiple_of(FF + chunk * FF_CHUNK, FF_CHUNK), FF_CHUNK)
            a = dot(grad_low, w_down[low, :], 1, 1)
            grad_gate = (a * gate_slope[0, :, low].astype(F32)).astype(BF16)
            grad_up = (a * up_slope[0, :, low].astype(F32)).astype(BF16)
            back[...] += dot(grad_gate, w_mlp[:, low], 1, 1) + dot(grad_up, w_mlp[:, high], 1, 1)
            g_mlp[:, low] += dot(mixed_t, grad_gate, 1, 0)
            g_mlp[:, high] += dot(mixed_t, grad_up, 1, 0)
            g_down_t[:, low] += dot(grad_low_t, act_low[0, :, low], 1, 0)

        b = back[...]
        g_gain[0:1] += jnp.sum(b * hidden * scale, axis=0, keepdims=True)
        bg = b * gain
        grad_h = grad_low.astype(F32) + scale * bg - hidden * (scale * scale * scale * jnp.mean(hidden * bg, axis=1, keepdims=True))
        grad_hidden_t[0] = grad_h.T
        branch = grad_h.astype(BF16)
        g_out[...] += dot(gated_t, branch, 1, 0)
        c = dot(w_out[...], branch, 1, 1).reshape(HEADS, HEAD_DIM, MLP_BLOCK)
        grad_att = (c * sig).astype(BF16)
        grad_att_t[0] = grad_att.reshape(WIDTH_Q, MLP_BLOCK)
        sig2 = sig[:, 0, :]
        logit_delta[0, :HEADS] = jnp.sum(c * att, axis=1) * (sig2 * (1.0 - sig2))
        logit_delta[0, 16 : 16 + HEADS] = jnp.sum(grad_att.astype(F32) * att, axis=1)

    @pl.when((lane == pl.num_programs(0) - 1) & (block == pl.num_programs(1) - 1))
    def _():
        @pl.loop(0, WIDTH_Q // (2 * PAIR_STEP))
        def _(piece):
            set_tiles(pair_rows, g_out[pl.ds(pl.multiple_of(piece * 2 * PAIR_STEP, 2 * PAIR_STEP), 2 * PAIR_STEP), :])
            pack_pairs(pair_rows, stage)
            late[pl.ds(pl.multiple_of(piece * PAIR_ROWS, 16), PAIR_ROWS), :] = stage[:PAIR_ROWS].astype(BF16)

        pack_wide(g_mlp, late, stage, OUT_ROWS)

        @pl.loop(0, FF // 128)
        def _(piece):
            turned = g_down_t[:, pl.ds(pl.multiple_of(piece * 128, 128), 128)].T
            for h in range(128 // (2 * PAIR_STEP)):
                set_tiles(pair_rows, turned[h * 2 * PAIR_STEP : (h + 1) * 2 * PAIR_STEP])
                pack_pairs(pair_rows, stage)
                start = OUT_ROWS + MLP_ROWS + (piece * 2 + h) * PAIR_ROWS
                late[pl.ds(pl.multiple_of(start, 16), PAIR_ROWS), :] = stage[:PAIR_ROWS].astype(BF16)

        late[LATE_ROWS:] = jnp.zeros((late.shape[0] - LATE_ROWS, 128), BF16)


def mlp_back(lens, att_t, gate, cot_parts, hidden_in, act_low, gate_slope, up_slope, gains, w_out, w_mlp, w_down, late_rows):
    dp_size, lanes, _, width = cot_parts.shape
    shape = jax.ShapeDtypeStruct
    return pl.pallas_call(
        mlp_back_kernel,
        name="mlp_back",
        grid_spec=pltpu.PrefetchScalarGridSpec(
            num_scalar_prefetch=1,
            grid=(lanes, MLP_BLOCKS),
            in_specs=[
                pl.BlockSpec((1, WIDTH_Q, MLP_BLOCK), mlp_col_map),
                pl.BlockSpec((1, 16, MLP_BLOCK), mlp_col_map),
                pl.BlockSpec((dp_size // MLP_BLOCKS, 1, D, width), kept_part_map),
                pl.BlockSpec((1, MLP_BLOCK, D), mlp_row_map),
                pl.BlockSpec((1, MLP_BLOCK, FF), mlp_row_map),
                pl.BlockSpec((1, MLP_BLOCK, FF), mlp_row_map),
                pl.BlockSpec((1, MLP_BLOCK, FF), mlp_row_map),
                whole((2, D)),
                whole((WIDTH_Q, D)),
                whole((D, 2 * FF)),
                whole((FF, D)),
            ],
            out_specs=[
                pl.BlockSpec((1, D, MLP_BLOCK), mlp_col_map),
                pl.BlockSpec((1, WIDTH_Q, MLP_BLOCK), full_col_map),
                pl.BlockSpec((1, 32, MLP_BLOCK), full_col_map),
                whole((late_rows, 128)),
                whole((8, D)),
            ],
            scratch_shapes=[
                pltpu.VMEM((MLP_BLOCK, D), F32),
                pltpu.VMEM((WIDTH_Q, D), F32),
                pltpu.VMEM((D, 2 * FF), F32),
                pltpu.VMEM((D, FF), F32),
                pltpu.VMEM((WIDE_STEP * WIDE_TILES, 128), F32),
                pltpu.VMEM((5, 2 * PAIR_STEP, 128), F32),
            ],
        ),
        out_shape=[
            shape((lanes, D, LANE), F32),
            shape((lanes, WIDTH_Q, LANE), BF16),
            shape((lanes, 32, LANE), F32),
            shape((late_rows, 128), BF16),
            shape((8, D), F32),
        ],
        compiler_params=pltpu.CompilerParams(vmem_limit_bytes=VMEM_LIMIT),
    )(lens, att_t, gate, cot_parts, hidden_in, act_low, gate_slope, up_slope, gains, w_out, w_mlp, w_down)


def project_back_kernel(lens, dq_t, dk_t, dv_t, logit_delta, raw, tok_t, grad_hidden_t, w_in, gain_cols, head_gains,
                        cosine, sine, grad_tok_t, g_in, g_gain, g_head, dproj, head_sum, gain_sum):
    lane, block = pl.program_id(0), pl.program_id(1)

    @pl.when((lane == 0) & (block == 0))
    def _():
        g_in[...] = jnp.zeros_like(g_in)
        gain_sum[...] = jnp.zeros_like(gain_sum)
        head_sum[...] = jnp.zeros_like(head_sum)

    @pl.when(block * PROJ_BLOCK >= lens[lane])
    def _():
        grad_tok_t[...] = jnp.zeros_like(grad_tok_t)

    @pl.when(block * PROJ_BLOCK < lens[lane])
    def _():
        cos, sin = cosine[...], sine[...]
        for head in range(HEADS + KV_HEADS):
            rows = slice(head * HEAD_DIM, (head + 1) * HEAD_DIM)
            side = 0 if head < HEADS else 1
            source = dq_t if head < HEADS else dk_t
            at = (head if head < HEADS else head - HEADS) * HEAD_DIM
            d1, d2 = source[0, at : at + HALF], source[0, at + HALF : at + HEAD_DIM]
            d = jnp.concatenate([d1 * cos + d2 * sin, d2 * cos - d1 * sin], axis=0)
            u = raw[0, rows]
            r = mean_square_scale(u, 0)
            ur = u * r
            head_sum[side] += d * ur
            dg = d * head_gains[side]
            dproj[rows] = (r * (dg - ur * jnp.mean(ur * dg, axis=0, keepdims=True))).astype(BF16)
        dproj[WIDTH_Q + WIDTH_K : WIDTH_Q + 2 * WIDTH_K] = dv_t[0].astype(BF16)
        row = lax.broadcasted_iota(jnp.int32, (16, PROJ_BLOCK), 0)
        logits = jnp.where(row < HEADS, logit_delta[0], 0.0).astype(BF16)
        dproj[WIDTH_Q + 2 * WIDTH_K :] = jnp.concatenate(
            [logits, jnp.zeros((QKVG_PAD - WIDTH_Q - 2 * WIDTH_K - 16, PROJ_BLOCK), BF16)], axis=0
        )
        x = tok_t[0].astype(F32)
        scale = mean_square_scale(x, 0)
        xs = x * scale
        gain = gain_cols[0]
        normed = (xs * gain).astype(BF16)
        g_in[...] += dot(normed, dproj[...], 1, 1)
        back = dot(w_in[...], dproj[...], 1, 0)
        gain_sum[...] += back * xs
        bg = back * gain
        grad_x = scale * (bg - xs * jnp.mean(xs * bg, axis=0, keepdims=True))
        grad_tok_t[0] = (grad_hidden_t[0] + grad_x).astype(BF16)

    @pl.when((lane == pl.num_programs(0) - 1) & (block == pl.num_programs(1) - 1))
    def _():
        g_head[...] = jnp.sum(head_sum[...], axis=2)
        g_gain[...] = jnp.sum(gain_sum[...], axis=1)[None]


def project_back(lens, dq_t, dk_t, dv_t, logit_delta, raw, tokens_t, grad_hidden_t, w_in, gain_cols, head_gains, cosine, sine):
    lanes = tokens_t.shape[0]
    shape = jax.ShapeDtypeStruct
    full_col = lambda lane, block, lens: (lane, 0, block)
    return pl.pallas_call(
        project_back_kernel,
        name="project_back",
        grid_spec=pltpu.PrefetchScalarGridSpec(
            num_scalar_prefetch=1,
            grid=(lanes, PROJ_BLOCKS),
            in_specs=[
                pl.BlockSpec((1, WIDTH_Q, PROJ_BLOCK), proj_col_map),
                pl.BlockSpec((1, WIDTH_K, PROJ_BLOCK), proj_col_map),
                pl.BlockSpec((1, WIDTH_K, PROJ_BLOCK), proj_col_map),
                pl.BlockSpec((1, 16, PROJ_BLOCK), proj_col_map),
                pl.BlockSpec((1, WIDTH_Q + WIDTH_K, PROJ_BLOCK), proj_col_map),
                pl.BlockSpec((1, D, PROJ_BLOCK), proj_col_map),
                pl.BlockSpec((1, D, PROJ_BLOCK), proj_col_map),
                whole((D, QKVG_PAD)),
                whole((2, D, 1)),
                whole((2, HEAD_DIM, 1)),
                pl.BlockSpec((HALF, PROJ_BLOCK), proj_table_map),
                pl.BlockSpec((HALF, PROJ_BLOCK), proj_table_map),
            ],
            out_specs=[
                pl.BlockSpec((1, D, PROJ_BLOCK), full_col),
                whole((D, QKVG_PAD)),
                whole((1, D)),
                whole((2, HEAD_DIM)),
            ],
            scratch_shapes=[
                pltpu.VMEM((QKVG_PAD, PROJ_BLOCK), BF16),
                pltpu.VMEM((2, HEAD_DIM, PROJ_BLOCK), F32),
                pltpu.VMEM((D, PROJ_BLOCK), F32),
            ],
        ),
        out_shape=[
            shape((lanes, D, LANE), BF16),
            shape((D, QKVG_PAD), F32),
            shape((1, D), F32),
            shape((2, HEAD_DIM), F32),
        ],
        compiler_params=pltpu.CompilerParams(vmem_limit_bytes=VMEM_LIMIT),
    )(lens, dq_t, dk_t, dv_t, logit_delta, raw, tokens_t, grad_hidden_t, w_in, gain_cols, head_gains, cosine, sine)


def layer_forward(tokens_t, lens, weights):
    w_in, gains, head_gains = weights
    gain_cols, head_gains = gains[:, :, None], head_gains[:, :, None]
    cosine, sine = (jnp.asarray(t) for t in rope_tables())
    q_t, k_n, k_t, v_n, v_t, raw, gate = project(lens, tokens_t, w_in, gain_cols, head_gains, cosine, sine)
    att_t, log_total = attend(lens, q_t, k_n, v_t)
    return att_t, gate, (q_t, k_n, k_t, v_n, log_total, raw)


def head_groups(rows):
    return rows[:, :HEADS].reshape(rows.shape[0], KV_HEADS, GROUP, LANE)


SHARD = PARAMS // 4
LANES128 = 128
EDGE = 16
STEP = 6928
BODY = STEP - EDGE
SPAN = STEP + EDGE
IN_ROWS = 4361
SPLIT_AT = D * QKVG
MESH = pl.DeviceIdType.MESH


def shard_shift(s):
    offset = EDGE * LANES128 - (STEP * LANES128 - SHARD) * s + (64 if s else 0)
    return offset // LANES128, offset % LANES128


def flip(index, bit):
    return index + (1 - 2 * (index // (1 << bit) % 2)) * (1 << bit)


def bit_of(index, bit):
    return index // (1 << bit) % 2


def greet(partners):
    barrier = pltpu.get_barrier_semaphore()
    for partner in partners:
        pl.semaphore_signal(barrier, inc=1, device_id=partner, device_id_type=MESH)
    pl.semaphore_wait(barrier, len(partners))


PACK_TILE = 496
FIRST_ROWS = 4368
LAST_TILE = 32
GAIN_AT = EDGE + IN_ROWS + LATE_ROWS - 3 * STEP - (SPAN - LAST_TILE)
FIRST_CUTS = (0, 1088, 2176, 3264, FIRST_ROWS)


def pack_kernel(master, own, first_rows, last_rows, rows_in, packed, load_sem, keep_sem, own_sem, send_sem, recv_sem):
    dp, zero = lax.axis_index("dp"), lax.axis_index("zero")
    core, across, side = (dp, flip(zero, 0)), (dp, flip(zero, 1)), (flip(dp, 0), zero)
    y = bit_of(dp, 0)
    load = pltpu.make_async_copy(master, rows_in.at[pl.ds(24, STEP)], load_sem)
    load.start()
    rows_in[:24] = jnp.zeros((24, LANES128), F32)
    rows_in[24 + STEP :] = jnp.zeros((24, LANES128), F32)
    greet((core, across, side))
    load.wait()
    lane = lax.broadcasted_iota(jnp.int32, (PACK_TILE, LANES128), 1)

    def shifted(start, a, k):
        if k == 0:
            return rows_in[pl.ds(start + 24 - a, PACK_TILE), :]
        here = pltpu.roll(rows_in[pl.ds(start + 24 - a, PACK_TILE), :], k, 1)
        above = pltpu.roll(rows_in[pl.ds(start + 23 - a, PACK_TILE), :], k, 1)
        return jnp.where(lane >= k, here, above)

    def pack(s, start):
        if s == 0 and start + PACK_TILE <= EDGE + IN_ROWS:
            value = shifted(start, EDGE, 0)
        elif s == 0 and start < EDGE + IN_ROWS:
            row = lax.broadcasted_iota(jnp.int32, (PACK_TILE, LANES128), 0) + start
            value = jnp.where(row < EDGE + IN_ROWS, shifted(start, EDGE, 0), shifted(start, EDGE, 64))
        elif s == 0:
            value = shifted(start, EDGE, 64)
        else:
            value = shifted(start, *shard_shift(s))
        packed[pl.ds(start, PACK_TILE), :] = value.astype(BF16)

    def piece_rows(piece):
        return pl.ds(EDGE + FIRST_CUTS[piece], FIRST_CUTS[piece + 1] - FIRST_CUTS[piece])

    def mine(piece):
        return packed.at[piece_rows(piece)]

    def theirs(piece):
        return first_rows.at[piece_rows(piece)]

    def copy(source, target, device, slot):
        return pltpu.make_async_remote_copy(source, target, send_sem.at[slot], recv_sem.at[slot],
                                            device_id=device, device_id_type=MESH)

    for s in range(4):

        @pl.when(zero == s)
        def _():
            for t in range(SPAN // PACK_TILE):
                pack(s, t * PACK_TILE)

    keep = pltpu.make_async_copy(packed, own, own_sem)
    keep.start()
    tail = packed.at[pl.ds(SPAN - LAST_TILE, LAST_TILE)]

    @pl.when(zero == 3)
    def _():
        copy(tail, last_rows, across, 9).start()
        copy(tail, last_rows, core, 8).start()
        stay = pltpu.make_async_copy(tail, last_rows, keep_sem)
        stay.start()
        stay.wait()
        copy(tail, last_rows, across, 9).wait_send()
        copy(tail, last_rows, core, 8).wait_send()

    @pl.when(zero == 1)
    def _():
        copy(last_rows, last_rows, across, 9).wait_recv()
        copy(last_rows, last_rows, core, 8).start()
        copy(last_rows, last_rows, core, 8).wait_send()

    for half in range(2):
        pieces = (2 * half, 2 * half + 1)
        others = (2 - 2 * half, 3 - 2 * half)

        @pl.when((zero == 0) & (y == half))
        def _():
            for piece in pieces:
                copy(mine(piece), theirs(piece), across, piece).start()
            for piece in range(4):
                copy(mine(piece), theirs(piece), core, 4 + piece).start()
            stay = pltpu.make_async_copy(packed.at[pl.ds(EDGE, FIRST_ROWS)], first_rows.at[pl.ds(EDGE, FIRST_ROWS)], keep_sem)
            stay.start()
            for piece in pieces:
                copy(mine(piece), theirs(piece), across, piece).wait_send()
            for piece in range(4):
                copy(mine(piece), theirs(piece), core, 4 + piece).wait_send()
            stay.wait()

        @pl.when((zero == 2) & (y == half))
        def _():
            for piece in pieces:
                copy(theirs(piece), theirs(piece), across, piece).wait_recv()
                copy(theirs(piece), theirs(piece), side, piece).start()
                copy(theirs(piece), theirs(piece), core, 4 + piece).start()
            for piece in others:
                copy(theirs(piece), theirs(piece), side, piece).wait_recv()
                copy(theirs(piece), theirs(piece), core, 4 + piece).start()
            for piece in pieces:
                copy(theirs(piece), theirs(piece), side, piece).wait_send()
            for piece in range(4):
                copy(theirs(piece), theirs(piece), core, 4 + piece).wait_send()

    @pl.when(bit_of(zero, 0) == 0)
    def _():
        copy(last_rows, last_rows, core, 8).wait_recv()

    @pl.when(bit_of(zero, 0) == 1)
    def _():
        for piece in range(4):
            copy(theirs(piece), theirs(piece), core, 4 + piece).wait_recv()

    keep.wait()


def pack_master(master):
    rows = jnp.pad(master, (0, STEP * LANES128 - SHARD)).reshape(STEP, LANES128)
    shape = jax.ShapeDtypeStruct
    return pl.pallas_call(
        pack_kernel,
        name="pack_master",
        out_shape=[shape((SPAN, LANES128), BF16), shape((EDGE + FIRST_ROWS, LANES128), BF16), shape((LAST_TILE, LANES128), BF16)],
        in_specs=[pl.BlockSpec(memory_space=pl.ANY)],
        out_specs=[pl.BlockSpec(memory_space=pl.ANY)] * 3,
        scratch_shapes=[
            pltpu.VMEM((24 + STEP + 24, LANES128), F32),
            pltpu.VMEM((SPAN, LANES128), BF16),
            pltpu.SemaphoreType.DMA,
            pltpu.SemaphoreType.DMA,
            pltpu.SemaphoreType.DMA,
            pltpu.SemaphoreType.DMA((10,)),
            pltpu.SemaphoreType.DMA((10,)),
        ],
        cost_estimate=pl.CostEstimate(flops=0, bytes_accessed=0, transcendentals=0),
        compiler_params=pltpu.CompilerParams(collective_id=0, has_side_effects=True, vmem_limit_bytes=VMEM_LIMIT),
    )(rows)


REDUCE_PARTS = 11


def window_start(s):
    return jnp.minimum(s, 1) * (((s * SHARD + 64) // LANES128 - IN_ROWS) // 16 * 16)


LAST_WINDOW = ((3 * SHARD + 64) // LANES128 - IN_ROWS) // 16 * 16


def window_rows(dp_size):
    unit = REDUCE_PARTS * 16 * dp_size
    return -(-(SHARD // LANES128 + 17) // unit) * unit


CLASSES = ((0, 6), (6, 5))


def bit_order(bits, kind):
    order = list(range(bits))
    if kind and bits > 1:
        order[0], order[1] = 1, 0
    return order


def part_region(dp, rows, bits, kind, count):
    offset, size = 0, rows
    for k in bit_order(bits, kind)[:count]:
        size = size // 2
        offset = offset + bit_of(dp, k) * size
    return offset, size


def aligned(offset, size):
    return pl.ds(pl.multiple_of(offset, 16), size)


def zero_sum(rows, late, window, own, first, second, local_sem, send_sem, recv_sem):
    dp, zero = lax.axis_index("dp"), lax.axis_index("zero")
    core, across = (dp, flip(zero, 0)), (dp, flip(zero, 1))
    low, high = bit_of(zero, 0), bit_of(zero, 1)
    parts = range(REDUCE_PARTS)

    def local(h, part):
        source = late.at[aligned(window_start(2 * h + low) + part * rows, rows)]
        return pltpu.make_async_copy(source, own.at[part, h], local_sem.at[h, part])

    def flight(step, part):
        if step < 2:
            source = late.at[aligned(window_start(2 * step + 1 - low) + part * rows, rows)]
            target, device = first.at[part, step], core
        else:
            source, target, device = own.at[part, 1 - high], second.at[part], across
        return pltpu.make_async_remote_copy(source, target, send_sem.at[step, part], recv_sem.at[step, part],
                                            device_id=device, device_id_type=MESH)

    def begin():
        greet([core, across])
        for part in parts:
            for h in range(2):
                flight(h, part).start()
                local(h, part).start()

    def receive(step, part):
        if step == 1:
            for h in range(2):
                local(h, part).wait()
                flight(h, part).wait_recv()
            for h in range(2):
                own[part, h] = (own[part, h].astype(F32) + first[part, h].astype(F32)).astype(BF16)
            flight(2, part).start()
        else:
            flight(2, part).wait_recv()
            window[part] = (own[part, high].astype(F32) + second[part].astype(F32)).astype(BF16)

    def finish():
        for part in parts:
            for step in range(3):
                flight(step, part).wait_send()

    return begin, receive, finish


LATE_HOP = 12.0
HOP = 1.5


def arrival_order(chains, hops):
    free, order = {}, []
    pending = [(0.0, index, 0) for index in range(len(chains))]
    while pending:
        pending.sort()
        start, index, step = pending.pop(0)
        link, span = chains[index][step]
        end = max(start, free.get(link, 0.0)) + span
        free[link] = end
        hop = hops[index]
        order.append((end + hop, index, step))
        if step + 1 < len(chains[index]):
            pending.append((end + hop, index, step + 1))
    return sorted(order)


SLOTS = (((0, 0), 0.13), ((0, 2), 0.4), ((1, 2), 0.7), ((3, 2), 1.0))


def receive_slots(step_us):
    chains = [[("core", 0.8), ("x", 40.0 / REDUCE_PARTS)]] * REDUCE_PARTS
    ends = [(step + done) * step_us for step in range(LANE_STEPS) for _, done in SLOTS]
    table = [[] for _ in ends]
    place = 0
    for at, part, step in arrival_order(chains, [HOP] * len(chains)):
        while place + 1 < len(ends) and ends[place] < at:
            place += 1
        table[place].append((step + 1, part))
    return table


def attend_back_kernel(rows, q_t, k_n, k_t, v_n, grad_t, log_total, delta, late, dq_t, dk_t, dv_t, window,
                       own, first, second, local_sem, send_sem, recv_sem):
    begin, receive, finish = zero_sum(rows, late, window, own, first, second, local_sem, send_sem, recv_sem)
    step = pl.program_id(0) * KV_HEADS + pl.program_id(1)
    table = receive_slots(8.6)
    pl.when(step == 0)(begin)
    dq_t[...] = jnp.zeros_like(dq_t)

    def advance(slot):
        for place in range(slot, len(table), len(SLOTS)):
            if table[place]:

                @pl.when(step == place // len(SLOTS))
                def _():
                    for receipt in table[place]:
                        receive(*receipt)

    for block in range(BLOCKS):
        keys = pl.ds(block * BLOCK, BLOCK)
        k_rows, v_rows, k_cols = k_n[0, 0, keys, :], v_n[0, 0, keys, :], k_t[0, :, keys]
        dk = jnp.zeros((HEAD_DIM, BLOCK), F32)
        dv = jnp.zeros((HEAD_DIM, BLOCK), F32)
        for r in range(GROUP):
            head = slice(r * HEAD_DIM, (r + 1) * HEAD_DIM)
            for part in range(block, BLOCKS):
                cols = pl.ds(part * BLOCK, BLOCK)
                query, grad = q_t[0, head, cols], grad_t[0, head, cols]
                logs = log_total[0, 0, r : r + 1, cols]
                prob = jnp.exp2(dot(k_rows, query, 1, 0) * EXP_SCALE - logs)
                if part == block:
                    prob = causal_tile(prob, 0.0)
                grad_prob = dot(v_rows, grad, 1, 0) - delta[0, 0, r : r + 1, cols]
                grad_score = (prob * grad_prob).astype(BF16)
                dv += dot(grad, prob.astype(BF16), 1, 1)
                dk += dot(query, grad_score, 1, 1)
                dq_t[0, head, cols] += dot(k_cols, grad_score, 1, 0) * SCALE
            for slot, (after, _) in enumerate(SLOTS):
                if after == (block, r) and r + 1 < GROUP:
                    advance(slot)
        dk_t[0, :, keys] = dk * SCALE
        dv_t[0, :, keys] = dv
        for slot, (after, _) in enumerate(SLOTS):
            if after == (block, GROUP - 1):
                advance(slot)
    pl.when(step == LANE_STEPS - 1)(finish)


LANE_STEPS = 2 * KV_HEADS


def attend_back(q_t, k_n, k_t, v_n, grad_t, log_total, delta, late, dp_size):
    lanes = q_t.shape[0]
    rows = window_rows(dp_size) // REDUCE_PARTS
    shape = jax.ShapeDtypeStruct
    group_rows = lambda lane, g: (lane, g, 0)
    group_heads = lambda lane, g: (lane, g, 0, 0)
    held = lambda *dims: pltpu.VMEM((REDUCE_PARTS, *dims, LANES128), BF16)
    return pl.pallas_call(
        functools.partial(attend_back_kernel, rows),
        name="attend_back",
        grid=(lanes, KV_HEADS),
        in_specs=[
            pl.BlockSpec((1, GROUP * HEAD_DIM, LANE), group_rows),
            pl.BlockSpec((1, 1, LANE, HEAD_DIM), group_heads),
            pl.BlockSpec((1, HEAD_DIM, LANE), group_rows),
            pl.BlockSpec((1, 1, LANE, HEAD_DIM), group_heads),
            pl.BlockSpec((1, GROUP * HEAD_DIM, LANE), group_rows),
            pl.BlockSpec((1, 1, GROUP, LANE), group_heads),
            pl.BlockSpec((1, 1, GROUP, LANE), group_heads),
            pl.BlockSpec(memory_space=pl.ANY),
        ],
        out_specs=[
            pl.BlockSpec((1, GROUP * HEAD_DIM, LANE), group_rows),
            pl.BlockSpec((1, HEAD_DIM, LANE), group_rows),
            pl.BlockSpec((1, HEAD_DIM, LANE), group_rows),
            whole((REDUCE_PARTS, rows, LANES128)),
        ],
        out_shape=[
            shape((lanes, WIDTH_Q, LANE), F32),
            shape((lanes, WIDTH_K, LANE), F32),
            shape((lanes, WIDTH_K, LANE), F32),
            shape((REDUCE_PARTS, rows, LANES128), BF16),
        ],
        scratch_shapes=[
            held(2, rows),
            held(2, rows),
            held(rows),
            pltpu.SemaphoreType.DMA((2, REDUCE_PARTS)),
            pltpu.SemaphoreType.DMA((3, REDUCE_PARTS)),
            pltpu.SemaphoreType.DMA((3, REDUCE_PARTS)),
        ],
        compiler_params=pltpu.CompilerParams(collective_id=1, has_side_effects=True, vmem_limit_bytes=VMEM_LIMIT),
    )(q_t, k_n, k_t, v_n, grad_t, log_total, delta, late)


TAIL_AT = 4368


HEAD_PARTS = 3
HEAD_HOP = 3.0
LATE_GROUPS = ((0, 0, 3), (1, 0, 3), (0, 3, 3), (1, 3, 2))


def head_rows(dp_size):
    unit = 2 * HEAD_PARTS * 16 * 2 * dp_size
    return -(-(TAIL_AT + 16) // unit) * unit


def sum_head_kernel(bits, rows, late_rows, source, gain_rows, share_one, share_two, result, late_sum, total, *rest):
    received, (load_sem, send_sem, recv_sem, late_send, late_recv) = rest[:-5], rest[-5:]
    dp, zero = lax.axis_index("dp"), lax.axis_index("zero")
    axes = [("zero", 1)] + [("dp", k) for k in range(bits)]

    def partner(axis, k):
        return (flip(dp, k), zero) if axis == "dp" else (dp, flip(zero, k))

    def bit(axis, k):
        return bit_of(dp if axis == "dp" else zero, k)

    load = pltpu.make_async_copy(source, total, load_sem)
    load.start()
    load.wait()
    total[TAIL_AT : TAIL_AT + 16] = gain_rows[...]
    greet([partner("zero", 0)] + [partner(*axis) for axis in axes])

    def step(index, slot, source_ref, target_ref, axis):
        copy = pltpu.make_async_remote_copy(source_ref, target_ref, send_sem.at[index, slot], recv_sem.at[index, slot],
                                            device_id=partner(*axis), device_id_type=MESH)
        copy.start()
        return copy

    def order_of(index):
        return [("zero", 0)] + [axes[(index + j) % len(axes)] for j in range(len(axes))]

    def spans_of(index):
        spans = [(axis, 0.5 if axis == ("zero", 0) else 9.0 / HEAD_PARTS / (1 << slot)) for slot, axis in enumerate(order_of(index))]
        return spans + spans[::-1]

    def chain_of(index):
        order = order_of(index)
        size = rows // HEAD_PARTS
        offset = index * size
        regions = []
        for slot, axis in enumerate(order):
            half = size // 2
            mine, other = offset + bit(*axis) * half, offset + (1 - bit(*axis)) * half
            landing = received[slot].at[index]
            yield step(index, slot, total.at[aligned(other, half)], landing, axis)
            at = aligned(mine, half)
            target = total if slot + 1 < len(order) else result
            target[at] = (total[at].astype(F32) + landing[...].astype(F32)).astype(BF16)
            offset, size = mine, half
            regions.append(at)
        for slot in reversed(range(len(order))):
            place = result.at[regions[slot]]
            yield step(index, 2 * len(order) - 1 - slot, place, place, order[slot])

    def late_spans(index):
        kind, _, count = LATE_GROUPS[index]
        spans = [(("dp", k), 20.0 / (1 << slot) * count / REDUCE_PARTS) for slot, k in enumerate(bit_order(bits, kind))]
        return spans[::-1]

    def late_chain(index):
        kind, start, count = LATE_GROUPS[index]
        parts = pl.ds(CLASSES[kind][0] + start, count)
        share = (share_one, share_two)[kind]
        late_sum[parts, aligned(*part_region(dp, late_rows, bits, kind, bits))] = share[start : start + count]
        for slot, k in reversed(list(enumerate(bit_order(bits, kind)))):
            place = late_sum.at[parts, aligned(*part_region(dp, late_rows, bits, kind, slot + 1))]
            copy = pltpu.make_async_remote_copy(place, place, late_send.at[index, slot], late_recv.at[index, slot],
                                                device_id=partner("dp", k), device_id_type=MESH)
            copy.start()
            yield copy

    chains = [chain_of(i) for i in range(HEAD_PARTS)] + [late_chain(i) for i in range(len(LATE_GROUPS))]
    spans = [spans_of(i) for i in range(HEAD_PARTS)] + [late_spans(i) for i in range(len(LATE_GROUPS))]
    flying = [next(chain) for chain in chains]
    sent = list(flying)
    for _, index, _ in arrival_order(spans, [HEAD_HOP] * HEAD_PARTS + [LATE_HOP] * len(LATE_GROUPS)):
        flying[index].wait_recv()
        following = next(chains[index], None)
        if following is not None:
            flying[index] = following
            sent.append(following)
    for copy in sent:
        copy.wait_send()


def sum_head(source, gain_rows, shares, late_rows, dp_size):
    bits = dp_size.bit_length() - 1
    rows = source.shape[0]
    steps = bits + 2
    shape = jax.ShapeDtypeStruct
    return pl.pallas_call(
        functools.partial(sum_head_kernel, bits, rows, late_rows),
        name="sum_head",
        out_shape=[shape((rows, LANES128), BF16), shape((REDUCE_PARTS, late_rows, LANES128), BF16)],
        in_specs=[pl.BlockSpec(memory_space=pl.ANY)] + [pl.BlockSpec(memory_space=pltpu.VMEM)] * 3,
        out_specs=[pl.BlockSpec(memory_space=pltpu.VMEM)] * 2,
        scratch_shapes=[
            pltpu.VMEM((rows, LANES128), BF16),
            *[pltpu.VMEM((HEAD_PARTS, rows // HEAD_PARTS >> (k + 1), LANES128), BF16) for k in range(steps)],
            pltpu.SemaphoreType.DMA,
            pltpu.SemaphoreType.DMA((HEAD_PARTS, 2 * steps)),
            pltpu.SemaphoreType.DMA((HEAD_PARTS, 2 * steps)),
            pltpu.SemaphoreType.DMA((len(LATE_GROUPS), bits)),
            pltpu.SemaphoreType.DMA((len(LATE_GROUPS), bits)),
        ],
        compiler_params=pltpu.CompilerParams(collective_id=2, has_side_effects=True, vmem_limit_bytes=VMEM_LIMIT),
    )(source, gain_rows, *shares)


def flat_rows(g_in, rows):
    flat = g_in[:, :QKVG].astype(BF16).reshape(-1)
    return jnp.pad(flat, (0, rows * LANES128 - SPLIT_AT)).reshape(rows, LANES128)


def pack_gains(g_gain_one, g_gain_two, g_head):
    flat = jnp.concatenate([g_gain_one[0], g_gain_two[0], g_head.reshape(-1)]).astype(BF16)
    return jnp.pad(flat.reshape(10, LANES128), ((0, 6), (0, 0)))


def unpack_shard(late, head, zero_rank):
    late = late.reshape(-1)
    head_flat = head.reshape(-1)
    starts = [s * SHARD - SPLIT_AT - LANES128 * max(0, ((s * SHARD + 64) // LANES128 - IN_ROWS) // 16 * 16) for s in range(1, 4)]
    tail = head_flat[TAIL_AT * LANES128 : (TAIL_AT + 10) * LANES128]

    def pick(s):
        if s == 0:
            return lambda: jnp.concatenate([head_flat[:SPLIT_AT], late[: SHARD - SPLIT_AT]])
        if s == 3:
            return lambda: jnp.concatenate([late[starts[2] : starts[2] + SHARD - 10 * LANES128], tail])
        return lambda: late[starts[s - 1] : starts[s - 1] + SHARD]

    return lax.switch(zero_rank, [pick(s) for s in range(4)]).astype(F32)


UNPACK_SKEW = (EDGE + IN_ROWS) % 16


def unpack_kernel(own, near, far, both, w_out, w_mlp, w_down, packed, edges, stage, pair_rows, load_sem, edge_sem):
    zero = lax.axis_index("zero")
    shards = [(own, zero), (near, flip(zero, 0)), (far, flip(zero, 1)), (both, flip(flip(zero, 0), 1))]
    loads = [
        pltpu.make_async_copy(shard.at[pl.ds(EDGE, BODY)], packed.at[pl.ds(pl.multiple_of(STEP * s + EDGE, 16), BODY)], load_sem.at[k])
        for k, (shard, s) in enumerate(shards)
    ]
    ends = [pltpu.make_async_copy(shard.at[pl.ds(at, EDGE)], edges.at[s, h], edge_sem.at[k, h])
            for k, (shard, s) in enumerate(shards) for h, at in enumerate((0, EDGE + BODY))]
    for copy in ends + loads:
        copy.start()
    for copy in ends:
        copy.wait()
    packed[:EDGE] = edges[0, 0]
    for s in range(4):
        tile = edges[s, 1].astype(F32)
        if s < 3:
            tile = tile + edges[s + 1, 0].astype(F32)
        packed[pl.ds(STEP * (s + 1), EDGE), :] = tile.astype(BF16)
    for copy in loads:
        copy.wait()

    def fetch(first_row, count):
        stage[: count + 16] = packed[pl.ds(pl.multiple_of(first_row - UNPACK_SKEW, 16), count + 16), :].astype(F32)

    def split_pairs(first_row, target, row):
        fetch(first_row, PAIR_ROWS)
        tiles = [stage[pl.ds(UNPACK_SKEW + t, PAIR_STEP, stride=9), :] for t in range(9)]
        even, odd = pl.ds(0, PAIR_STEP, stride=2), pl.ds(1, PAIR_STEP, stride=2)
        for t in range(4):
            pair_rows[t, even, :] = tiles[t]
        pair_rows[4, even, :] = tiles[4]
        for t in range(4):
            pair_rows[t, odd, :] = jnp.concatenate([tiles[4 + t][:, 64:], tiles[5 + t][:, :64]], axis=1)
        pair_rows[4, odd, :] = jnp.concatenate([tiles[8][:, 64:], tiles[8][:, :64]], axis=1)
        at = pl.ds(pl.multiple_of(row, 2 * PAIR_STEP), 2 * PAIR_STEP)
        for t in range(4):
            target[at, t * 128 : (t + 1) * 128] = pair_rows[t].astype(BF16)
        target[at, 512:] = pair_rows[4, :, :64].astype(BF16)

    out_at = EDGE + IN_ROWS
    mlp_at = out_at + OUT_ROWS
    down_at = mlp_at + MLP_ROWS

    @pl.loop(0, WIDTH_Q // (2 * PAIR_STEP))
    def _(piece):
        split_pairs(out_at + piece * PAIR_ROWS, w_out, piece * 2 * PAIR_STEP)

    @pl.loop(0, FF // (2 * PAIR_STEP))
    def _(piece):
        split_pairs(down_at + piece * PAIR_ROWS, w_down, piece * 2 * PAIR_STEP)

    @pl.loop(0, D // WIDE_STEP)
    def _(piece):
        fetch(mlp_at + piece * WIDE_STEP * WIDE_TILES, WIDE_STEP * WIDE_TILES)
        rows = pl.ds(pl.multiple_of(piece * WIDE_STEP, WIDE_STEP), WIDE_STEP)
        for tile in range(WIDE_TILES):
            w_mlp[rows, tile * 128 : (tile + 1) * 128] = stage[pl.ds(UNPACK_SKEW + tile, WIDE_STEP, stride=WIDE_TILES), :].astype(BF16)


def unpack_weights(shards):
    shape = jax.ShapeDtypeStruct
    return pl.pallas_call(
        unpack_kernel,
        name="unpack_weights",
        in_specs=[pl.BlockSpec(memory_space=pl.ANY)] * 4,
        out_shape=[shape((WIDTH_Q, D), BF16), shape((D, 2 * FF), BF16), shape((FF, D), BF16)],
        scratch_shapes=[
            pltpu.VMEM((3 * STEP + SPAN, LANES128), BF16),
            pltpu.VMEM((4, 2, EDGE, LANES128), BF16),
            pltpu.VMEM((WIDE_STEP * WIDE_TILES + 16, 128), F32),
            pltpu.VMEM((5, 2 * PAIR_STEP, 128), F32),
            pltpu.SemaphoreType.DMA((4,)),
            pltpu.SemaphoreType.DMA((4, 2)),
        ],
        cost_estimate=pl.CostEstimate(flops=0, bytes_accessed=0, transcendentals=0),
        compiler_params=pltpu.CompilerParams(vmem_limit_bytes=VMEM_LIMIT),
    )(*shards)


def column_parts(lanes_t, dp_size):
    seqs, width, columns = lanes_t.shape
    return lanes_t.reshape(seqs, width, dp_size, columns // dp_size).transpose(2, 0, 1, 3)


def spread(parts):
    return lax.all_to_all(parts, "dp", split_axis=0, concat_axis=0, tiled=True)


def regroup(parts, order):
    dp_size, seqs, width, columns = parts.shape
    parts = jnp.take(parts.reshape(dp_size * seqs, width, columns), order, axis=0, mode="clip")
    return lax.all_to_all(parts.reshape(dp_size, seqs, width, columns), "dp", split_axis=0, concat_axis=0, tiled=True)


def joined(parts):
    dp_size, seqs, width, rows = parts.shape
    return parts.transpose(1, 2, 0, 3).reshape(seqs, width, dp_size * rows)


def exchange(values, axis, bit):
    return lax.ppermute(values, axis, [(i, i ^ (1 << bit)) for i in range(lax.axis_size(axis))])


def quarter(parts, dp_rank, order):
    size = parts.shape[1] // 4

    def rows_of(flips):
        first, second = (bit_of(dp_rank, bit) ^ flip for bit, flip in zip(order, flips))
        return lax.dynamic_slice_in_dim(parts, first * (2 * size) + second * size, size, 1)

    def sent(flips):
        mask = sum(flip << bit for bit, flip in zip(order, flips))
        return lax.ppermute(rows_of(flips), "dp", [(i, i ^ mask) for i in range(lax.axis_size("dp"))])

    return [rows_of((0, 0)), sent((1, 0)), sent((0, 1)), sent((1, 1))]


def halve(parts, dp_rank, bit):
    half = parts.shape[1] // 2
    mine = bit_of(dp_rank, bit)
    sent = lax.dynamic_slice_in_dim(parts, (1 - mine) * half, half, 1)
    return [lax.dynamic_slice_in_dim(parts, mine * half, half, 1), exchange(sent, "dp", bit)]


def added(pieces):
    return sum(piece.astype(F32) for piece in pieces).astype(BF16)


def unpack_first(first_rows, last_rows):
    w_in = first_rows[EDGE : EDGE + IN_ROWS].reshape(-1)[:SPLIT_AT].reshape(D, QKVG)
    w_in = jnp.pad(w_in, ((0, 0), (0, QKVG_PAD - QKVG)))
    rows = last_rows[GAIN_AT : GAIN_AT + 10].astype(F32)
    return w_in, rows[:9].reshape(2, D), rows[9].reshape(2, HEAD_DIM)


def local(tokens, cotangent, lengths, balance, master, moment_one, moment_two):
    dp_rank, zero_rank = lax.axis_index("dp"), lax.axis_index("zero")
    dp_size, zero_size = lax.axis_size("dp"), lax.axis_size("zero")
    seqs = tokens.shape[0]
    order = lax.dynamic_index_in_dim(balance, zero_rank, 0, keepdims=False)
    inverse = jnp.zeros_like(order).at[order].set(jnp.arange(order.shape[0], dtype=order.dtype))
    lens = lax.dynamic_slice_in_dim(lengths, (dp_rank * zero_size + zero_rank) * seqs, seqs)
    tokens_t = tokens.swapaxes(1, 2)
    cot_parts = spread(column_parts(cotangent.swapaxes(1, 2), dp_size))
    own, first_rows, last_rows = pack_master(master)
    far, near = exchange(own, "zero", 1), exchange(own, "zero", 0)
    first = unpack_first(first_rows, last_rows)
    att_t, gate, kept = layer_forward(tokens_t, lens, first)
    far, near, att_t, cot_parts = lax.optimization_barrier((far, near, att_t, cot_parts))
    both = exchange(far, "zero", 0)
    cot_here = regroup(cot_parts, inverse)
    w_out, w_mlp, w_down = unpack_weights((own, near, far, both))
    w_in, gains, head_gains = first
    gain_cols, head_gains = gains[:, :, None], head_gains[:, :, None]
    out_columns, *stash = mlp(lens, att_t, gate, tokens_t, gains, w_out, w_mlp, w_down, dp_size)
    output_parts = spread(out_columns)
    grad_hidden_t, grad_att_t, logit_delta, late, g_gain_two = mlp_back(
        lens, att_t, gate, cot_here, *stash, gains, w_out, w_mlp, w_down, LAST_WINDOW + window_rows(dp_size))
    output_parts, grad_att_t = lax.optimization_barrier((output_parts, grad_att_t))
    output_parts = regroup(output_parts, order)
    q_t, k_n, k_t, v_n, log_total, raw = kept
    dq_t, dk_t, dv_t, window = attend_back(
        q_t, k_n, k_t, v_n, grad_att_t, head_groups(log_total), head_groups(logit_delta[:, 16:]), late, dp_size)
    output_parts, dq_t = lax.optimization_barrier((output_parts, dq_t))
    dp_bits = dp_size.bit_length() - 1
    orders = [bit_order(dp_bits, kind) for kind in range(2)]
    pieces = [quarter(window[at : at + count], dp_rank, orders[kind][:2]) for kind, (at, count) in enumerate(CLASSES)]
    cosine, sine = (jnp.asarray(t) for t in rope_tables())
    grad_tokens_t, g_in, g_gain_one, g_head = project_back(
        lens, dq_t, dk_t, dv_t, logit_delta, raw, tokens_t, grad_hidden_t, w_in, gain_cols, head_gains, cosine, sine)
    pieces, g_in = lax.optimization_barrier((pieces, g_in))
    shares = [added(piece) for piece in pieces]
    head = flat_rows(g_in, head_rows(dp_size))
    gain_rows = pack_gains(g_gain_one, g_gain_two, g_head)
    for step in range(2, dp_bits):
        pieces = [halve(share, dp_rank, order[step]) for share, order in zip(shares, orders)]
        pieces, head, gain_rows = lax.optimization_barrier((pieces, head, gain_rows))
        shares = [added(piece) for piece in pieces]
    grad_tokens = grad_tokens_t.swapaxes(1, 2)
    head_sum, late_sum = sum_head(head, gain_rows, shares, window.shape[1], dp_size)
    output = joined(output_parts).swapaxes(1, 2)
    grad_shard = unpack_shard(late_sum, head_sum, zero_rank)
    gain_width = D // zero_size
    gain_sums = head_sum[TAIL_AT : TAIL_AT + 9].reshape(2, zero_size, gain_width)
    grad_gains = lax.dynamic_index_in_dim(gain_sums, zero_rank, 1, keepdims=False).astype(F32)
    next_one = BETA_ONE * moment_one + (1.0 - BETA_ONE) * grad_shard
    next_two = BETA_TWO * moment_two + (1.0 - BETA_TWO) * grad_shard * grad_shard
    update_dir = next_one / BIAS_ONE / jnp.sqrt(next_two / BIAS_TWO)
    return output, grad_tokens, grad_shard, update_dir, next_one, next_two, grad_gains


def solution(mesh):
    lanes = P(("dp", "zero"), None, None)
    return jax.shard_map(
        local,
        mesh=mesh,
        in_specs=(lanes, lanes, P(), P(), P("zero"), P("zero"), P("zero")),
        out_specs=(lanes, lanes, P("zero"), P("zero"), P("zero"), P("zero"), P(None, "zero")),
        check_vma=False,
    )
```

time: 1520 us -> 383 us (0.25)
  waiting for transfers between devices: 477 us -> 32 us
  matrix products: 321 us -> 0 us
  local copies, waits for them, and re-layouts: 307 us -> 37.4 us
  Pallas kernels: 0 us -> 251 us
  blocking collectives: 190 us -> 0 us
  other arithmetic: 177 us -> 15.8 us
  starting transfers between devices: 13.1 us -> 39.3 us
  between operations: 16.6 us -> 1.24 us
    unnamed x5 -> x0, waiting for transfers between devices: 372 us -> none
    dot_general x40 -> x0, matrix products: 321 us -> none  [the longest x4 52.3 us: attend_back(): jnp.einsum('qkrd,nkd->krqn', grad_slice, value_low, preferred_element_typ...]
    pallas_call x0 -> x9, Pallas kernels: none -> 251 us  [the longest x1 56.5 us: attend_back(): pl.pallas_call(functools.partial(attend_back_kernel, rows), name='attend_...]
    psum x1 -> x0, blocking collectives: 183 us -> none  [local(): grad_shard, gain_shard = lax.psum((grad_part, gain_part), 'dp')]
    concatenate x1, local copies, waits for them, and re-layouts: 115 us -> 0.09 us  [pack_gains(): jnp.concatenate([g_gain_one[0], g_gain_two[0], g_head.reshape(-1)])]
    psum x1 -> x0, waiting for transfers between devices: 94.8 us -> none  [local(): grad_shard, gain_shard = lax.psum((grad_part, gain_part), 'dp')]
    convert_element_type x8 -> x6, other arithmetic: 70.5 us -> 3.32 us  [the longest x4 2.74 us: added(): return sum((piece.astype(F32) for piece in pieces)).astype(BF16)]
    unnamed x159 -> x19, local copies, waits for them, and re-layouts: 53.9 us -> 2.08 us
  transfers between devices with their start and end apart: 5 -> 15, of which waited for: 4 -> 5; matrix products, arithmetic and copies ran while one was open for 7% -> 7% of each run, Pallas kernels for 0% -> 52%
where the time goes in v1:
time: 383 us; the launch traced here: 377 us
  Pallas kernels  251 us (66%)
  starting transfers between devices  39.3 us (10%)
  local copies, waits for them, and re-layouts  37.4 us (10%)
  waiting for transfers between devices  32 us (8%)
  other arithmetic  15.8 us (4%)
    pallas_call x1, Pallas kernels, attend_back(): pl.pallas_call(functools.partial(attend_back_kernel, rows), name='attend_...  56.5 us
    pallas_call x1, Pallas kernels, mlp_back(): pl.pallas_call(mlp_back_kernel, name='mlp_back', grid_spec=pltpu.Prefetch...  49.3 us
    pallas_call x1, Pallas kernels, sum_head(): pl.pallas_call(functools.partial(sum_head_kernel, bits, rows, late_rows),...  43.7 us
    pallas_call x1, Pallas kernels, mlp(): pl.pallas_call(mlp_kernel, name='mlp', grid_spec=pltpu.PrefetchScalarGrid...  28.7 us
    pallas_call x1, Pallas kernels, attend(): pl.pallas_call(attend_kernel, name='attend', grid_spec=pltpu.PrefetchScal...  20 us
    pallas_call x1, Pallas kernels, project_back(): pl.pallas_call(project_back_kernel, name='project_back', grid_spec=pltpu....  18.7 us
    ppermute x5, starting transfers between devices, exchange(): lax.ppermute(values, axis, [(i, i ^ 1 << bit) for i in range(lax.axis_siz...  14.8 us
    all_to_all x2, waiting for transfers between devices, spread(): return lax.all_to_all(parts, 'dp', split_axis=0, concat_axis=0, tiled=True)  14.3 us
  transfers between devices with their start and end apart: 15, of which 5 were waited for; matrix products, arithmetic and copies ran while one was open for 7% of the time, Pallas kernels for 52%

profile of v1, /device:TPU:0, one launch (start us, length us, event | category | flops | bytes accessed | tf_op | source)
XLA Modules:
  0.0 376.6 jit_solution(14586398033945544778)
XLA Ops:
  0.6 4.0 %pad_bitcast_fusion.master = f32[6928,128]{1,0:T(8,128)} fusion(f32[886352]{0:T(1024)} %param.19), kind=kLoop, calls=%fused_computation.10 | loop fusion | bytes 7092544 | tf_op jit(solution)/shard_map/reshape | solution.py:755
  4.7 10.7 %pack_master.1 = (bf16[6944,128]{1,0:T(8,128)(2,1)}, bf16[4384,128]{1,0:T(8,128)(2,1)}, bf16[32,128]{1,0:T(8,128)(2,1)}) custom-call(f32[6928,128]{1,0:T(8,128)} %pad_bitcast_fusion.master), custom_call_target="tpu_custom_call" | custom-call | tf_op jit(solution)/shard_map/pack_master/pallas_call | solution.py:757
  15.5 11.6 %collective-permute-start = (bf16[6944,128]{1,0:T(8,128)(2,1)}, bf16[6944,128]{1,0:T(8,128)(2,1)}, u32[]{:S(2)}, u32[]{:S(2)}) collective-permute-start(bf16[6944,128]{1,0:T(8,128)(2,1)} %get-tuple-element.93.own), channel_id=1, source_target_pairs={{0,2},{1,3},{2,0},{3,1},{4,6},{5,7},{6,4},{7,5},{8,10},{9,11},{10,... | collective-permute-start | bytes 5333000 | tf_op jit(solution)/shard_map/ppermute | solution.py:1237
  29.8 5.0 %all-to-all-start = ((bf16[8,2,576,128]{3,2,1,0:T(8,128)(2,1)}), bf16[8,2,576,128]{3,2,1,0:T(8,128)(2,1)S(1)}, u32[]{:S(2)}, u32[]{:S(2)}) async-start(bf16[8,2,576,128]{3,2,1,0:T(8,128)(2,1)} %copy.55), calls=%async_computation | async-start | bytes 4718592 | tf_op jit(solution)/shard_map/all_to_all | solution.py:1222
  35.9 3.2 reshape.114
  45.7 12.0 %project.1 = (bf16[2,576,1024]{2,1,0:T(8,128)(2,1)}, bf16[2,3,1024,64]{3,2,1,0:T(8,128)(2,1)}, bf16[2,192,1024]{2,1,0:T(8,128)(2,1)}, bf16[2,3,1024,64]{3,2,1,0:...) custom-call(s32[2]{0:T(128)} %dynamic_slice.47.lens, ...), custom_call_target="tpu_custom_call" | custom-call | tf_op jit(solution)/shard_map/project/pallas_call | solution.py:139
  57.7 20.0 %attend.1 = (f32[2,576,1024]{2,1,0:T(8,128)}, f32[2,16,1024]{2,1,0:T(8,128)}) custom-call(s32[2]{0:T(128)} %dynamic_slice.47.lens, bf16[2,576,1024]{2,1,0:T(8,128)(2,1)} %get-tuple-element.96.q_t, bf16[2,3,1024,64]{3,2,1,0:T(8,128)(2,1)} %get-tuple-element.97.k_n, bf16[2,192,1024]{2,1,0:T(8,128)(2,1)} %get-tuple-element.98.v_t), custom_call_target="tpu_custom_call" | custom-call | tf_op jit(solution)/shard_map/attend/pallas_call | solution.py:212
  77.7 10.9 %all-to-all-done = bf16[8,2,576,128]{3,2,1,0:T(8,128)(2,1)S(1)} async-done(((bf16[8,2,576,128]{3,2,1,0:T(8,128)(2,1)}), bf16[8,2,576,128]{3,2,1,0:T(8,128)(2,1)S(1)}, u32[]{:S(2)}, u32[]{:S(2)}) %all-to-all-start) | async-done | bytes 2359328 | tf_op jit(solution)/shard_map/all_to_all | solution.py:1222
  90.9 4.1 %all-to-all-start.2 = ((bf16[8,2,576,128]{3,2,1,0:T(8,128)(2,1)}), bf16[8,2,576,128]{3,2,1,0:T(8,128)(2,1)S(1)}, u32[]{:S(2)}, u32[]{:S(2)}) async-start(bf16[8,2,576,128]{3,2,1,0:T(8,128)(2,1)} %bitcast.60), calls=%async_computation.2 | async-start | bytes 4718592 | tf_op jit(solution)/shard_map/all_to_all | solution.py:1228
  95.7 3.4 collective-permute-done.2.both
  99.1 11.2 %unpack_weights.1 = (bf16[576,576]{1,0:T(8,128)(2,1)}, bf16[576,3072]{1,0:T(8,128)(2,1)}, bf16[1536,576]{1,0:T(8,128)(2,1)}) custom-call(bf16[6944,128]{1,0:T(8,128)(2,1)} %get-tuple-element.93.own, bf16[6944,128]{1,0:T(8,128)(2,1)} %collective-permute-done.1.near, bf16[6944,128]{1,0:T(8,128)(2,1)} %collective-permute-done.far, ...), custom_call_target="tpu_custom_call" | custom-call | tf_op jit(solution)/shard_map/unpack_weights/pallas_call | solution.py:1198
  110.4 28.7 %mlp.1 = (bf16[8,2,576,128]{3,2,1,0:T(8,128)(2,1)}, f32[2,1024,576]{2,1,0:T(8,128)}, bf16[2,1024,1536]{2,1,0:T(8,128)(2,1)}, bf16[2,1024,1536]{2,1,0:T(8,128)(2,1)}, bf16[2,1024,1536]{2,1,0:T(8,128)(2,1)}) custom-call(s32[2]{0:T(128)} %dynamic_slice.47.lens, f32[2,576,1024]{2,1,0:T(8,128)} %get-tuple-element.100.att_t, ...), custom_call_target="tpu_custom_call" | custom-call | tf_op jit(solution)/shard_map/mlp/pallas_call | solution.py:324
  139.0 10.0 %all-to-all-done.2.cot_parts = bf16[8,2,576,128]{3,2,1,0:T(8,128)(2,1)S(1)} async-done(((bf16[8,2,576,128]{3,2,1,0:T(8,128)(2,1)}), bf16[8,2,576,128]{3,2,1,0:T(8,128)(2,1)S(1)}, u32[]{:S(2)}, u32[]{:S(2)}) %all-to-all-start.2) | async-done | bytes 2359328 | tf_op jit(solution)/shard_map/all_to_all | solution.py:1228
  150.4 4.4 %all-to-all-start.1 = ((bf16[8,2,576,128]{3,2,1,0:T(8,128)(2,1)}), bf16[8,2,576,128]{3,2,1,0:T(8,128)(2,1)}, u32[]{:S(2)}, u32[]{:S(2)}) async-start(bf16[8,2,576,128]{3,2,1,0:T(8,128)(2,1)} %get-tuple-element.107), calls=%async_computation.1 | async-start | bytes 4718592 | tf_op jit(solution)/shard_map/all_to_all | solution.py:1222
  155.5 49.3 %mlp_back.1 = (f32[2,576,1024]{2,1,0:T(8,128)}, bf16[2,576,1024]{2,1,0:T(8,128)(2,1)}, f32[2,32,1024]{2,1,0:T(8,128)}, bf16[23440,128]{1,0:T(8,128)(2,1)}, f32[8,576]{1,0:T(8,128)}) custom-call(s32[2]{0:T(128)} %dynamic_slice.47.lens, f32[2,576,1024]{2,1,0:T(8,128)} %get-tuple-element.100.att_t, f32[2,16,1024]{2,1,0:T(8,128)} %get-tuple-element.101.gate, ...), custom_call_target="tpu_custom_call" | custom-call | tf_op jit(solution)/shard_map/mlp_back/pallas_call | solution.py:442
  204.8 3.4 all-to-all-done.1
  208.2 3.9 %gather_fusion.1 = bf16[16,576,128]{2,1,0:T(8,128)(2,1)} fusion(bf16[16,576,128]{2,1,0:T(8,128)(2,1)} %bitcast.11, s32[1024]{0:T(1024)S(1)} %pad_clamp_fusion), kind=kCustom, calls=%fused_computation.1 | custom fusion | bytes 4718656 | tf_op jit(solution)/shard_map/jit(_take)/gather | solution.py:1227
  212.1 4.0 %all-to-all-start.3 = ((bf16[8,2,576,128]{3,2,1,0:T(8,128)(2,1)}), bf16[8,2,576,128]{3,2,1,0:T(8,128)(2,1)S(1)}, u32[]{:S(2)}, u32[]{:S(2)}) async-start(bf16[8,2,576,128]{3,2,1,0:T(8,128)(2,1)} %bitcast.58), calls=%async_computation.3 | async-start | bytes 4718592 | tf_op jit(solution)/shard_map/all_to_all | solution.py:1228
  217.6 56.5 %attend_back.1 = (f32[2,576,1024]{2,1,0:T(8,128)}, f32[2,192,1024]{2,1,0:T(8,128)}, f32[2,192,1024]{2,1,0:T(8,128)}, bf16[11,640,128]{2,1,0:T(8,128)(2,1)}) custom-call(bf16[2,576,1024]{2,1,0:T(8,128)(2,1)} %get-tuple-element.96.q_t, bf16[2,3,1024,64]{3,2,1,0:T(8,128)(2,1)} %get-tuple-element.97.k_n, bf16[2,192,1024]{2,1,0:T(8,128)(2,1)} %get-tuple-element.115.k_t, ...), custom_call_target="tpu_custom_call" | custom-call | tf_op jit(solution)/shard_map/attend_back/pallas_call | solution.py:952
  276.2 3.0 collective-permute-start.8
  285.3 18.7 %project_back.1 = (bf16[2,576,1024]{2,1,0:T(8,128)(2,1)}, f32[576,1024]{1,0:T(8,128)}, f32[1,576]{1,0:T(1,128)}, f32[2,64]{1,0:T(2,128)}) custom-call(s32[2]{0:T(128)} %dynamic_slice.47.lens, f32[2,576,1024]{2,1,0:T(8,128)} %get-tuple-element.123.dq_t, f32[2,192,1024]{2,1,0:T(8,128)} %get-tuple-element.124.dk_t, f32[2,192,1024]{2,1,0:T(8,128)} %get-tuple-element.125.dv_t, ...), custom_call_target="tpu_custom_call" | custom-call | tf_op jit(solution)/shard_map/project_back/pallas_call | solution.py:546
  306.0 4.4 %collective-permute-done.3 = bf16[6,160,128]{2,1,0:T(8,128)(2,1)S(1)} collective-permute-done((bf16[6,160,128]{2,1,0:T(8,128)(2,1)S(1)}, bf16[6,160,128]{2,1,0:T(8,128)(2,1)S(1)}, u32[]{:S(2)}, u32[]{:S(2)}) %collective-permute-start.3) | collective-permute-done | bytes 245792 | tf_op jit(solution)/shard_map/ppermute | solution.py:1249
  320.9 43.7 %sum_head.1 = (bf16[4608,128]{1,0:T(8,128)(2,1)S(1)}, bf16[11,640,128]{2,1,0:T(8,128)(2,1)S(1)}) custom-call(bf16[4608,128]{1,0:T(8,128)(2,1)} %pad_bitcast_fusion.1.source, bf16[16,128]{1,0:T(8,128)(2,1)} %pad.19.gain_rows, bf16[6,80,128]{2,1,0:T(8,128)(2,1)} %add_convert_fusion.2.share_one, bf16[5,80,128]{2,1,0:T(8,128)(2,1)} %add_convert_fusion.3.share_two), custom_call_target="tpu_custom_call" | custom-call | tf_op jit(solution)/shard_map/sum_head/pallas_call | solution.py:1088
  367.0 9.5 %rsqrt_multiply_fusion = (f32[886352]{0:T(1024)}, f32[886352]{0:T(1024)}, f32[886352]{0:T(1024)}, f32[886352]{0:T(1024)}) fusion(f32[886352]{0:T(1024)} %param.20, f32[886352]{0:T(1024)} %param.21, bf16[886352]{0:T(1024)(128)(2,1)} %get-tuple-element.169), kind=kLoop, calls=%fused_computation.8 | loop fusion | flops 9749872 | bytes 23045152 | tf_op jit(solution)/shard_map/div | solution.py:1324
  (87 shorter events, 41.7 us)
Async XLA Ops:
  4.7 22.4 %copy-start.1 = (bf16[2,1024,576]{1,2,0:T(8,128)(2,1)S(1)}, bf16[2,1024,576]{1,2,0:T(8,128)(2,1)}, u32[]{:S(2)}) copy-start(bf16[2,1024,576]{1,2,0:T(8,128)(2,1)} %param.16) | copy-start | bytes 7077892
  15.4 62.3 %collective-permute-start.1 = (bf16[6944,128]{1,0:T(8,128)(2,1)}, bf16[6944,128]{1,0:T(8,128)(2,1)}, u32[]{:S(2)}, u32[]{:S(2)}) collective-permute-start(bf16[6944,128]{1,0:T(8,128)(2,1)} %get-tuple-element.93.own), channel_id=1, source_target_pairs={{0,1},{1,0},{2,3},{3,2},{4,5},{5,4},{6,7},{7,6},{8,9},{9,8},{10,11... | collective-permute-start | bytes 5333000 | tf_op jit(solution)/shard_map/ppermute | solution.py:1237
  15.5 62.3 %collective-permute-start = (bf16[6944,128]{1,0:T(8,128)(2,1)}, bf16[6944,128]{1,0:T(8,128)(2,1)}, u32[]{:S(2)}, u32[]{:S(2)}) collective-permute-start(bf16[6944,128]{1,0:T(8,128)(2,1)} %get-tuple-element.93.own), channel_id=1, source_target_pairs={{0,2},{1,3},{2,0},{3,1},{4,6},{5,7},{6,4},{7,5},{8,10},{9,11},{10,... | collective-permute-start | bytes 5333000 | tf_op jit(solution)/shard_map/ppermute | solution.py:1237
  29.8 5.0 %copy-start.2 = (bf16[4384,128]{1,0:T(8,128)(2,1)S(1)}, bf16[4384,128]{1,0:T(8,128)(2,1)}, u32[]{:S(2)}) copy-start(bf16[4384,128]{1,0:T(8,128)(2,1)} %get-tuple-element.94) | copy-start | bytes 3366916
  29.8 58.9 %all-to-all-start = ((bf16[8,2,576,128]{3,2,1,0:T(8,128)(2,1)}), bf16[8,2,576,128]{3,2,1,0:T(8,128)(2,1)S(1)}, u32[]{:S(2)}, u32[]{:S(2)}) async-start(bf16[8,2,576,128]{3,2,1,0:T(8,128)(2,1)} %copy.55), calls=%async_computation | async-start | bytes 4718592 | tf_op jit(solution)/shard_map/all_to_all | solution.py:1222
  34.8 4.3 %copy-start.7 = (bf16[32,128]{1,0:T(8,128)(2,1)S(1)}, bf16[32,128]{1,0:T(8,128)(2,1)}, u32[]{:S(2)}) copy-start(bf16[32,128]{1,0:T(8,128)(2,1)} %get-tuple-element.95) | copy-start | bytes 24580
  90.9 58.1 %all-to-all-start.2 = ((bf16[8,2,576,128]{3,2,1,0:T(8,128)(2,1)}), bf16[8,2,576,128]{3,2,1,0:T(8,128)(2,1)S(1)}, u32[]{:S(2)}, u32[]{:S(2)}) async-start(bf16[8,2,576,128]{3,2,1,0:T(8,128)(2,1)} %bitcast.60), calls=%async_computation.2 | async-start | bytes 4718592 | tf_op jit(solution)/shard_map/all_to_all | solution.py:1228
  95.0 4.1 %collective-permute-start.2 = (bf16[6944,128]{1,0:T(8,128)(2,1)}, bf16[6944,128]{1,0:T(8,128)(2,1)}, u32[]{:S(2)}, u32[]{:S(2)}) collective-permute-start(bf16[6944,128]{1,0:T(8,128)(2,1)} %collective-permute-done.far), channel_id=1, source_target_pairs={{0,1},{1,0},{2,3},{3,2},{4,5},{5,4},{6,7},{7,6},{8,9},{9,8},{10,11... | collective-permute-start | bytes 5333000 | tf_op jit(solution)/shard_map/ppermute | solution.py:1237
  149.0 1.4 copy-start
  150.4 57.8 %all-to-all-start.1 = ((bf16[8,2,576,128]{3,2,1,0:T(8,128)(2,1)}), bf16[8,2,576,128]{3,2,1,0:T(8,128)(2,1)}, u32[]{:S(2)}, u32[]{:S(2)}) async-start(bf16[8,2,576,128]{3,2,1,0:T(8,128)(2,1)} %get-tuple-element.107), calls=%async_computation.1 | async-start | bytes 4718592 | tf_op jit(solution)/shard_map/all_to_all | solution.py:1222
  212.1 4.0 %copy-start.5 = (f32[2,16,1024]{2,1,0:T(8,128)S(1)}, f32[2,16,1024]{2,1,0:T(8,128)}, u32[]{:S(2)}) copy-start(f32[2,16,1024]{2,1,0:T(8,128)} %get-tuple-element.118) | copy-start | bytes 393220
  212.1 4.8 %copy-start.3 = (f32[2,32,1024]{2,1,0:T(8,128)S(1)}, f32[2,32,1024]{2,1,0:T(8,128)}, u32[]{:S(2)}) copy-start(f32[2,32,1024]{2,1,0:T(8,128)} %get-tuple-element.119.logit_delta) | copy-start | bytes 786436
  212.1 73.2 %all-to-all-start.3 = ((bf16[8,2,576,128]{3,2,1,0:T(8,128)(2,1)}), bf16[8,2,576,128]{3,2,1,0:T(8,128)(2,1)S(1)}, u32[]{:S(2)}, u32[]{:S(2)}) async-start(bf16[8,2,576,128]{3,2,1,0:T(8,128)(2,1)} %bitcast.58), calls=%async_computation.3 | async-start | bytes 4718592 | tf_op jit(solution)/shard_map/all_to_all | solution.py:1228
  276.2 27.9 %collective-permute-start.8 = (bf16[5,160,128]{2,1,0:T(8,128)(2,1)}, bf16[5,160,128]{2,1,0:T(8,128)(2,1)}, u32[]{:S(2)}, u32[]{:S(2)}) collective-permute-start(bf16[5,160,128]{2,1,0:T(8,128)(2,1)} %get-tuple-element.159), channel_id=1, source_target_pairs={{0,12},{4,8},{8,4},{12,0},{16,28},{20,24},{24,20},{28,16},{1,13},{... | collective-permute-start | bytes 614408 | tf_op jit(solution)/shard_map/ppermute | solution.py:1249
  280.4 25.6 %collective-permute-start.7 = (bf16[5,160,128]{2,1,0:T(8,128)(2,1)}, bf16[5,160,128]{2,1,0:T(8,128)(2,1)}, u32[]{:S(2)}, u32[]{:S(2)}) collective-permute-start(bf16[5,160,128]{2,1,0:T(8,128)(2,1)} %get-tuple-element.160), channel_id=1, source_target_pairs={{0,4},{4,0},{8,12},{12,8},{16,20},{20,16},{24,28},{28,24},{1,5},{5... | collective-permute-start | bytes 614408 | tf_op jit(solution)/shard_map/ppermute | solution.py:1249
  281.0 24.9 %collective-permute-start.6 = (bf16[5,160,128]{2,1,0:T(8,128)(2,1)}, bf16[5,160,128]{2,1,0:T(8,128)(2,1)}, u32[]{:S(2)}, u32[]{:S(2)}) collective-permute-start(bf16[5,160,128]{2,1,0:T(8,128)(2,1)} %get-tuple-element.161), channel_id=1, source_target_pairs={{0,8},{4,12},{8,0},{12,4},{16,24},{20,28},{24,16},{28,20},{1,9},{5... | collective-permute-start | bytes 614408 | tf_op jit(solution)/shard_map/ppermute | solution.py:1249
  281.9 24.0 %collective-permute-start.5 = (bf16[6,160,128]{2,1,0:T(8,128)(2,1)}, bf16[6,160,128]{2,1,0:T(8,128)(2,1)S(1)}, u32[]{:S(2)}, u32[]{:S(2)}) collective-permute-start(bf16[6,160,128]{2,1,0:T(8,128)(2,1)} %get-tuple-element.155), channel_id=1, source_target_pairs={{0,12},{4,8},{8,4},{12,0},{16,28},{20,24},{24,20},{28,16},{1,13},{... | collective-permute-start | bytes 737288 | tf_op jit(solution)/shard_map/ppermute | solution.py:1249
  284.8 21.2 %collective-permute-start.4 = (bf16[6,160,128]{2,1,0:T(8,128)(2,1)}, bf16[6,160,128]{2,1,0:T(8,128)(2,1)S(1)}, u32[]{:S(2)}, u32[]{:S(2)}) collective-permute-start(bf16[6,160,128]{2,1,0:T(8,128)(2,1)} %get-tuple-element.156), channel_id=1, source_target_pairs={{0,8},{4,12},{8,0},{12,4},{16,24},{20,28},{24,16},{28,20},{1,9},{5... | collective-permute-start | bytes 737288 | tf_op jit(solution)/shard_map/ppermute | solution.py:1249
  304.1 6.3 %collective-permute-start.3 = (bf16[6,160,128]{2,1,0:T(8,128)(2,1)S(1)}, bf16[6,160,128]{2,1,0:T(8,128)(2,1)S(1)}, u32[]{:S(2)}, u32[]{:S(2)}) collective-permute-start(bf16[6,160,128]{2,1,0:T(8,128)(2,1)S(1)} %get-tuple-element.157), channel_id=1, source_target_pairs={{0,4},{4,0},{8,12},{12,8},{16,20},{20,16},{24,28},{28,24},{1,5},{5... | collective-permute-start | bytes 737288 | tf_op jit(solution)/shard_map/ppermute | solution.py:1249
  305.9 8.9 %copy-start.4 = (f32[576,1024]{1,0:T(8,128)S(1)}, f32[576,1024]{1,0:T(8,128)}, u32[]{:S(2)}) copy-start(f32[576,1024]{1,0:T(8,128)} %get-tuple-element.139) | copy-start | bytes 7077892
  310.5 9.0 %collective-permute-start.9 = (bf16[6,80,128]{2,1,0:T(8,128)(2,1)S(1)}, bf16[6,80,128]{2,1,0:T(8,128)(2,1)S(1)}, u32[]{:S(2)}, u32[]{:S(2)}) collective-permute-start(bf16[6,80,128]{2,1,0:T(8,128)(2,1)S(1)} %get-tuple-element.163), channel_id=1, source_target_pairs={{0,16},{4,20},{8,24},{12,28},{16,0},{20,4},{24,8},{28,12},{1,17},{... | collective-permute-start | bytes 368648 | tf_op jit(solution)/shard_map/ppermute | solution.py:1237
  312.8 6.8 %collective-permute-start.10 = (bf16[5,80,128]{2,1,0:T(8,128)(2,1)S(1)}, bf16[5,80,128]{2,1,0:T(8,128)(2,1)S(1)}, u32[]{:S(2)}, u32[]{:S(2)}) collective-permute-start(bf16[5,80,128]{2,1,0:T(8,128)(2,1)S(1)} %get-tuple-element.165), channel_id=1, source_target_pairs={{0,16},{4,20},{8,24},{12,28},{16,0},{20,4},{24,8},{28,12},{1,17},{... | collective-permute-start | bytes 307208 | tf_op jit(solution)/shard_map/ppermute | solution.py:1237
  315.0 3.0 copy-start.8
  315.0 3.0 copy-start.6

commit v2 on v1

--- a/solution.py
+++ b/solution.py
@@ -357,8 +357,8 @@
 
 
 def mlp_back_kernel(lens, att_t, gate, cot_parts, hidden_in, act_low, gate_slope, up_slope, gains, w_out, w_mlp, w_down,
-                    grad_hidden_t, grad_att_t, logit_delta, late, g_gain,
-                    back, g_out, g_mlp, g_down_t, stage, pair_rows):
+                    grad_hidden_t, grad_att_t, logit_delta, kept, sent, g_gain,
+                    back, g_out, g_mlp, g_down_t, late, stage, pair_rows, copy_sem):
     lane, block = pl.program_id(0), pl.program_id(1)
 
     @pl.when((lane == 0) & (block == 0))
@@ -434,9 +434,19 @@
                 late[pl.ds(pl.multiple_of(start, 16), PAIR_ROWS), :] = stage[:PAIR_ROWS].astype(BF16)
 
         late[LATE_ROWS:] = jnp.zeros((late.shape[0] - LATE_ROWS, 128), BF16)
-
-
-def mlp_back(lens, att_t, gate, cot_parts, hidden_in, act_low, gate_slope, up_slope, gains, w_out, w_mlp, w_down, late_rows):
+        low = bit_of(lax.axis_index("zero"), 0)
+        copies = []
+        for h in range(2):
+            for side, target in enumerate((kept, sent)):
+                start = pl.multiple_of(window_start(2 * h + (low if side == 0 else 1 - low)), 16)
+                copies.append(pltpu.make_async_copy(late.at[pl.ds(start, kept.shape[1])], target.at[h], copy_sem.at[h, side]))
+        for copy in copies:
+            copy.start()
+        for copy in copies:
+            copy.wait()
+
+
+def mlp_back(lens, att_t, gate, cot_parts, hidden_in, act_low, gate_slope, up_slope, gains, w_out, w_mlp, w_down, window):
     dp_size, lanes, _, width = cot_parts.shape
     shape = jax.ShapeDtypeStruct
     return pl.pallas_call(
@@ -462,7 +472,8 @@
                 pl.BlockSpec((1, D, MLP_BLOCK), mlp_col_map),
                 pl.BlockSpec((1, WIDTH_Q, MLP_BLOCK), full_col_map),
                 pl.BlockSpec((1, 32, MLP_BLOCK), full_col_map),
-                whole((late_rows, 128)),
+                pl.BlockSpec(memory_space=pl.ANY),
+                pl.BlockSpec(memory_space=pl.ANY),
                 whole((8, D)),
             ],
             scratch_shapes=[
@@ -470,15 +481,18 @@
                 pltpu.VMEM((WIDTH_Q, D), F32),
                 pltpu.VMEM((D, 2 * FF), F32),
                 pltpu.VMEM((D, FF), F32),
+                pltpu.VMEM((LAST_WINDOW + window, 128), BF16),
                 pltpu.VMEM((WIDE_STEP * WIDE_TILES, 128), F32),
                 pltpu.VMEM((5, 2 * PAIR_STEP, 128), F32),
+                pltpu.SemaphoreType.DMA((2, 2)),
             ],
         ),
         out_shape=[
             shape((lanes, D, LANE), F32),
             shape((lanes, WIDTH_Q, LANE), BF16),
             shape((lanes, 32, LANE), F32),
-            shape((late_rows, 128), BF16),
+            shape((2, window, 128), BF16),
+            shape((2, window, 128), BF16),
             shape((8, D), F32),
         ],
         compiler_params=pltpu.CompilerParams(vmem_limit_bytes=VMEM_LIMIT),
@@ -581,6 +595,7 @@
             shape((1, D), F32),
             shape((2, HEAD_DIM), F32),
         ],
+        cost_estimate=pl.CostEstimate(flops=20_000_000_000, bytes_accessed=60_000_000, transcendentals=0),
         compiler_params=pltpu.CompilerParams(vmem_limit_bytes=VMEM_LIMIT),
     )(lens, dq_t, dk_t, dv_t, logit_delta, raw, tokens_t, grad_hidden_t, w_in, gain_cols, head_gains, cosine, sine)
 
@@ -811,54 +826,7 @@
     return pl.ds(pl.multiple_of(offset, 16), size)
 
 
-def zero_sum(rows, late, window, own, first, second, local_sem, send_sem, recv_sem):
-    dp, zero = lax.axis_index("dp"), lax.axis_index("zero")
-    core, across = (dp, flip(zero, 0)), (dp, flip(zero, 1))
-    low, high = bit_of(zero, 0), bit_of(zero, 1)
-    parts = range(REDUCE_PARTS)
-
-    def local(h, part):
-        source = late.at[aligned(window_start(2 * h + low) + part * rows, rows)]
-        return pltpu.make_async_copy(source, own.at[part, h], local_sem.at[h, part])
-
-    def flight(step, part):
-        if step < 2:
-            source = late.at[aligned(window_start(2 * step + 1 - low) + part * rows, rows)]
-            target, device = first.at[part, step], core
-        else:
-            source, target, device = own.at[part, 1 - high], second.at[part], across
-        return pltpu.make_async_remote_copy(source, target, send_sem.at[step, part], recv_sem.at[step, part],
-                                            device_id=device, device_id_type=MESH)
-
-    def begin():
-        greet([core, across])
-        for part in parts:
-            for h in range(2):
-                flight(h, part).start()
-                local(h, part).start()
-
-    def receive(step, part):
-        if step == 1:
-            for h in range(2):
-                local(h, part).wait()
-                flight(h, part).wait_recv()
-            for h in range(2):
-                own[part, h] = (own[part, h].astype(F32) + first[part, h].astype(F32)).astype(BF16)
-            flight(2, part).start()
-        else:
-            flight(2, part).wait_recv()
-            window[part] = (own[part, high].astype(F32) + second[part].astype(F32)).astype(BF16)
-
-    def finish():
-        for part in parts:
-            for step in range(3):
-                flight(step, part).wait_send()
-
-    return begin, receive, finish
-
-
 LATE_HOP = 12.0
-HOP = 1.5
 
 
 def arrival_order(chains, hops):
@@ -877,114 +845,71 @@
     return sorted(order)
 
 
-SLOTS = (((0, 0), 0.13), ((0, 2), 0.4), ((1, 2), 0.7), ((3, 2), 1.0))
-
-
-def receive_slots(step_us):
-    chains = [[("core", 0.8), ("x", 40.0 / REDUCE_PARTS)]] * REDUCE_PARTS
-    ends = [(step + done) * step_us for step in range(LANE_STEPS) for _, done in SLOTS]
-    table = [[] for _ in ends]
-    place = 0
-    for at, part, step in arrival_order(chains, [HOP] * len(chains)):
-        while place + 1 < len(ends) and ends[place] < at:
-            place += 1
-        table[place].append((step + 1, part))
-    return table
-
-
-def attend_back_kernel(rows, q_t, k_n, k_t, v_n, grad_t, log_total, delta, late, dq_t, dk_t, dv_t, window,
-                       own, first, second, local_sem, send_sem, recv_sem):
-    begin, receive, finish = zero_sum(rows, late, window, own, first, second, local_sem, send_sem, recv_sem)
-    step = pl.program_id(0) * KV_HEADS + pl.program_id(1)
-    table = receive_slots(8.6)
-    pl.when(step == 0)(begin)
+def attend_back_kernel(lens, q_t, k_n, k_t, v_n, grad_t, log_total, delta, dq_t, dk_t, dv_t):
+    lane = pl.program_id(0)
     dq_t[...] = jnp.zeros_like(dq_t)
-
-    def advance(slot):
-        for place in range(slot, len(table), len(SLOTS)):
-            if table[place]:
-
-                @pl.when(step == place // len(SLOTS))
-                def _():
-                    for receipt in table[place]:
-                        receive(*receipt)
-
     for block in range(BLOCKS):
         keys = pl.ds(block * BLOCK, BLOCK)
-        k_rows, v_rows, k_cols = k_n[0, 0, keys, :], v_n[0, 0, keys, :], k_t[0, :, keys]
-        dk = jnp.zeros((HEAD_DIM, BLOCK), F32)
-        dv = jnp.zeros((HEAD_DIM, BLOCK), F32)
-        for r in range(GROUP):
-            head = slice(r * HEAD_DIM, (r + 1) * HEAD_DIM)
-            for part in range(block, BLOCKS):
-                cols = pl.ds(part * BLOCK, BLOCK)
+
+        @pl.when(block * BLOCK >= lens[lane])
+        def _():
+            dk_t[0, :, keys] = jnp.zeros((HEAD_DIM, BLOCK), F32)
+            dv_t[0, :, keys] = jnp.zeros((HEAD_DIM, BLOCK), F32)
+
+        @pl.when(block * BLOCK < lens[lane])
+        def _():
+            k_rows, v_rows, k_cols = k_n[0, 0, keys, :], v_n[0, 0, keys, :], k_t[0, :, keys]
+            dk = jnp.zeros((HEAD_DIM, BLOCK), F32)
+            dv = jnp.zeros((HEAD_DIM, BLOCK), F32)
+            cols = pl.ds(block * BLOCK, LANE - block * BLOCK)
+            for r in range(GROUP):
+                head = slice(r * HEAD_DIM, (r + 1) * HEAD_DIM)
                 query, grad = q_t[0, head, cols], grad_t[0, head, cols]
-                logs = log_total[0, 0, r : r + 1, cols]
-                prob = jnp.exp2(dot(k_rows, query, 1, 0) * EXP_SCALE - logs)
-                if part == block:
-                    prob = causal_tile(prob, 0.0)
+                prob = jnp.exp2(dot(k_rows, query, 1, 0) * EXP_SCALE - log_total[0, 0, r : r + 1, cols])
+                prob = causal_tile(prob, 0.0)
                 grad_prob = dot(v_rows, grad, 1, 0) - delta[0, 0, r : r + 1, cols]
                 grad_score = (prob * grad_prob).astype(BF16)
                 dv += dot(grad, prob.astype(BF16), 1, 1)
                 dk += dot(query, grad_score, 1, 1)
                 dq_t[0, head, cols] += dot(k_cols, grad_score, 1, 0) * SCALE
-            for slot, (after, _) in enumerate(SLOTS):
-                if after == (block, r) and r + 1 < GROUP:
-                    advance(slot)
-        dk_t[0, :, keys] = dk * SCALE
-        dv_t[0, :, keys] = dv
-        for slot, (after, _) in enumerate(SLOTS):
-            if after == (block, GROUP - 1):
-                advance(slot)
-    pl.when(step == LANE_STEPS - 1)(finish)
-
-
-LANE_STEPS = 2 * KV_HEADS
-
-
-def attend_back(q_t, k_n, k_t, v_n, grad_t, log_total, delta, late, dp_size):
+            dk_t[0, :, keys] = dk * SCALE
+            dv_t[0, :, keys] = dv
+
+
+def attend_back(lens, q_t, k_n, k_t, v_n, grad_t, log_total, delta):
     lanes = q_t.shape[0]
-    rows = window_rows(dp_size) // REDUCE_PARTS
     shape = jax.ShapeDtypeStruct
-    group_rows = lambda lane, g: (lane, g, 0)
-    group_heads = lambda lane, g: (lane, g, 0, 0)
-    held = lambda *dims: pltpu.VMEM((REDUCE_PARTS, *dims, LANES128), BF16)
+    group_rows = lambda lane, g, lens: (lane, g, 0)
+    group_heads = lambda lane, g, lens: (lane, g, 0, 0)
     return pl.pallas_call(
-        functools.partial(attend_back_kernel, rows),
+        attend_back_kernel,
         name="attend_back",
-        grid=(lanes, KV_HEADS),
-        in_specs=[
-            pl.BlockSpec((1, GROUP * HEAD_DIM, LANE), group_rows),
-            pl.BlockSpec((1, 1, LANE, HEAD_DIM), group_heads),
-            pl.BlockSpec((1, HEAD_DIM, LANE), group_rows),
-            pl.BlockSpec((1, 1, LANE, HEAD_DIM), group_heads),
-            pl.BlockSpec((1, GROUP * HEAD_DIM, LANE), group_rows),
-            pl.BlockSpec((1, 1, GROUP, LANE), group_heads),
-            pl.BlockSpec((1, 1, GROUP, LANE), group_heads),
-            pl.BlockSpec(memory_space=pl.ANY),
-        ],
-        out_specs=[
-            pl.BlockSpec((1, GROUP * HEAD_DIM, LANE), group_rows),
-            pl.BlockSpec((1, HEAD_DIM, LANE), group_rows),
-            pl.BlockSpec((1, HEAD_DIM, LANE), group_rows),
-            whole((REDUCE_PARTS, rows, LANES128)),
-        ],
+        grid_spec=pltpu.PrefetchScalarGridSpec(
+            num_scalar_prefetch=1,
+            grid=(lanes, KV_HEADS),
+            in_specs=[
+                pl.BlockSpec((1, GROUP * HEAD_DIM, LANE), group_rows),
+                pl.BlockSpec((1, 1, LANE, HEAD_DIM), group_heads),
+                pl.BlockSpec((1, HEAD_DIM, LANE), group_rows),
+                pl.BlockSpec((1, 1, LANE, HEAD_DIM), group_heads),
+                pl.BlockSpec((1, GROUP * HEAD_DIM, LANE), group_rows),
+                pl.BlockSpec((1, 1, GROUP, LANE), group_heads),
+                pl.BlockSpec((1, 1, GROUP, LANE), group_heads),
+            ],
+            out_specs=[
+                pl.BlockSpec((1, GROUP * HEAD_DIM, LANE), group_rows),
+                pl.BlockSpec((1, HEAD_DIM, LANE), group_rows),
+                pl.BlockSpec((1, HEAD_DIM, LANE), group_rows),
+            ],
+        ),
         out_shape=[
             shape((lanes, WIDTH_Q, LANE), F32),
             shape((lanes, WIDTH_K, LANE), F32),
             shape((lanes, WIDTH_K, LANE), F32),
-            shape((REDUCE_PARTS, rows, LANES128), BF16),
         ],
-        scratch_shapes=[
-            held(2, rows),
-            held(2, rows),
-            held(rows),
-            pltpu.SemaphoreType.DMA((2, REDUCE_PARTS)),
-            pltpu.SemaphoreType.DMA((3, REDUCE_PARTS)),
-            pltpu.SemaphoreType.DMA((3, REDUCE_PARTS)),
-        ],
-        compiler_params=pltpu.CompilerParams(collective_id=1, has_side_effects=True, vmem_limit_bytes=VMEM_LIMIT),
-    )(q_t, k_n, k_t, v_n, grad_t, log_total, delta, late)
+        cost_estimate=pl.CostEstimate(flops=40_000_000_000, bytes_accessed=40_000_000, transcendentals=0),
+        compiler_params=pltpu.CompilerParams(vmem_limit_bytes=VMEM_LIMIT),
+    )(lens, q_t, k_n, k_t, v_n, grad_t, log_total, delta)
 
 
 TAIL_AT = 4368
@@ -1000,7 +925,7 @@
     return -(-(TAIL_AT + 16) // unit) * unit
 
 
-def sum_head_kernel(bits, rows, late_rows, source, gain_rows, share_one, share_two, result, late_sum, total, *rest):
+def sum_head_kernel(bits, rows, late_rows, source, gain_rows, late_share, result, late_sum, total, *rest):
     received, (load_sem, send_sem, recv_sem, late_send, late_recv) = rest[:-5], rest[-5:]
     dp, zero = lax.axis_index("dp"), lax.axis_index("zero")
     axes = [("zero", 1)] + [("dp", k) for k in range(bits)]
@@ -1057,8 +982,7 @@
     def late_chain(index):
         kind, start, count = LATE_GROUPS[index]
         parts = pl.ds(CLASSES[kind][0] + start, count)
-        share = (share_one, share_two)[kind]
-        late_sum[parts, aligned(*part_region(dp, late_rows, bits, kind, bits))] = share[start : start + count]
+        late_sum[parts, aligned(*part_region(dp, late_rows, bits, kind, bits))] = late_share[parts]
         for slot, k in reversed(list(enumerate(bit_order(bits, kind)))):
             place = late_sum.at[parts, aligned(*part_region(dp, late_rows, bits, kind, slot + 1))]
             copy = pltpu.make_async_remote_copy(place, place, late_send.at[index, slot], late_recv.at[index, slot],
@@ -1080,7 +1004,7 @@
         copy.wait_send()
 
 
-def sum_head(source, gain_rows, shares, late_rows, dp_size):
+def sum_head(source, gain_rows, share, late_rows, dp_size):
     bits = dp_size.bit_length() - 1
     rows = source.shape[0]
     steps = bits + 2
@@ -1089,7 +1013,7 @@
         functools.partial(sum_head_kernel, bits, rows, late_rows),
         name="sum_head",
         out_shape=[shape((rows, LANES128), BF16), shape((REDUCE_PARTS, late_rows, LANES128), BF16)],
-        in_specs=[pl.BlockSpec(memory_space=pl.ANY)] + [pl.BlockSpec(memory_space=pltpu.VMEM)] * 3,
+        in_specs=[pl.BlockSpec(memory_space=pl.ANY)] + [pl.BlockSpec(memory_space=pltpu.VMEM)] * 2,
         out_specs=[pl.BlockSpec(memory_space=pltpu.VMEM)] * 2,
         scratch_shapes=[
             pltpu.VMEM((rows, LANES128), BF16),
@@ -1101,7 +1025,7 @@
             pltpu.SemaphoreType.DMA((len(LATE_GROUPS), bits)),
         ],
         compiler_params=pltpu.CompilerParams(collective_id=2, has_side_effects=True, vmem_limit_bytes=VMEM_LIMIT),
-    )(source, gain_rows, *shares)
+    )(source, gain_rows, share)
 
 
 def flat_rows(g_in, rows):
@@ -1237,18 +1161,22 @@
     return lax.ppermute(values, axis, [(i, i ^ (1 << bit)) for i in range(lax.axis_size(axis))])
 
 
-def quarter(parts, dp_rank, order):
-    size = parts.shape[1] // 4
-
-    def rows_of(flips):
-        first, second = (bit_of(dp_rank, bit) ^ flip for bit, flip in zip(order, flips))
-        return lax.dynamic_slice_in_dim(parts, first * (2 * size) + second * size, size, 1)
-
-    def sent(flips):
-        mask = sum(flip << bit for bit, flip in zip(order, flips))
-        return lax.ppermute(rows_of(flips), "dp", [(i, i ^ mask) for i in range(lax.axis_size("dp"))])
-
-    return [rows_of((0, 0)), sent((1, 0)), sent((0, 1)), sent((1, 1))]
+def quarters(window, dp_rank):
+    size = window.shape[1] // 4
+
+    def rows_for(mask, kind):
+        at, count = CLASSES[kind]
+        first, second = (bit_of(dp_rank, bit) ^ (mask >> bit & 1) for bit in bit_order(2, kind))
+        return lax.dynamic_slice_in_dim(window[at : at + count], first * (2 * size) + second * size, size, 1)
+
+    return [jnp.concatenate([rows_for(mask, kind) for kind in range(2)]) for mask in range(4)]
+
+
+def exchange_quarters(rows):
+    def sent(values, mask):
+        return lax.ppermute(values, "dp", [(i, i ^ mask) for i in range(lax.axis_size("dp"))])
+
+    return [rows[0]] + [sent(rows[mask], mask) for mask in range(1, 4)]
 
 
 def halve(parts, dp_rank, bit):
@@ -1290,30 +1218,37 @@
     gain_cols, head_gains = gains[:, :, None], head_gains[:, :, None]
     out_columns, *stash = mlp(lens, att_t, gate, tokens_t, gains, w_out, w_mlp, w_down, dp_size)
     output_parts = spread(out_columns)
-    grad_hidden_t, grad_att_t, logit_delta, late, g_gain_two = mlp_back(
-        lens, att_t, gate, cot_here, *stash, gains, w_out, w_mlp, w_down, LAST_WINDOW + window_rows(dp_size))
+    grad_hidden_t, grad_att_t, logit_delta, late_kept, late_sent, g_gain_two = mlp_back(
+        lens, att_t, gate, cot_here, *stash, gains, w_out, w_mlp, w_down, window_rows(dp_size))
+    late_in = exchange(late_sent, "zero", 0)
     output_parts, grad_att_t = lax.optimization_barrier((output_parts, grad_att_t))
     output_parts = regroup(output_parts, order)
     q_t, k_n, k_t, v_n, log_total, raw = kept
-    dq_t, dk_t, dv_t, window = attend_back(
-        q_t, k_n, k_t, v_n, grad_att_t, head_groups(log_total), head_groups(logit_delta[:, 16:]), late, dp_size)
-    output_parts, dq_t = lax.optimization_barrier((output_parts, dq_t))
+    high = bit_of(zero_rank, 1)
+    side = lambda windows, h: lax.dynamic_index_in_dim(windows, h, 0, keepdims=False)
+    crossing = added([side(late_kept, 1 - high), side(late_in, 1 - high)])
+    crossing, grad_att_t = lax.optimization_barrier((crossing, grad_att_t))
+    crossed = exchange(crossing, "zero", 1)
+    dq_t, dk_t, dv_t = attend_back(
+        lens, q_t, k_n, k_t, v_n, grad_att_t, head_groups(log_total), head_groups(logit_delta[:, 16:]))
+    dq_t, crossed = lax.optimization_barrier((dq_t, crossed))
+    window = added([side(late_kept, high), side(late_in, high), crossed]).reshape(REDUCE_PARTS, -1, LANES128)
     dp_bits = dp_size.bit_length() - 1
-    orders = [bit_order(dp_bits, kind) for kind in range(2)]
-    pieces = [quarter(window[at : at + count], dp_rank, orders[kind][:2]) for kind, (at, count) in enumerate(CLASSES)]
+    rows, dq_t = lax.optimization_barrier((quarters(window, dp_rank), dq_t))
+    pieces = exchange_quarters(rows)
     cosine, sine = (jnp.asarray(t) for t in rope_tables())
     grad_tokens_t, g_in, g_gain_one, g_head = project_back(
         lens, dq_t, dk_t, dv_t, logit_delta, raw, tokens_t, grad_hidden_t, w_in, gain_cols, head_gains, cosine, sine)
-    pieces, g_in = lax.optimization_barrier((pieces, g_in))
-    shares = [added(piece) for piece in pieces]
+    pieces, g_in, output_parts = lax.optimization_barrier((pieces, g_in, output_parts))
+    share = added(pieces)
     head = flat_rows(g_in, head_rows(dp_size))
     gain_rows = pack_gains(g_gain_one, g_gain_two, g_head)
     for step in range(2, dp_bits):
-        pieces = [halve(share, dp_rank, order[step]) for share, order in zip(shares, orders)]
+        pieces = halve(share, dp_rank, step)
         pieces, head, gain_rows = lax.optimization_barrier((pieces, head, gain_rows))
-        shares = [added(piece) for piece in pieces]
+        share = added(pieces)
     grad_tokens = grad_tokens_t.swapaxes(1, 2)
-    head_sum, late_sum = sum_head(head, gain_rows, shares, window.shape[1], dp_size)
+    head_sum, late_sum = sum_head(head, gain_rows, share, window.shape[1], dp_size)
     output = joined(output_parts).swapaxes(1, 2)
     grad_shard = unpack_shard(late_sum, head_sum, zero_rank)
     gain_width = D // zero_size

time: 383 us -> 373 us (0.974)
  Pallas kernels: 251 us -> 184 us
  waiting for transfers between devices: 32 us -> 69.3 us
  other arithmetic: 15.8 us -> 25.7 us
  starting transfers between devices: 39.3 us -> 48.6 us
    pallas_call x1, Pallas kernels: 56.5 us -> 22 us  [attend_back(): pl.pallas_call(attend_back_kernel, name='attend_back', grid_spec=pltpu.Pr...]
    ppermute x5 -> x6, waiting for transfers between devices: 3.38 us -> 27.5 us  [exchange(): lax.ppermute(values, axis, [(i, i ^ 1 << bit) for i in range(lax.axis_siz...]
    pallas_call x1, Pallas kernels: 49.3 us -> 38.1 us  [mlp_back(): pl.pallas_call(mlp_back_kernel, name='mlp_back', grid_spec=pltpu.Prefetch...]
    ppermute x5 -> x6, starting transfers between devices: 14.8 us -> 24.4 us  [exchange(): lax.ppermute(values, axis, [(i, i ^ 1 << bit) for i in range(lax.axis_siz...]
    pallas_call x1, Pallas kernels: 28.7 us -> 20.4 us  [mlp(): pl.pallas_call(mlp_kernel, name='mlp', grid_spec=pltpu.PrefetchScalarGrid...]
    all_to_all x2, waiting for transfers between devices: 9.96 us -> 18.2 us  [regroup(): lax.all_to_all(parts.reshape(dp_size, seqs, width, columns), 'dp', split_...]
    pallas_call x1, Pallas kernels: 20 us -> 12.1 us  [attend(): pl.pallas_call(attend_kernel, name='attend', grid_spec=pltpu.PrefetchScal...]
    convert_element_type x4, other arithmetic: 2.74 us -> 10.4 us  [added(): return sum((piece.astype(F32) for piece in pieces)).astype(BF16)]
  transfers between devices with their start and end apart: 15 -> 13, of which waited for: 5 -> 6; matrix products, arithmetic and copies ran while one was open for 7% -> 11% of each run, Pallas kernels for 52% -> 35%
where the time goes in v2:
time: 373 us; the launch traced here: 367 us
  Pallas kernels  184 us (49%)
  waiting for transfers between devices  69.3 us (19%)
  starting transfers between devices  48.6 us (13%)
  local copies, waits for them, and re-layouts  38.2 us (10%)
  other arithmetic  25.7 us (7%)
    pallas_call x1, Pallas kernels, sum_head(): pl.pallas_call(functools.partial(sum_head_kernel, bits, rows, late_rows),...  43.5 us
    pallas_call x1, Pallas kernels, mlp_back(): pl.pallas_call(mlp_back_kernel, name='mlp_back', grid_spec=pltpu.Prefetch...  38.1 us
    ppermute x6, waiting for transfers between devices, exchange(): lax.ppermute(values, axis, [(i, i ^ 1 << bit) for i in range(lax.axis_siz...  27.5 us
    ppermute x6, starting transfers between devices, exchange(): lax.ppermute(values, axis, [(i, i ^ 1 << bit) for i in range(lax.axis_siz...  24.4 us
    pallas_call x1, Pallas kernels, attend_back(): pl.pallas_call(attend_back_kernel, name='attend_back', grid_spec=pltpu.Pr...  22 us
    all_to_all x2, waiting for transfers between devices, spread(): return lax.all_to_all(parts, 'dp', split_axis=0, concat_axis=0, tiled=True)  20.5 us
    pallas_call x1, Pallas kernels, mlp(): pl.pallas_call(mlp_kernel, name='mlp', grid_spec=pltpu.PrefetchScalarGrid...  20.4 us
    all_to_all x2, waiting for transfers between devices, regroup(): lax.all_to_all(parts.reshape(dp_size, seqs, width, columns), 'dp', split_...  18.2 us
  transfers between devices with their start and end apart: 13, of which 6 were waited for; matrix products, arithmetic and copies ran while one was open for 11% of the time, Pallas kernels for 35%

profile of v2, /device:TPU:0, one launch (start us, length us, event | category | flops | bytes accessed | tf_op | source)
XLA Modules:
  0.0 366.6 jit_solution(6912456147337650183)
XLA Ops:
  0.6 4.0 %pad_bitcast_fusion.master = f32[6928,128]{1,0:T(8,128)} fusion(f32[886352]{0:T(1024)} %param.19), kind=kLoop, calls=%fused_computation.13 | loop fusion | bytes 7092544 | tf_op jit(solution)/shard_map/reshape | solution.py:770
  4.7 10.7 %pack_master.1 = (bf16[6944,128]{1,0:T(8,128)(2,1)}, bf16[4384,128]{1,0:T(8,128)(2,1)}, bf16[32,128]{1,0:T(8,128)(2,1)}) custom-call(f32[6928,128]{1,0:T(8,128)} %pad_bitcast_fusion.master), custom_call_target="tpu_custom_call" | custom-call | tf_op jit(solution)/shard_map/pack_master/pallas_call | solution.py:772
  15.5 11.6 %collective-permute-start = (bf16[6944,128]{1,0:T(8,128)(2,1)}, bf16[6944,128]{1,0:T(8,128)(2,1)}, u32[]{:S(2)}, u32[]{:S(2)}) collective-permute-start(bf16[6944,128]{1,0:T(8,128)(2,1)} %get-tuple-element.95.own), channel_id=1, source_target_pairs={{0,2},{1,3},{2,0},{3,1},{4,6},{5,7},{6,4},{7,5},{8,10},{9,11},{10,... | collective-permute-start | bytes 5333000 | tf_op jit(solution)/shard_map/ppermute | solution.py:1161
  29.8 5.0 %all-to-all-start = ((bf16[8,2,576,128]{3,2,1,0:T(8,128)(2,1)}), bf16[8,2,576,128]{3,2,1,0:T(8,128)(2,1)S(1)}, u32[]{:S(2)}, u32[]{:S(2)}) async-start(bf16[8,2,576,128]{3,2,1,0:T(8,128)(2,1)} %copy.55), calls=%async_computation | async-start | bytes 4718592 | tf_op jit(solution)/shard_map/all_to_all | solution.py:1146
  45.7 10.3 %project.1 = (bf16[2,576,1024]{2,1,0:T(8,128)(2,1)}, bf16[2,3,1024,64]{3,2,1,0:T(8,128)(2,1)}, bf16[2,192,1024]{2,1,0:T(8,128)(2,1)}, bf16[2,3,1024,64]{3,2,1,0:...) custom-call(s32[2]{0:T(128)} %dynamic_slice.54.lens, ...), custom_call_target="tpu_custom_call" | custom-call | tf_op jit(solution)/shard_map/project/pallas_call | solution.py:139
  56.0 12.1 %attend.1 = (f32[2,576,1024]{2,1,0:T(8,128)}, f32[2,16,1024]{2,1,0:T(8,128)}) custom-call(s32[2]{0:T(128)} %dynamic_slice.54.lens, bf16[2,576,1024]{2,1,0:T(8,128)(2,1)} %get-tuple-element.98.q_t, bf16[2,3,1024,64]{3,2,1,0:T(8,128)(2,1)} %get-tuple-element.99.k_n, bf16[2,192,1024]{2,1,0:T(8,128)(2,1)} %get-tuple-element.100.v_t), custom_call_target="tpu_custom_call" | custom-call | tf_op jit(solution)/shard_map/attend/pallas_call | solution.py:212
  68.1 20.5 %all-to-all-done = bf16[8,2,576,128]{3,2,1,0:T(8,128)(2,1)S(1)} async-done(((bf16[8,2,576,128]{3,2,1,0:T(8,128)(2,1)}), bf16[8,2,576,128]{3,2,1,0:T(8,128)(2,1)S(1)}, u32[]{:S(2)}, u32[]{:S(2)}) %all-to-all-start) | async-done | bytes 2359328 | tf_op jit(solution)/shard_map/all_to_all | solution.py:1146
  90.9 4.1 %all-to-all-start.1 = ((bf16[8,2,576,128]{3,2,1,0:T(8,128)(2,1)}), bf16[8,2,576,128]{3,2,1,0:T(8,128)(2,1)S(1)}, u32[]{:S(2)}, u32[]{:S(2)}) async-start(bf16[8,2,576,128]{3,2,1,0:T(8,128)(2,1)} %bitcast.68), calls=%async_computation.1 | async-start | bytes 4718592 | tf_op jit(solution)/shard_map/all_to_all | solution.py:1152
  95.7 3.4 collective-permute-done.2.both
  99.1 11.2 %unpack_weights.1 = (bf16[576,576]{1,0:T(8,128)(2,1)}, bf16[576,3072]{1,0:T(8,128)(2,1)}, bf16[1536,576]{1,0:T(8,128)(2,1)}) custom-call(bf16[6944,128]{1,0:T(8,128)(2,1)} %get-tuple-element.95.own, bf16[6944,128]{1,0:T(8,128)(2,1)} %collective-permute-done.1.near, bf16[6944,128]{1,0:T(8,128)(2,1)} %collective-permute-done.far, ...), custom_call_target="tpu_custom_call" | custom-call | tf_op jit(solution)/shard_map/unpack_weights/pallas_call | solution.py:1122
  110.4 20.4 %mlp.1 = (bf16[8,2,576,128]{3,2,1,0:T(8,128)(2,1)}, f32[2,1024,576]{2,1,0:T(8,128)}, bf16[2,1024,1536]{2,1,0:T(8,128)(2,1)}, bf16[2,1024,1536]{2,1,0:T(8,128)(2,1)}, bf16[2,1024,1536]{2,1,0:T(8,128)(2,1)}) custom-call(s32[2]{0:T(128)} %dynamic_slice.54.lens, f32[2,576,1024]{2,1,0:T(8,128)} %get-tuple-element.102.att_t, ...), custom_call_target="tpu_custom_call" | custom-call | tf_op jit(solution)/shard_map/mlp/pallas_call | solution.py:324
  130.7 18.2 %all-to-all-done.1.cot_parts = bf16[8,2,576,128]{3,2,1,0:T(8,128)(2,1)S(1)} async-done(((bf16[8,2,576,128]{3,2,1,0:T(8,128)(2,1)}), bf16[8,2,576,128]{3,2,1,0:T(8,128)(2,1)S(1)}, u32[]{:S(2)}, u32[]{:S(2)}) %all-to-all-start.1) | async-done | bytes 2359328 | tf_op jit(solution)/shard_map/all_to_all | solution.py:1152
  150.4 4.4 %all-to-all-start.2 = ((bf16[8,2,576,128]{3,2,1,0:T(8,128)(2,1)}), bf16[8,2,576,128]{3,2,1,0:T(8,128)(2,1)}, u32[]{:S(2)}, u32[]{:S(2)}) async-start(bf16[8,2,576,128]{3,2,1,0:T(8,128)(2,1)} %get-tuple-element.118), calls=%async_computation.2 | async-start | bytes 4718592 | tf_op jit(solution)/shard_map/all_to_all | solution.py:1146
  154.8 38.1 %mlp_back.1 = (f32[2,576,1024]{2,1,0:T(8,128)}, bf16[2,576,1024]{2,1,0:T(8,128)(2,1)}, f32[2,32,1024]{2,1,0:T(8,128)}, bf16[2,7040,128]{2,1,0:T(8,128)(2,1)}, bf...) custom-call(s32[2]{0:T(128)} %dynamic_slice.54.lens, f32[2,576,1024]{2,1,0:T(8,128)} %get-tuple-element.102.att_t, ...), custom_call_target="tpu_custom_call" | custom-call | tf_op jit(solution)/shard_map/mlp_back/pallas_call | solution.py:452
  192.9 11.5 %collective-permute-start.3 = (bf16[2,7040,128]{2,1,0:T(8,128)(2,1)}, bf16[2,7040,128]{2,1,0:T(8,128)(2,1)}, u32[]{:S(2)}, u32[]{:S(2)}) collective-permute-start(bf16[2,7040,128]{2,1,0:T(8,128)(2,1)} %get-tuple-element.115), channel_id=1, source_target_pairs={{0,1},{1,0},{2,3},{3,2},{4,5},{5,4},{6,7},{7,6},{8,9},{9,8},{10,11... | collective-permute-start | bytes 10813448 | tf_op jit(solution)/shard_map/ppermute | solution.py:1161
  208.2 3.9 %gather_fusion.1 = bf16[16,576,128]{2,1,0:T(8,128)(2,1)} fusion(bf16[16,576,128]{2,1,0:T(8,128)(2,1)} %bitcast.17, s32[1024]{0:T(1024)S(1)} %pad_clamp_fusion), kind=kCustom, calls=%fused_computation.1 | custom fusion | bytes 4718656 | tf_op jit(solution)/shard_map/jit(_take)/gather | solution.py:1151
  212.1 7.3 %all-to-all-start.3 = ((bf16[8,2,576,128]{3,2,1,0:T(8,128)(2,1)}), bf16[8,2,576,128]{3,2,1,0:T(8,128)(2,1)S(1)}, u32[]{:S(2)}, u32[]{:S(2)}) async-start(bf16[8,2,576,128]{3,2,1,0:T(8,128)(2,1)} %bitcast.66), calls=%async_computation.3 | async-start | bytes 4718592 | tf_op jit(solution)/shard_map/all_to_all | solution.py:1152
  219.4 3.7 %fusion.2 = bf16[7040,128]{1,0:T(8,128)(2,1)} fusion(bf16[2,7040,128]{2,1,0:T(8,128)(2,1)} %collective-permute-done.3, s32[]{:T(128)S(6)} %select_n.136, bf16[2,7040,128]{2,1,0:T(8,128)(2,1)} %get-tuple-element.114), kind=kLoop, calls=%fused_computation.17 | loop fusion | flops 3604480 | bytes 5406724 | tf_op jit(solution)/shard_map/convert_element_type | solution.py:1190
  223.4 22.0 %attend_back.1 = (f32[2,576,1024]{2,1,0:T(8,128)}, f32[2,192,1024]{2,1,0:T(8,128)}, f32[2,192,1024]{2,1,0:T(8,128)}) custom-call(s32[2]{0:T(128)} %dynamic_slice.54.lens, bf16[2,576,1024]{2,1,0:T(8,128)(2,1)} %get-tuple-element.98.q_t, bf16[2,3,1024,64]{3,2,1,0:T(8,128)(2,1)} %get-tuple-element.99.k_n, bf16[2,192,1024]{2,1,0:T(8,128)(2,1)} %get-tuple-element.116.k_t, ...), custom_call_target="tpu_custom_call" | custom-call | flops 40000000000 | bytes 40000000 | tf_op jit(solution)/shard_map/attend_back/pallas_call | solution.py:884
  245.4 19.3 %collective-permute-done.4 = bf16[7040,128]{1,0:T(8,128)(2,1)} collective-permute-done((bf16[7040,128]{1,0:T(8,128)(2,1)}, bf16[7040,128]{1,0:T(8,128)(2,1)}, u32[]{:S(2)}, u32[]{:S(2)}) %collective-permute-start.4) | collective-permute-done | bytes 1802272 | tf_op jit(solution)/shard_map/ppermute | solution.py:1161
  273.5 15.3 %project_back.1 = (bf16[2,576,1024]{2,1,0:T(8,128)(2,1)}, f32[576,1024]{1,0:T(8,128)}, f32[1,576]{1,0:T(1,128)}, f32[2,64]{1,0:T(2,128)}) custom-call(s32[2]{0:T(128)} %dynamic_slice.54.lens, f32[2,576,1024]{2,1,0:T(8,128)} %get-tuple-element.132.dq_t, f32[2,192,1024]{2,1,0:T(8,128)} %get-tuple-element.133.dk_t, f32[2,192,1024]{2,1,0:T(8,128)} %get-tuple-element.134.dv_t, ...), custom_call_target="tpu_custom_call" | custom-call | flops 20000000000 | bytes 60000000 | tf_op jit(solution)/shard_map/project_back/pallas_call | solution.py:560
  304.5 4.8 %collective-permute-done.8 = bf16[11,80,128]{2,1,0:T(8,128)(2,1)} collective-permute-done((bf16[11,80,128]{2,1,0:T(8,128)(2,1)}, bf16[11,80,128]{2,1,0:T(8,128)(2,1)}, u32[]{:S(2)}, u32[]{:S(2)}) %collective-permute-start.8) | collective-permute-done | bytes 225312 | tf_op jit(solution)/shard_map/ppermute | solution.py:1161
  311.1 43.5 %sum_head.1 = (bf16[4608,128]{1,0:T(8,128)(2,1)S(1)}, bf16[11,640,128]{2,1,0:T(8,128)(2,1)S(1)}) custom-call(bf16[4608,128]{1,0:T(8,128)(2,1)} %pad_bitcast_fusion.1.source, bf16[16,128]{1,0:T(8,128)(2,1)} %pad.19.gain_rows, bf16[11,80,128]{2,1,0:T(8,128)(2,1)} %add_convert_fusion.2.late_share), custom_call_target="tpu_custom_call" | custom-call | tf_op jit(solution)/shard_map/sum_head/pallas_call | solution.py:1012
  356.9 9.5 %rsqrt_multiply_fusion = (f32[886352]{0:T(1024)}, f32[886352]{0:T(1024)}, f32[886352]{0:T(1024)}, f32[886352]{0:T(1024)}) fusion(f32[886352]{0:T(1024)} %param.20, f32[886352]{0:T(1024)} %param.21, bf16[886352]{0:T(1024)(128)(2,1)} %get-tuple-element.173), kind=kLoop, calls=%fused_computation.11 | loop fusion | flops 9749872 | bytes 23045152 | tf_op jit(solution)/shard_map/div | solution.py:1259
  (81 shorter events, 52.3 us)
Async XLA Ops:
  4.7 22.4 %copy-start.1 = (bf16[2,1024,576]{1,2,0:T(8,128)(2,1)S(1)}, bf16[2,1024,576]{1,2,0:T(8,128)(2,1)}, u32[]{:S(2)}) copy-start(bf16[2,1024,576]{1,2,0:T(8,128)(2,1)} %param.16) | copy-start | bytes 7077892
  15.4 52.7 %collective-permute-start.1 = (bf16[6944,128]{1,0:T(8,128)(2,1)}, bf16[6944,128]{1,0:T(8,128)(2,1)}, u32[]{:S(2)}, u32[]{:S(2)}) collective-permute-start(bf16[6944,128]{1,0:T(8,128)(2,1)} %get-tuple-element.95.own), channel_id=1, source_target_pairs={{0,1},{1,0},{2,3},{3,2},{4,5},{5,4},{6,7},{7,6},{8,9},{9,8},{10,11... | collective-permute-start | bytes 5333000 | tf_op jit(solution)/shard_map/ppermute | solution.py:1161
  15.5 52.6 %collective-permute-start = (bf16[6944,128]{1,0:T(8,128)(2,1)}, bf16[6944,128]{1,0:T(8,128)(2,1)}, u32[]{:S(2)}, u32[]{:S(2)}) collective-permute-start(bf16[6944,128]{1,0:T(8,128)(2,1)} %get-tuple-element.95.own), channel_id=1, source_target_pairs={{0,2},{1,3},{2,0},{3,1},{4,6},{5,7},{6,4},{7,5},{8,10},{9,11},{10,... | collective-permute-start | bytes 5333000 | tf_op jit(solution)/shard_map/ppermute | solution.py:1161
  29.8 5.0 %copy-start.2 = (bf16[4384,128]{1,0:T(8,128)(2,1)S(1)}, bf16[4384,128]{1,0:T(8,128)(2,1)}, u32[]{:S(2)}) copy-start(bf16[4384,128]{1,0:T(8,128)(2,1)} %get-tuple-element.96) | copy-start | bytes 3366916
  29.8 58.9 %all-to-all-start = ((bf16[8,2,576,128]{3,2,1,0:T(8,128)(2,1)}), bf16[8,2,576,128]{3,2,1,0:T(8,128)(2,1)S(1)}, u32[]{:S(2)}, u32[]{:S(2)}) async-start(bf16[8,2,576,128]{3,2,1,0:T(8,128)(2,1)} %copy.55), calls=%async_computation | async-start | bytes 4718592 | tf_op jit(solution)/shard_map/all_to_all | solution.py:1146
  34.8 4.3 %copy-start.6 = (bf16[32,128]{1,0:T(8,128)(2,1)S(1)}, bf16[32,128]{1,0:T(8,128)(2,1)}, u32[]{:S(2)}) copy-start(bf16[32,128]{1,0:T(8,128)(2,1)} %get-tuple-element.97) | copy-start | bytes 24580
  90.9 58.1 %all-to-all-start.1 = ((bf16[8,2,576,128]{3,2,1,0:T(8,128)(2,1)}), bf16[8,2,576,128]{3,2,1,0:T(8,128)(2,1)S(1)}, u32[]{:S(2)}, u32[]{:S(2)}) async-start(bf16[8,2,576,128]{3,2,1,0:T(8,128)(2,1)} %bitcast.68), calls=%async_computation.1 | async-start | bytes 4718592 | tf_op jit(solution)/shard_map/all_to_all | solution.py:1152
  95.0 4.1 %collective-permute-start.2 = (bf16[6944,128]{1,0:T(8,128)(2,1)}, bf16[6944,128]{1,0:T(8,128)(2,1)}, u32[]{:S(2)}, u32[]{:S(2)}) collective-permute-start(bf16[6944,128]{1,0:T(8,128)(2,1)} %collective-permute-done.far), channel_id=1, source_target_pairs={{0,1},{1,0},{2,3},{3,2},{4,5},{5,4},{6,7},{7,6},{8,9},{9,8},{10,11... | collective-permute-start | bytes 5333000 | tf_op jit(solution)/shard_map/ppermute | solution.py:1161
  149.0 1.4 copy-start
  150.4 57.8 %all-to-all-start.2 = ((bf16[8,2,576,128]{3,2,1,0:T(8,128)(2,1)}), bf16[8,2,576,128]{3,2,1,0:T(8,128)(2,1)}, u32[]{:S(2)}, u32[]{:S(2)}) async-start(bf16[8,2,576,128]{3,2,1,0:T(8,128)(2,1)} %get-tuple-element.118), calls=%async_computation.2 | async-start | bytes 4718592 | tf_op jit(solution)/shard_map/all_to_all | solution.py:1146
  154.8 49.6 %copy-start.5 = (f32[2,16,1024]{2,1,0:T(8,128)S(1)}, f32[2,16,1024]{2,1,0:T(8,128)}, u32[]{:S(2)}) copy-start(f32[2,16,1024]{2,1,0:T(8,128)} %get-tuple-element.122) | copy-start | bytes 393220
  192.9 26.5 %collective-permute-start.3 = (bf16[2,7040,128]{2,1,0:T(8,128)(2,1)}, bf16[2,7040,128]{2,1,0:T(8,128)(2,1)}, u32[]{:S(2)}, u32[]{:S(2)}) collective-permute-start(bf16[2,7040,128]{2,1,0:T(8,128)(2,1)} %get-tuple-element.115), channel_id=1, source_target_pairs={{0,1},{1,0},{2,3},{3,2},{4,5},{5,4},{6,7},{7,6},{8,9},{9,8},{10,11... | collective-permute-start | bytes 10813448 | tf_op jit(solution)/shard_map/ppermute | solution.py:1161
  212.1 81.9 %all-to-all-start.3 = ((bf16[8,2,576,128]{3,2,1,0:T(8,128)(2,1)}), bf16[8,2,576,128]{3,2,1,0:T(8,128)(2,1)S(1)}, u32[]{:S(2)}, u32[]{:S(2)}) async-start(bf16[8,2,576,128]{3,2,1,0:T(8,128)(2,1)} %bitcast.66), calls=%async_computation.3 | async-start | bytes 4718592 | tf_op jit(solution)/shard_map/all_to_all | solution.py:1152
  223.1 41.6 %collective-permute-start.4 = (bf16[7040,128]{1,0:T(8,128)(2,1)}, bf16[7040,128]{1,0:T(8,128)(2,1)}, u32[]{:S(2)}, u32[]{:S(2)}) collective-permute-start(bf16[7040,128]{1,0:T(8,128)(2,1)} %fusion.2), channel_id=1, source_target_pairs={{0,2},{1,3},{2,0},{3,1},{4,6},{5,7},{6,4},{7,5},{8,10},{9,11},{10,... | collective-permute-start | bytes 5406728 | tf_op jit(solution)/shard_map/ppermute | solution.py:1161
  270.0 21.0 %collective-permute-start.5 = (bf16[11,160,128]{2,1,0:T(8,128)(2,1)}, bf16[11,160,128]{2,1,0:T(8,128)(2,1)}, u32[]{:S(2)}, u32[]{:S(2)}) collective-permute-start(bf16[11,160,128]{2,1,0:T(8,128)(2,1)} %get-tuple-element.129), channel_id=1, source_target_pairs={{0,4},{4,0},{8,12},{12,8},{16,20},{20,16},{24,28},{28,24},{1,5},{5... | collective-permute-start | bytes 1351688 | tf_op jit(solution)/shard_map/ppermute | solution.py:1177
  271.7 19.2 %collective-permute-start.6 = (bf16[11,160,128]{2,1,0:T(8,128)(2,1)}, bf16[11,160,128]{2,1,0:T(8,128)(2,1)}, u32[]{:S(2)}, u32[]{:S(2)}) collective-permute-start(bf16[11,160,128]{2,1,0:T(8,128)(2,1)} %get-tuple-element.130), channel_id=1, source_target_pairs={{0,8},{4,12},{8,0},{12,4},{16,24},{20,28},{24,16},{28,20},{1,9},{5... | collective-permute-start | bytes 1351688 | tf_op jit(solution)/shard_map/ppermute | solution.py:1177
  273.2 20.8 %collective-permute-start.7 = (bf16[11,160,128]{2,1,0:T(8,128)(2,1)S(1)}, bf16[11,160,128]{2,1,0:T(8,128)(2,1)}, u32[]{:S(2)}, u32[]{:S(2)}) collective-permute-start(bf16[11,160,128]{2,1,0:T(8,128)(2,1)S(1)} %get-tuple-element.131), channel_id=1, source_target_pairs={{0,12},{4,8},{8,4},{12,0},{16,28},{20,24},{24,20},{28,16},{1,13},{... | collective-permute-start | bytes 1351688 | tf_op jit(solution)/shard_map/ppermute | solution.py:1177
  294.0 3.4 copy-start.4
  296.5 12.9 %collective-permute-start.8 = (bf16[11,80,128]{2,1,0:T(8,128)(2,1)}, bf16[11,80,128]{2,1,0:T(8,128)(2,1)}, u32[]{:S(2)}, u32[]{:S(2)}) collective-permute-start(bf16[11,80,128]{2,1,0:T(8,128)(2,1)} %get-tuple-element.167), channel_id=1, source_target_pairs={{0,16},{4,20},{8,24},{12,28},{16,0},{20,4},{24,8},{28,12},{1,17},{... | collective-permute-start | bytes 675848 | tf_op jit(solution)/shard_map/ppermute | solution.py:1161
  302.8 6.6 %copy-start.3 = (bf16[11,80,128]{2,1,0:T(8,128)(2,1)S(1)}, bf16[11,80,128]{2,1,0:T(8,128)(2,1)}, u32[]{:S(2)}) copy-start(bf16[11,80,128]{2,1,0:T(8,128)(2,1)} %get-tuple-element.151) | copy-start | bytes 675844

commit v3 on v2

--- a/solution.py
+++ b/solution.py
@@ -648,7 +648,9 @@
 FIRST_ROWS = 4368
 LAST_TILE = 32
 GAIN_AT = EDGE + IN_ROWS + LATE_ROWS - 3 * STEP - (SPAN - LAST_TILE)
-FIRST_CUTS = (0, 1088, 2176, 3264, FIRST_ROWS)
+FIRST_PIECES = 8
+FIRST_CUTS = (0, 544, 1088, 1632, 2176, 2720, 3264, 3808, FIRST_ROWS)
+FIRST_TILES = -(-(EDGE + FIRST_ROWS) // PACK_TILE)
 
 
 def pack_kernel(master, own, first_rows, last_rows, rows_in, packed, load_sem, keep_sem, own_sem, send_sem, recv_sem):
@@ -695,12 +697,28 @@
         return pltpu.make_async_remote_copy(source, target, send_sem.at[slot], recv_sem.at[slot],
                                             device_id=device, device_id_type=MESH)
 
+    def pieces_of(half):
+        return range(half * FIRST_PIECES // 2, (half + 1) * FIRST_PIECES // 2)
+
+    def send_first():
+        for half in range(2):
+
+            @pl.when(y == half)
+            def _():
+                for piece in pieces_of(half):
+                    copy(mine(piece), theirs(piece), across, piece).start()
+
+        for piece in range(FIRST_PIECES):
+            copy(mine(piece), theirs(piece), core, FIRST_PIECES + piece).start()
+
     for s in range(4):
 
         @pl.when(zero == s)
         def _():
             for t in range(SPAN // PACK_TILE):
                 pack(s, t * PACK_TILE)
+                if s == 0 and t + 1 == FIRST_TILES:
+                    send_first()
 
     keep = pltpu.make_async_copy(packed, own, own_sem)
     keep.start()
@@ -708,36 +726,31 @@
 
     @pl.when(zero == 3)
     def _():
-        copy(tail, last_rows, across, 9).start()
-        copy(tail, last_rows, core, 8).start()
+        copy(tail, last_rows, across, 2 * FIRST_PIECES + 1).start()
+        copy(tail, last_rows, core, 2 * FIRST_PIECES).start()
         stay = pltpu.make_async_copy(tail, last_rows, keep_sem)
         stay.start()
         stay.wait()
-        copy(tail, last_rows, across, 9).wait_send()
-        copy(tail, last_rows, core, 8).wait_send()
+        copy(tail, last_rows, across, 2 * FIRST_PIECES + 1).wait_send()
+        copy(tail, last_rows, core, 2 * FIRST_PIECES).wait_send()
 
     @pl.when(zero == 1)
     def _():
-        copy(last_rows, last_rows, across, 9).wait_recv()
-        copy(last_rows, last_rows, core, 8).start()
-        copy(last_rows, last_rows, core, 8).wait_send()
+        copy(last_rows, last_rows, across, 2 * FIRST_PIECES + 1).wait_recv()
+        copy(last_rows, last_rows, core, 2 * FIRST_PIECES).start()
+        copy(last_rows, last_rows, core, 2 * FIRST_PIECES).wait_send()
 
     for half in range(2):
-        pieces = (2 * half, 2 * half + 1)
-        others = (2 - 2 * half, 3 - 2 * half)
+        pieces, others = pieces_of(half), pieces_of(1 - half)
 
         @pl.when((zero == 0) & (y == half))
         def _():
-            for piece in pieces:
-                copy(mine(piece), theirs(piece), across, piece).start()
-            for piece in range(4):
-                copy(mine(piece), theirs(piece), core, 4 + piece).start()
             stay = pltpu.make_async_copy(packed.at[pl.ds(EDGE, FIRST_ROWS)], first_rows.at[pl.ds(EDGE, FIRST_ROWS)], keep_sem)
             stay.start()
             for piece in pieces:
                 copy(mine(piece), theirs(piece), across, piece).wait_send()
-            for piece in range(4):
-                copy(mine(piece), theirs(piece), core, 4 + piece).wait_send()
+            for piece in range(FIRST_PIECES):
+                copy(mine(piece), theirs(piece), core, FIRST_PIECES + piece).wait_send()
             stay.wait()
 
         @pl.when((zero == 2) & (y == half))
@@ -745,23 +758,23 @@
             for piece in pieces:
                 copy(theirs(piece), theirs(piece), across, piece).wait_recv()
                 copy(theirs(piece), theirs(piece), side, piece).start()
-                copy(theirs(piece), theirs(piece), core, 4 + piece).start()
+                copy(theirs(piece), theirs(piece), core, FIRST_PIECES + piece).start()
             for piece in others:
                 copy(theirs(piece), theirs(piece), side, piece).wait_recv()
-                copy(theirs(piece), theirs(piece), core, 4 + piece).start()
+                copy(theirs(piece), theirs(piece), core, FIRST_PIECES + piece).start()
             for piece in pieces:
                 copy(theirs(piece), theirs(piece), side, piece).wait_send()
-            for piece in range(4):
-                copy(theirs(piece), theirs(piece), core, 4 + piece).wait_send()
+            for piece in range(FIRST_PIECES):
+                copy(theirs(piece), theirs(piece), core, FIRST_PIECES + piece).wait_send()
 
     @pl.when(bit_of(zero, 0) == 0)
     def _():
-        copy(last_rows, last_rows, core, 8).wait_recv()
+        copy(last_rows, last_rows, core, 2 * FIRST_PIECES).wait_recv()
 
     @pl.when(bit_of(zero, 0) == 1)
     def _():
-        for piece in range(4):
-            copy(theirs(piece), theirs(piece), core, 4 + piece).wait_recv()
+        for piece in range(FIRST_PIECES):
+            copy(theirs(piece), theirs(piece), core, FIRST_PIECES + piece).wait_recv()
 
     keep.wait()
 
@@ -781,8 +794,8 @@
             pltpu.SemaphoreType.DMA,
             pltpu.SemaphoreType.DMA,
             pltpu.SemaphoreType.DMA,
-            pltpu.SemaphoreType.DMA((10,)),
-            pltpu.SemaphoreType.DMA((10,)),
+            pltpu.SemaphoreType.DMA((2 * FIRST_PIECES + 2,)),
+            pltpu.SemaphoreType.DMA((2 * FIRST_PIECES + 2,)),
         ],
         cost_estimate=pl.CostEstimate(flops=0, bytes_accessed=0, transcendentals=0),
         compiler_params=pltpu.CompilerParams(collective_id=0, has_side_effects=True, vmem_limit_bytes=VMEM_LIMIT),

time: 373 us -> 371 us (level)
  starting transfers between devices: 48.6 us -> 37.5 us
  waiting for transfers between devices: 69.3 us -> 75.9 us
    all_to_all x2, waiting for transfers between devices: 20.5 us -> 31.8 us  [spread(): return lax.all_to_all(parts, 'dp', split_axis=0, concat_axis=0, tiled=True)]
    ppermute x6, starting transfers between devices: 24.4 us -> 15.5 us  [exchange(): lax.ppermute(values, axis, [(i, i ^ 1 << bit) for i in range(lax.axis_siz...]
    ppermute x6, waiting for transfers between devices: 27.5 us -> 23.7 us  [exchange(): lax.ppermute(values, axis, [(i, i ^ 1 << bit) for i in range(lax.axis_siz...]
  transfers between devices with their start and end apart: 13 -> 13, of which waited for: 6 -> 7; matrix products, arithmetic and copies ran while one was open for 11% -> 11% of each run, Pallas kernels for 35% -> 36%
where the time goes in v3:
time: 371 us; the launch traced here: 364 us
  Pallas kernels  186 us (50%)
  waiting for transfers between devices  75.9 us (20%)
  local copies, waits for them, and re-layouts  38.2 us (10%)
  starting transfers between devices  37.5 us (10%)
  other arithmetic  25.7 us (7%)
    pallas_call x1, Pallas kernels, sum_head(): pl.pallas_call(functools.partial(sum_head_kernel, bits, rows, late_rows),...  45.6 us
    pallas_call x1, Pallas kernels, mlp_back(): pl.pallas_call(mlp_back_kernel, name='mlp_back', grid_spec=pltpu.Prefetch...  38.1 us
    all_to_all x2, waiting for transfers between devices, spread(): return lax.all_to_all(parts, 'dp', split_axis=0, concat_axis=0, tiled=True)  31.8 us
    ppermute x6, waiting for transfers between devices, exchange(): lax.ppermute(values, axis, [(i, i ^ 1 << bit) for i in range(lax.axis_siz...  23.7 us
    pallas_call x1, Pallas kernels, attend_back(): pl.pallas_call(attend_back_kernel, name='attend_back', grid_spec=pltpu.Pr...  22 us
    pallas_call x1, Pallas kernels, mlp(): pl.pallas_call(mlp_kernel, name='mlp', grid_spec=pltpu.PrefetchScalarGrid...  20.4 us
    all_to_all x2, waiting for transfers between devices, regroup(): lax.all_to_all(parts.reshape(dp_size, seqs, width, columns), 'dp', split_...  18.3 us
    ppermute x6, starting transfers between devices, exchange(): lax.ppermute(values, axis, [(i, i ^ 1 << bit) for i in range(lax.axis_siz...  15.5 us
  transfers between devices with their start and end apart: 13, of which 7 were waited for; matrix products, arithmetic and copies ran while one was open for 11% of the time, Pallas kernels for 36%

profile of v3, /device:TPU:0, one launch (start us, length us, event | category | flops | bytes accessed | tf_op | source)
XLA Modules:
  0.0 364.1 jit_solution(10050140510822281678)
XLA Ops:
  0.6 4.0 %pad_bitcast_fusion.master = f32[6928,128]{1,0:T(8,128)} fusion(f32[886352]{0:T(1024)} %param.19), kind=kLoop, calls=%fused_computation.13 | loop fusion | bytes 7092544 | tf_op jit(solution)/shard_map/reshape | solution.py:783
  4.7 10.6 %pack_master.1 = (bf16[6944,128]{1,0:T(8,128)(2,1)}, bf16[4384,128]{1,0:T(8,128)(2,1)}, bf16[32,128]{1,0:T(8,128)(2,1)}) custom-call(f32[6928,128]{1,0:T(8,128)} %pad_bitcast_fusion.master), custom_call_target="tpu_custom_call" | custom-call | tf_op jit(solution)/shard_map/pack_master/pallas_call | solution.py:785
  15.3 9.8 %collective-permute-start = (bf16[6944,128]{1,0:T(8,128)(2,1)}, bf16[6944,128]{1,0:T(8,128)(2,1)}, u32[]{:S(2)}, u32[]{:S(2)}) collective-permute-start(bf16[6944,128]{1,0:T(8,128)(2,1)} %get-tuple-element.95.own), channel_id=1, source_target_pairs={{0,2},{1,3},{2,0},{3,1},{4,6},{5,7},{6,4},{7,5},{8,10},{9,11},{10,... | collective-permute-start | bytes 5333000 | tf_op jit(solution)/shard_map/ppermute | solution.py:1174
  27.8 5.0 %all-to-all-start = ((bf16[8,2,576,128]{3,2,1,0:T(8,128)(2,1)}), bf16[8,2,576,128]{3,2,1,0:T(8,128)(2,1)S(1)}, u32[]{:S(2)}, u32[]{:S(2)}) async-start(bf16[8,2,576,128]{3,2,1,0:T(8,128)(2,1)} %copy.55), calls=%async_computation | async-start | bytes 4718592 | tf_op jit(solution)/shard_map/all_to_all | solution.py:1159
  43.8 10.3 %project.1 = (bf16[2,576,1024]{2,1,0:T(8,128)(2,1)}, bf16[2,3,1024,64]{3,2,1,0:T(8,128)(2,1)}, bf16[2,192,1024]{2,1,0:T(8,128)(2,1)}, bf16[2,3,1024,64]{3,2,1,0:...) custom-call(s32[2]{0:T(128)} %dynamic_slice.54.lens, ...), custom_call_target="tpu_custom_call" | custom-call | tf_op jit(solution)/shard_map/project/pallas_call | solution.py:139
  54.0 12.1 %attend.1 = (f32[2,576,1024]{2,1,0:T(8,128)}, f32[2,16,1024]{2,1,0:T(8,128)}) custom-call(s32[2]{0:T(128)} %dynamic_slice.54.lens, bf16[2,576,1024]{2,1,0:T(8,128)(2,1)} %get-tuple-element.98.q_t, bf16[2,3,1024,64]{3,2,1,0:T(8,128)(2,1)} %get-tuple-element.99.k_n, bf16[2,192,1024]{2,1,0:T(8,128)(2,1)} %get-tuple-element.100.v_t), custom_call_target="tpu_custom_call" | custom-call | tf_op jit(solution)/shard_map/attend/pallas_call | solution.py:212
  66.2 20.5 %all-to-all-done = bf16[8,2,576,128]{3,2,1,0:T(8,128)(2,1)S(1)} async-done(((bf16[8,2,576,128]{3,2,1,0:T(8,128)(2,1)}), bf16[8,2,576,128]{3,2,1,0:T(8,128)(2,1)S(1)}, u32[]{:S(2)}, u32[]{:S(2)}) %all-to-all-start) | async-done | bytes 2359328 | tf_op jit(solution)/shard_map/all_to_all | solution.py:1159
  89.0 4.1 %all-to-all-start.1 = ((bf16[8,2,576,128]{3,2,1,0:T(8,128)(2,1)}), bf16[8,2,576,128]{3,2,1,0:T(8,128)(2,1)S(1)}, u32[]{:S(2)}, u32[]{:S(2)}) async-start(bf16[8,2,576,128]{3,2,1,0:T(8,128)(2,1)} %bitcast.68), calls=%async_computation.1 | async-start | bytes 4718592 | tf_op jit(solution)/shard_map/all_to_all | solution.py:1165
  93.8 3.4 collective-permute-done.2.both
  97.2 11.2 %unpack_weights.1 = (bf16[576,576]{1,0:T(8,128)(2,1)}, bf16[576,3072]{1,0:T(8,128)(2,1)}, bf16[1536,576]{1,0:T(8,128)(2,1)}) custom-call(bf16[6944,128]{1,0:T(8,128)(2,1)} %get-tuple-element.95.own, bf16[6944,128]{1,0:T(8,128)(2,1)} %collective-permute-done.1.near, bf16[6944,128]{1,0:T(8,128)(2,1)} %collective-permute-done.far, ...), custom_call_target="tpu_custom_call" | custom-call | tf_op jit(solution)/shard_map/unpack_weights/pallas_call | solution.py:1135
  108.4 20.4 %mlp.1 = (bf16[8,2,576,128]{3,2,1,0:T(8,128)(2,1)}, f32[2,1024,576]{2,1,0:T(8,128)}, bf16[2,1024,1536]{2,1,0:T(8,128)(2,1)}, bf16[2,1024,1536]{2,1,0:T(8,128)(2,1)}, bf16[2,1024,1536]{2,1,0:T(8,128)(2,1)}) custom-call(s32[2]{0:T(128)} %dynamic_slice.54.lens, f32[2,576,1024]{2,1,0:T(8,128)} %get-tuple-element.102.att_t, ...), custom_call_target="tpu_custom_call" | custom-call | tf_op jit(solution)/shard_map/mlp/pallas_call | solution.py:324
  128.8 18.3 %all-to-all-done.1.cot_parts = bf16[8,2,576,128]{3,2,1,0:T(8,128)(2,1)S(1)} async-done(((bf16[8,2,576,128]{3,2,1,0:T(8,128)(2,1)}), bf16[8,2,576,128]{3,2,1,0:T(8,128)(2,1)S(1)}, u32[]{:S(2)}, u32[]{:S(2)}) %all-to-all-start.1) | async-done | bytes 2359328 | tf_op jit(solution)/shard_map/all_to_all | solution.py:1165
  148.4 4.4 %all-to-all-start.2 = ((bf16[8,2,576,128]{3,2,1,0:T(8,128)(2,1)}), bf16[8,2,576,128]{3,2,1,0:T(8,128)(2,1)}, u32[]{:S(2)}, u32[]{:S(2)}) async-start(bf16[8,2,576,128]{3,2,1,0:T(8,128)(2,1)} %get-tuple-element.118), calls=%async_computation.2 | async-start | bytes 4718592 | tf_op jit(solution)/shard_map/all_to_all | solution.py:1159
  152.8 38.1 %mlp_back.1 = (f32[2,576,1024]{2,1,0:T(8,128)}, bf16[2,576,1024]{2,1,0:T(8,128)(2,1)}, f32[2,32,1024]{2,1,0:T(8,128)}, bf16[2,7040,128]{2,1,0:T(8,128)(2,1)}, bf...) custom-call(s32[2]{0:T(128)} %dynamic_slice.54.lens, f32[2,576,1024]{2,1,0:T(8,128)} %get-tuple-element.102.att_t, ...), custom_call_target="tpu_custom_call" | custom-call | tf_op jit(solution)/shard_map/mlp_back/pallas_call | solution.py:452
  195.0 11.3 %all-to-all-done.2 = bf16[8,2,576,128]{3,2,1,0:T(8,128)(2,1)} async-done(((bf16[8,2,576,128]{3,2,1,0:T(8,128)(2,1)}), bf16[8,2,576,128]{3,2,1,0:T(8,128)(2,1)}, u32[]{:S(2)}, u32[]{:S(2)}) %all-to-all-start.2) | async-done | bytes 2359328 | tf_op jit(solution)/shard_map/all_to_all | solution.py:1159
  206.2 3.9 %gather_fusion.1 = bf16[16,576,128]{2,1,0:T(8,128)(2,1)} fusion(bf16[16,576,128]{2,1,0:T(8,128)(2,1)} %bitcast.17, s32[1024]{0:T(1024)S(1)} %pad_clamp_fusion), kind=kCustom, calls=%fused_computation.1 | custom fusion | bytes 4718656 | tf_op jit(solution)/shard_map/jit(_take)/gather | solution.py:1164
  210.2 5.0 %all-to-all-start.3 = ((bf16[8,2,576,128]{3,2,1,0:T(8,128)(2,1)}), bf16[8,2,576,128]{3,2,1,0:T(8,128)(2,1)S(1)}, u32[]{:S(2)}, u32[]{:S(2)}) async-start(bf16[8,2,576,128]{3,2,1,0:T(8,128)(2,1)} %bitcast.66), calls=%async_computation.3 | async-start | bytes 4718592 | tf_op jit(solution)/shard_map/all_to_all | solution.py:1165
  215.2 3.7 %fusion.2 = bf16[7040,128]{1,0:T(8,128)(2,1)} fusion(bf16[2,7040,128]{2,1,0:T(8,128)(2,1)} %collective-permute-done.3, s32[]{:T(128)S(6)} %select_n.136, bf16[2,7040,128]{2,1,0:T(8,128)(2,1)} %get-tuple-element.114), kind=kLoop, calls=%fused_computation.17 | loop fusion | flops 3604480 | bytes 5406724 | tf_op jit(solution)/shard_map/convert_element_type | solution.py:1203
  221.5 22.0 %attend_back.1 = (f32[2,576,1024]{2,1,0:T(8,128)}, f32[2,192,1024]{2,1,0:T(8,128)}, f32[2,192,1024]{2,1,0:T(8,128)}) custom-call(s32[2]{0:T(128)} %dynamic_slice.54.lens, bf16[2,576,1024]{2,1,0:T(8,128)(2,1)} %get-tuple-element.98.q_t, bf16[2,3,1024,64]{3,2,1,0:T(8,128)(2,1)} %get-tuple-element.99.k_n, bf16[2,192,1024]{2,1,0:T(8,128)(2,1)} %get-tuple-element.116.k_t, ...), custom_call_target="tpu_custom_call" | custom-call | flops 40000000000 | bytes 40000000 | tf_op jit(solution)/shard_map/attend_back/pallas_call | solution.py:897
  243.5 17.8 %collective-permute-done.4 = bf16[7040,128]{1,0:T(8,128)(2,1)} collective-permute-done((bf16[7040,128]{1,0:T(8,128)(2,1)}, bf16[7040,128]{1,0:T(8,128)(2,1)}, u32[]{:S(2)}, u32[]{:S(2)}) %collective-permute-start.4) | collective-permute-done | bytes 1802272 | tf_op jit(solution)/shard_map/ppermute | solution.py:1174
  261.3 3.3 fusion
  270.1 15.3 %project_back.1 = (bf16[2,576,1024]{2,1,0:T(8,128)(2,1)}, f32[576,1024]{1,0:T(8,128)}, f32[1,576]{1,0:T(1,128)}, f32[2,64]{1,0:T(2,128)}) custom-call(s32[2]{0:T(128)} %dynamic_slice.54.lens, f32[2,576,1024]{2,1,0:T(8,128)} %get-tuple-element.132.dq_t, f32[2,192,1024]{2,1,0:T(8,128)} %get-tuple-element.133.dk_t, f32[2,192,1024]{2,1,0:T(8,128)} %get-tuple-element.134.dv_t, ...), custom_call_target="tpu_custom_call" | custom-call | flops 20000000000 | bytes 60000000 | tf_op jit(solution)/shard_map/project_back/pallas_call | solution.py:560
  306.5 45.6 %sum_head.1 = (bf16[4608,128]{1,0:T(8,128)(2,1)S(1)}, bf16[11,640,128]{2,1,0:T(8,128)(2,1)S(1)}) custom-call(bf16[4608,128]{1,0:T(8,128)(2,1)} %pad_bitcast_fusion.1.source, bf16[16,128]{1,0:T(8,128)(2,1)} %pad.19.gain_rows, bf16[11,80,128]{2,1,0:T(8,128)(2,1)} %add_convert_fusion.2.late_share), custom_call_target="tpu_custom_call" | custom-call | tf_op jit(solution)/shard_map/sum_head/pallas_call | solution.py:1025
  354.5 9.5 %rsqrt_multiply_fusion = (f32[886352]{0:T(1024)}, f32[886352]{0:T(1024)}, f32[886352]{0:T(1024)}, f32[886352]{0:T(1024)}) fusion(f32[886352]{0:T(1024)} %param.20, f32[886352]{0:T(1024)} %param.21, bf16[886352]{0:T(1024)(128)(2,1)} %get-tuple-element.173), kind=kLoop, calls=%fused_computation.11 | loop fusion | flops 9749872 | bytes 23045152 | tf_op jit(solution)/shard_map/div | solution.py:1272
  (81 shorter events, 55.0 us)
Async XLA Ops:
  4.7 20.4 %copy-start.1 = (bf16[2,1024,576]{1,2,0:T(8,128)(2,1)S(1)}, bf16[2,1024,576]{1,2,0:T(8,128)(2,1)}, u32[]{:S(2)}) copy-start(bf16[2,1024,576]{1,2,0:T(8,128)(2,1)} %param.16) | copy-start | bytes 7077892
  15.3 50.9 %collective-permute-start.1 = (bf16[6944,128]{1,0:T(8,128)(2,1)}, bf16[6944,128]{1,0:T(8,128)(2,1)}, u32[]{:S(2)}, u32[]{:S(2)}) collective-permute-start(bf16[6944,128]{1,0:T(8,128)(2,1)} %get-tuple-element.95.own), channel_id=1, source_target_pairs={{0,1},{1,0},{2,3},{3,2},{4,5},{5,4},{6,7},{7,6},{8,9},{9,8},{10,11... | collective-permute-start | bytes 5333000 | tf_op jit(solution)/shard_map/ppermute | solution.py:1174
  15.3 50.8 %collective-permute-start = (bf16[6944,128]{1,0:T(8,128)(2,1)}, bf16[6944,128]{1,0:T(8,128)(2,1)}, u32[]{:S(2)}, u32[]{:S(2)}) collective-permute-start(bf16[6944,128]{1,0:T(8,128)(2,1)} %get-tuple-element.95.own), channel_id=1, source_target_pairs={{0,2},{1,3},{2,0},{3,1},{4,6},{5,7},{6,4},{7,5},{8,10},{9,11},{10,... | collective-permute-start | bytes 5333000 | tf_op jit(solution)/shard_map/ppermute | solution.py:1174
  27.8 5.0 %copy-start.2 = (bf16[4384,128]{1,0:T(8,128)(2,1)S(1)}, bf16[4384,128]{1,0:T(8,128)(2,1)}, u32[]{:S(2)}) copy-start(bf16[4384,128]{1,0:T(8,128)(2,1)} %get-tuple-element.96) | copy-start | bytes 3366916
  27.8 58.9 %all-to-all-start = ((bf16[8,2,576,128]{3,2,1,0:T(8,128)(2,1)}), bf16[8,2,576,128]{3,2,1,0:T(8,128)(2,1)S(1)}, u32[]{:S(2)}, u32[]{:S(2)}) async-start(bf16[8,2,576,128]{3,2,1,0:T(8,128)(2,1)} %copy.55), calls=%async_computation | async-start | bytes 4718592 | tf_op jit(solution)/shard_map/all_to_all | solution.py:1159
  32.8 4.3 %copy-start.6 = (bf16[32,128]{1,0:T(8,128)(2,1)S(1)}, bf16[32,128]{1,0:T(8,128)(2,1)}, u32[]{:S(2)}) copy-start(bf16[32,128]{1,0:T(8,128)(2,1)} %get-tuple-element.97) | copy-start | bytes 24580
  89.0 58.1 %all-to-all-start.1 = ((bf16[8,2,576,128]{3,2,1,0:T(8,128)(2,1)}), bf16[8,2,576,128]{3,2,1,0:T(8,128)(2,1)S(1)}, u32[]{:S(2)}, u32[]{:S(2)}) async-start(bf16[8,2,576,128]{3,2,1,0:T(8,128)(2,1)} %bitcast.68), calls=%async_computation.1 | async-start | bytes 4718592 | tf_op jit(solution)/shard_map/all_to_all | solution.py:1165
  93.0 4.1 %collective-permute-start.2 = (bf16[6944,128]{1,0:T(8,128)(2,1)}, bf16[6944,128]{1,0:T(8,128)(2,1)}, u32[]{:S(2)}, u32[]{:S(2)}) collective-permute-start(bf16[6944,128]{1,0:T(8,128)(2,1)} %collective-permute-done.far), channel_id=1, source_target_pairs={{0,1},{1,0},{2,3},{3,2},{4,5},{5,4},{6,7},{7,6},{8,9},{9,8},{10,11... | collective-permute-start | bytes 5333000 | tf_op jit(solution)/shard_map/ppermute | solution.py:1174
  147.0 1.4 copy-start
  148.4 57.8 %all-to-all-start.2 = ((bf16[8,2,576,128]{3,2,1,0:T(8,128)(2,1)}), bf16[8,2,576,128]{3,2,1,0:T(8,128)(2,1)}, u32[]{:S(2)}, u32[]{:S(2)}) async-start(bf16[8,2,576,128]{3,2,1,0:T(8,128)(2,1)} %get-tuple-element.118), calls=%async_computation.2 | async-start | bytes 4718592 | tf_op jit(solution)/shard_map/all_to_all | solution.py:1159
  152.8 38.3 %copy-start.5 = (f32[2,16,1024]{2,1,0:T(8,128)S(1)}, f32[2,16,1024]{2,1,0:T(8,128)}, u32[]{:S(2)}) copy-start(f32[2,16,1024]{2,1,0:T(8,128)} %get-tuple-element.122) | copy-start | bytes 393220
  190.9 24.3 %collective-permute-start.3 = (bf16[2,7040,128]{2,1,0:T(8,128)(2,1)}, bf16[2,7040,128]{2,1,0:T(8,128)(2,1)}, u32[]{:S(2)}, u32[]{:S(2)}) collective-permute-start(bf16[2,7040,128]{2,1,0:T(8,128)(2,1)} %get-tuple-element.115), channel_id=1, source_target_pairs={{0,1},{1,0},{2,3},{3,2},{4,5},{5,4},{6,7},{7,6},{8,9},{9,8},{10,11... | collective-permute-start | bytes 10813448 | tf_op jit(solution)/shard_map/ppermute | solution.py:1174
  210.2 79.5 %all-to-all-start.3 = ((bf16[8,2,576,128]{3,2,1,0:T(8,128)(2,1)}), bf16[8,2,576,128]{3,2,1,0:T(8,128)(2,1)S(1)}, u32[]{:S(2)}, u32[]{:S(2)}) async-start(bf16[8,2,576,128]{3,2,1,0:T(8,128)(2,1)} %bitcast.66), calls=%async_computation.3 | async-start | bytes 4718592 | tf_op jit(solution)/shard_map/all_to_all | solution.py:1165
  218.9 42.4 %collective-permute-start.4 = (bf16[7040,128]{1,0:T(8,128)(2,1)}, bf16[7040,128]{1,0:T(8,128)(2,1)}, u32[]{:S(2)}, u32[]{:S(2)}) collective-permute-start(bf16[7040,128]{1,0:T(8,128)(2,1)} %fusion.2), channel_id=1, source_target_pairs={{0,2},{1,3},{2,0},{3,1},{4,6},{5,7},{6,4},{7,5},{8,10},{9,11},{10,... | collective-permute-start | bytes 5406728 | tf_op jit(solution)/shard_map/ppermute | solution.py:1174
  266.6 21.0 %collective-permute-start.5 = (bf16[11,160,128]{2,1,0:T(8,128)(2,1)}, bf16[11,160,128]{2,1,0:T(8,128)(2,1)}, u32[]{:S(2)}, u32[]{:S(2)}) collective-permute-start(bf16[11,160,128]{2,1,0:T(8,128)(2,1)} %get-tuple-element.129), channel_id=1, source_target_pairs={{0,4},{4,0},{8,12},{12,8},{16,20},{20,16},{24,28},{28,24},{1,5},{5... | collective-permute-start | bytes 1351688 | tf_op jit(solution)/shard_map/ppermute | solution.py:1190
  268.3 19.2 %collective-permute-start.6 = (bf16[11,160,128]{2,1,0:T(8,128)(2,1)}, bf16[11,160,128]{2,1,0:T(8,128)(2,1)}, u32[]{:S(2)}, u32[]{:S(2)}) collective-permute-start(bf16[11,160,128]{2,1,0:T(8,128)(2,1)} %get-tuple-element.130), channel_id=1, source_target_pairs={{0,8},{4,12},{8,0},{12,4},{16,24},{20,28},{24,16},{28,20},{1,9},{5... | collective-permute-start | bytes 1351688 | tf_op jit(solution)/shard_map/ppermute | solution.py:1190
  269.8 19.9 %collective-permute-start.7 = (bf16[11,160,128]{2,1,0:T(8,128)(2,1)S(1)}, bf16[11,160,128]{2,1,0:T(8,128)(2,1)}, u32[]{:S(2)}, u32[]{:S(2)}) collective-permute-start(bf16[11,160,128]{2,1,0:T(8,128)(2,1)S(1)} %get-tuple-element.131), channel_id=1, source_target_pairs={{0,12},{4,8},{8,4},{12,0},{16,28},{20,24},{24,20},{28,16},{1,13},{... | collective-permute-start | bytes 1351688 | tf_op jit(solution)/shard_map/ppermute | solution.py:1190
  289.6 5.5 %copy-start.4 = (f32[576,1024]{1,0:T(8,128)S(1)}, f32[576,1024]{1,0:T(8,128)}, u32[]{:S(2)}) copy-start(f32[576,1024]{1,0:T(8,128)} %get-tuple-element.145) | copy-start | bytes 7077892
  292.1 12.6 %collective-permute-start.8 = (bf16[11,80,128]{2,1,0:T(8,128)(2,1)}, bf16[11,80,128]{2,1,0:T(8,128)(2,1)}, u32[]{:S(2)}, u32[]{:S(2)}) collective-permute-start(bf16[11,80,128]{2,1,0:T(8,128)(2,1)} %get-tuple-element.167), channel_id=1, source_target_pairs={{0,16},{4,20},{8,24},{12,28},{16,0},{20,4},{24,8},{28,12},{1,17},{... | collective-permute-start | bytes 675848 | tf_op jit(solution)/shard_map/ppermute | solution.py:1174
  300.5 4.3 %copy-start.3 = (bf16[11,80,128]{2,1,0:T(8,128)(2,1)S(1)}, bf16[11,80,128]{2,1,0:T(8,128)(2,1)}, u32[]{:S(2)}) copy-start(bf16[11,80,128]{2,1,0:T(8,128)(2,1)} %get-tuple-element.151) | copy-start | bytes 675844
